TPU v7x, 32 devices: a whole 2x2x4 slice. The times are simulated.
32 devices in a mesh: grid: 8 (over z, y), tm: 2 (over core), pw: 2 (over x).
Axes of the slice: x: 2, y: 2, z: 4, core: 2. Of those that a mesh axis runs over, the one named last changes fastest.
Arguments:
- slab_orbitals: bfloat16 [8, 896, 512], P('grid'), may hold values from -6 to 6
- orbital_block: int32 [8], replicated, may hold values from 0 to 7, each once
- occupied_columns: bfloat16 [1024, 16, 4096], P(None, 'pw', 'grid'), may hold values from -0.1875 to 0.1875
- unoccupied_columns: bfloat16 [6144, 16, 4096], P(None, 'pw', 'grid'), may hold values from -0.078125 to 0.078125
- occupied_gap: float32 [1024], replicated, may hold values from 0.02 to 1
- unoccupied_gap: float32 [6144], replicated, may hold values from 0.02 to 2
- time_table: float32 [16], replicated, may hold values from 0.05 to 2
- frequency_table: float32 [16], replicated, may hold values from 0.1 to 4
- time_weight: float32 [16], replicated, may hold values from 1 to 4
- time_index: int32 [2], replicated, may hold values from 0 to 15
- frequency_index: int32 [2], replicated, may hold values from 0 to 15
Outputs:
- polarizability: float32 [2, 512, 16, 64, 128], P('tm', ('grid', 'pw'))
Inputs may be any that keep to these rules, and one draw needn't show every extreme that they name: orbital_block names each block 0 to 7 exactly once.
All inputs are finite; a program needn't handle non-finite values.
Results may differ from a plain program's by a relative error of at most 0.0051.
Values may be sent and summed in bfloat16 or wider, within the bound.
No kernel may reach another device: no remote copies, remote signals or barrier semaphores. Data moves between devices by JAX's collectives and lax.ppermute only.
A program may use at most 256 MiB of HBM per device.

v0:
```python
import math

import jax
import jax.numpy as jnp
from jax import lax
from jax.sharding import PartitionSpec as P

NX = 64
NY = 64
SLAB = 512


def dft_angles(number):
    indices = jnp.arange(number, dtype=jnp.int32)
    product = indices[:, None] * indices[None, :] % number
    return product.astype(jnp.float32) * (2.0 * math.pi / number)


def row_table(number):
    angles = dft_angles(number)
    factor = 1.0 / math.sqrt(number)
    return jnp.concatenate([jnp.cos(angles), -jnp.sin(angles)], axis=1) * factor


def column_table(number):
    angles = dft_angles(number)
    factor = 1.0 / math.sqrt(number)
    return (jnp.concatenate([jnp.cos(angles), jnp.sin(angles)], axis=0) * factor).astype(
        jnp.bfloat16
    )


def combine_parts(y_parts, width_y, width_x):
    cosine = y_parts[..., :width_y, :]
    sine = y_parts[..., width_y:, :]
    real_part = cosine[..., :width_x] + sine[..., width_x:]
    imag_part = cosine[..., width_x:] - sine[..., :width_x]
    return jnp.concatenate([real_part, imag_part], axis=-1)


def weigh_rows(values, rates, time_point):
    return (values * jnp.exp(-rates * time_point)[:, :, None]).astype(jnp.bfloat16)


def shards(
    slab_orbitals,
    orbital_block,
    occupied_columns,
    unoccupied_columns,
    occupied_gap,
    unoccupied_gap,
    time_table,
    frequency_table,
    time_weight,
    time_index,
    frequency_index,
):
    block_count = lax.axis_size("grid")
    occupied_block = occupied_columns.shape[0] // block_count
    unoccupied_block = unoccupied_columns.shape[0] // block_count
    planes_local = occupied_columns.shape[1]
    lines_local = occupied_columns.shape[2] // NX
    width = planes_local * occupied_columns.shape[2]
    occupied_blocks = occupied_columns.reshape(block_count, occupied_block, width)
    unoccupied_blocks = unoccupied_columns.reshape(block_count, unoccupied_block, width)
    occupied_rates = occupied_gap.reshape(block_count, occupied_block)
    unoccupied_rates = unoccupied_gap.reshape(block_count, unoccupied_block)
    moment = lax.axis_index("tm")
    time_slot = time_index[moment]
    time_point = time_table[time_slot]
    frequency_weights = time_weight[time_slot] * jnp.cos(
        frequency_table[frequency_index] * time_point
    )
    pieces = lax.all_gather(slab_orbitals, "grid", axis=0, tiled=True)
    occupied_part = weigh_rows(
        pieces[:, :occupied_block, :], jnp.take(occupied_rates, orbital_block, axis=0), time_point
    )
    unoccupied_part = weigh_rows(
        pieces[:, occupied_block:, :], jnp.take(unoccupied_rates, orbital_block, axis=0), time_point
    )
    green_occupied = jnp.einsum(
        "jis,jic->sc",
        occupied_part,
        jnp.take(occupied_blocks, orbital_block, axis=0),
        preferred_element_type=jnp.float32,
    )
    green_unoccupied = jnp.einsum(
        "jis,jic->sc",
        unoccupied_part,
        jnp.take(unoccupied_blocks, orbital_block, axis=0),
        preferred_element_type=jnp.float32,
    )
    green_occupied, green_unoccupied = (green_occupied, green_unoccupied)
    response = -green_occupied * green_unoccupied
    response = response.reshape(SLAB, planes_local, lines_local, NX)
    tiles = jnp.dot(response, row_table(NX), precision=lax.Precision.HIGHEST).astype(jnp.bfloat16)
    y_table = column_table(NY)
    received = lax.all_to_all(
        tiles[:, None], ("grid", "pw"), split_axis=0, concat_axis=1, tiled=True
    )
    stacked = received[None]
    sources = stacked.reshape(
        stacked.shape[0],
        stacked.shape[1],
        block_count,
        lax.axis_size("pw"),
        planes_local,
        lines_local,
        2 * NX,
    )
    y_parts = jnp.einsum(
        "kgy,trgpzyc->trpzkc",
        y_table.reshape(2 * NY, block_count, lines_local),
        sources,
        preferred_element_type=jnp.float32,
    )
    y_parts = y_parts.reshape(
        y_parts.shape[0], y_parts.shape[1], lax.axis_size("pw") * planes_local, 2 * NY, 2 * NX
    )
    plane_waves = combine_parts(y_parts, NY, NX)
    summed = lax.psum(frequency_weights[:, None, None, None, None] * plane_waves[0][None], "tm")
    return lax.dynamic_slice_in_dim(summed, moment, 1, 0)


def solution(mesh):
    placed = (
        P("grid", None, None),
        P(),
        P(None, "pw", "grid"),
        P(None, "pw", "grid"),
        P(),
        P(),
        P(),
        P(),
        P(),
        P(),
        P(),
    )
    return jax.shard_map(
        shards,
        mesh=mesh,
        in_specs=placed,
        out_specs=P("tm", ("grid", "pw"), None, None, None),
        check_vma=False,
    )
```

profile of v0, /device:TPU:0, one launch (start us, length us, event | category | flops | bytes accessed | tf_op | source)
XLA Modules:
  0.0 688.9 jit_solution(8808282476137112574)
XLA Ops:
  6.5 0.7 all-gather.2.cloned.1.call-update
  7.3 13.5 %reshape.91 = bf16[8,128,4096]{2,1,0:T(8,128)(2,1)} reshape(bf16[1024,8,512]{2,1,0:T(8,128)(2,1)} %param.13) | data formatting | bytes 16777216 | tf_op jit(solution)/shard_map/reshape | solution.py:64
  20.8 8.4 %gather_fusion.2 = bf16[8,128,4096]{2,1,0:T(8,128)(2,1)} fusion(bf16[8,128,4096]{2,1,0:T(8,128)(2,1)} %reshape.91, s32[1024]{0:T(1024)S(1)} %pad_clamp_fusion), kind=kCustom, calls=%fused_computation.2 | custom fusion | bytes 16777248 | tf_op jit(solution)/shard_map/jit(_take)/gather | solution.py:84
  29.2 0.6 gather_fusion.1
  29.8 0.6 dynamic_slice.12
  31.8 74.4 %reshape.93 = bf16[8,768,4096]{2,1,0:T(8,128)(2,1)} reshape(bf16[6144,8,512]{2,1,0:T(8,128)(2,1)} %param.14) | data formatting | bytes 100663296 | tf_op jit(solution)/shard_map/reshape | solution.py:65
  106.1 32.2 %fusion.50 = (bf16[8,768,1024]{2,1,0:T(8,128)(2,1)}, bf16[8,768,1024]{2,1,0:T(8,128)(2,1)}, bf16[8,768,1024]{2,1,0:T(8,128)(2,1)}, bf16[8,768,1024]{2,1,0:T(8,128)(2,1)}) fusion(bf16[8,768,4096]{2,1,0:T(8,128)(2,1)} %reshape.93), kind=kLoop, calls=%fused_computation.85 | loop fusion | bytes 100663296 | tf_op jit(solution)/shard_map/jit(_take)/gather | solution.py:90
  138.3 11.0 %gather_fusion.7 = bf16[8,768,1024]{2,1,0:T(8,128)(2,1)} fusion(bf16[8,768,1024]{2,1,0:T(8,128)(2,1)} %get-tuple-element.8, s32[1024]{0:T(1024)S(1)} %pad_clamp_fusion), kind=kCustom, calls=%fused_computation.7 | custom fusion | bytes 25165856 | tf_op jit(solution)/shard_map/jit(_take)/gather | solution.py:90
  149.3 10.9 %gather_fusion.6 = bf16[8,768,1024]{2,1,0:T(8,128)(2,1)} fusion(bf16[8,768,1024]{2,1,0:T(8,128)(2,1)} %get-tuple-element.6, s32[1024]{0:T(1024)S(1)} %pad_clamp_fusion), kind=kCustom, calls=%fused_computation.6 | custom fusion | bytes 25165856 | tf_op jit(solution)/shard_map/jit(_take)/gather | solution.py:90
  160.2 11.0 %gather_fusion.5 = bf16[8,768,1024]{2,1,0:T(8,128)(2,1)} fusion(bf16[8,768,1024]{2,1,0:T(8,128)(2,1)} %get-tuple-element.7, s32[1024]{0:T(1024)S(1)} %pad_clamp_fusion), kind=kCustom, calls=%fused_computation.5 | custom fusion | bytes 25165856 | tf_op jit(solution)/shard_map/jit(_take)/gather | solution.py:90
  171.3 10.9 %gather_fusion.4 = bf16[8,768,1024]{2,1,0:T(8,128)(2,1)} fusion(bf16[8,768,1024]{2,1,0:T(8,128)(2,1)} %get-tuple-element.5, s32[1024]{0:T(1024)S(1)} %pad_clamp_fusion), kind=kCustom, calls=%fused_computation.4 | custom fusion | bytes 25165856 | tf_op jit(solution)/shard_map/jit(_take)/gather | solution.py:90
  182.2 0.6 gather_fusion.3
  183.5 0.6 dynamic_slice.14
  184.2 0.6 multiply_exponential_fusion.1
  184.9 0.7 multiply_exponential_fusion
  185.6 11.9 %fusion.11 = f32[512,4096,1]{1,0,2:T(8,128)} fusion(bf16[8,128,4096]{2,1,0:T(8,128)(2,1)} %gather_fusion.2, pred[8]{0:T(512)(128)(4,1)S(1)} %compare_and_fusion, bf16[8,896,512]{2,1,0:T(8,128)(2,1)} %all-gather.2.cloned.1.call-done, f32[8,128]{1,0:T(8,128)S(1)} %multiply_exponential_fusion.1), kind=kOutput, calls=%fused_computation.28 | convolution fusion | flops 4300734464 | bytes 17829896 | tf_op jit(solution)/shard_map/jis,jic->sc/dot_general | solution.py:81
  197.5 42.5 %bitcast_multiply_fusion = f32[512,4096]{1,0:T(8,128)} fusion(f32[512,4096,1]{1,0,2:T(8,128)} %fusion.11, bf16[8,768,1024]{2,1,0:T(8,128)(2,1)} %gather_fusion.7, bf16[8,768,1024]{2,1,0:T(8,128)(2,1)} %gather_fusion.6, bf16[8,768,1024]{2,1,0:T(8,128)(2,1)} %gather_fusion.5, bf16[8,768,1024]{2,1,0:T(8,128)(2,1)S(1)} %copy-done.3, ...), kind=kOutput, calls=%fused_computation.25 | convolution fusion | flops 26009927680 | bytes 73424904 | tf_op jit(solution)/shard_map/jis,jic->sc/dot_general | solution.py:87
  240.0 9.0 %copy.27 = f32[512,4096]{0,1:T(8,128)} copy(f32[512,4096]{1,0:T(8,128)} %bitcast_multiply_fusion) | data formatting | bytes 16777216 | tf_op jit(solution)/shard_map/mul | solution.py:94
  249.1 30.0 %convert_bitcast_fusion = bf16[512,1,8,8,128]{4,0,3,2,1:T(8,128)(2,1)} fusion(f32[512,8,8,64]{0,3,2,1:T(8,128)} %bitcast.44, f32[64,64]{1,0:T(8,128)S(1)} %get-tuple-element.13, f32[64,64]{1,0:T(8,128)S(1)} %get-tuple-element.14), kind=kOutput, calls=%fused_computation.27 | convolution fusion | flops 3225436160 | bytes 16809984 | tf_op jit(solution)/shard_map/dot_general | solution.py:96
  279.1 12.0 %copy.28 = bf16[512,1,8,8,128]{4,3,2,1,0:T(8,128)(2,1)} copy(bf16[512,1,8,8,128]{4,0,3,2,1:T(8,128)(2,1)} %convert_bitcast_fusion) | data formatting | bytes 16777216 | tf_op jit(solution)/shard_map/broadcast_in_dim | solution.py:99
  291.1 8.3 %all-to-all-start = ((bf16[512,1,8,8,128]{4,3,2,1,0:T(8,128)(2,1)}), bf16[512,1,8,8,128]{4,3,2,1,0:T(8,128)(2,1)}, u32[]{:S(2)}, u32[]{:S(2)}) async-start(bf16[512,1,8,8,128]{4,3,2,1,0:T(8,128)(2,1)} %copy.28), calls=%async_computation | async-start | bytes 16777216 | tf_op jit(solution)/shard_map/all_to_all | solution.py:98
  299.4 0.6 dynamic_slice.13
  300.1 0.6 gather_fusion
  300.7 1.3 cosine_multiply_fusion
  302.0 0.2 fusion.40
  302.2 155.2 %all-to-all-done = bf16[512,1,8,8,128]{4,3,2,1,0:T(8,128)(2,1)} async-done(((bf16[512,1,8,8,128]{4,3,2,1,0:T(8,128)(2,1)}), bf16[512,1,8,8,128]{4,3,2,1,0:T(8,128)(2,1)}, u32[]{:S(2)}, u32[]{:S(2)}) %all-to-all-start) | async-done | bytes 8388640 | tf_op jit(solution)/shard_map/all_to_all | solution.py:98
  457.4 19.1 %fusion.9 = f32[32,2,8,128,128,1]{3,4,5,2,1,0:T(8,128)} fusion(bf16[32,8,2,8,8,128]{5,4,3,0,2,1:T(8,128)(2,1)} %bitcast.12, f32[64,8,8]{0,2,1:T(8,128)S(1)} %get-tuple-element.12, f32[64,8,8]{0,2,1:T(8,128)S(1)} %get-tuple-element.11), kind=kOutput, calls=%fused_computation.23 | convolution fusion | flops 1073766400 | bytes 41975808 | tf_op jit(solution)/shard_map/kgy,trgpzyc->trpzkc/dot_general | solution.py:111
  476.4 34.5 %slice_add_fusion = (f32[1,32,16,64,64]{4,3,2,1,0:T(8,128)}, f32[1,32,16,64,64]{4,3,2,1,0:T(8,128)}) fusion(f32[1,32,16,128,128]{4,3,2,1,0:T(8,128)} %bitcast.43), kind=kLoop, calls=%fused_computation.19 | loop fusion | flops 4194304 | bytes 50331648 | tf_op jit(solution)/shard_map/add | solution.py:36
  510.9 12.0 %maximum_bitcast_fusion = f32[32,16,64,128]{3,2,1,0:T(8,128)S(1)} fusion(f32[1,32,16,64,64]{4,3,2,1,0:T(8,128)} %get-tuple-element.10, f32[1,32,16,64,64]{4,3,2,1,0:T(8,128)} %get-tuple-element.9), kind=kLoop, calls=%fused_computation.20 | loop fusion | flops 4194304 | bytes 33554432 | tf_op jit(solution)/shard_map/mul | solution.py:121
  523.0 12.1 %broadcast_multiply_fusion = f32[2,32,16,64,128]{4,3,2,1,0:T(8,128)} fusion(f32[32,16,64,128]{3,2,1,0:T(8,128)S(1)} %maximum_bitcast_fusion, f32[2]{0:T(128)S(1)} %cosine_multiply_fusion), kind=kLoop, calls=%fused_computation.21 | loop fusion | flops 8388608 | bytes 50331656 | tf_op jit(solution)/shard_map/mul | solution.py:121
  535.1 134.6 %all-reduce.2.cloned.1.call-done = f32[2,32,16,64,128]{4,3,2,1,0:T(8,128)} async-done(((f32[2,32,16,64,128]{4,3,2,1,0:T(8,128)}), f32[2,32,16,64,128]{4,3,2,1,0:T(8,128)}) %all-reduce.2.cloned.1.call-update) | async-done | bytes 33554448 | tf_op jit(solution)/shard_map/psum | solution.py:121
  669.6 12.0 %constant_dynamic-slice_fusion = f32[1,32,16,64,128]{4,3,2,1,0:T(8,128)} fusion(f32[2,32,16,64,128]{4,3,2,1,0:T(8,128)} %all-reduce.2.cloned.1.call-done, s32[]{:T(128)S(6)} %select_n.63), kind=kLoop, calls=%fused_computation.77 | loop fusion | bytes 33554436 | tf_op jit(solution)/shard_map/dynamic_slice | solution.py:122
  (32 shorter events, 0.3 us)
Async XLA Ops:
  6.5 22.7 %copy-start = (f32[1024]{0:T(1024)S(1)}, f32[1024]{0:T(1024)}, u32[]{:S(2)}) copy-start(f32[1024]{0:T(1024)} %param.15) | copy-start | bytes 12292
  6.5 14.3 %copy-start.7 = (s32[8]{0:T(128)S(1)}, s32[8]{0:T(128)}, u32[]{:S(2)}) copy-start(s32[8]{0:T(128)} %param.12) | copy-start | bytes 100
  6.5 179.0 %all-gather.2.cloned.1.call-start = ((), (), s32[]{:S(2)}) async-start(), calls=%async_computation.1 | async-start | bytes 8257536 | tf_op jit(solution)/shard_map/all_gather | solution.py:74
  20.8 9.0 %copy-start.5 = (s32[2]{0:T(128)S(1)}, s32[2]{0:T(128)}, u32[]{:S(2)}) copy-start(s32[2]{0:T(128)} %param.20) | copy-start | bytes 28
  171.3 10.9 %copy-start.4 = (f32[6144]{0:T(1024)S(1)}, f32[6144]{0:T(1024)}, u32[]{:S(2)}) copy-start(f32[6144]{0:T(1024)} %param.16) | copy-start | bytes 73732
  171.3 12.2 %copy-start.6 = (f32[16]{0:T(128)S(1)}, f32[16]{0:T(128)}, u32[]{:S(2)}) copy-start(f32[16]{0:T(128)} %param.17) | copy-start | bytes 196
  185.6 11.9 %copy-start.3 = (bf16[8,768,1024]{2,1,0:T(8,128)(2,1)S(1)}, bf16[8,768,1024]{2,1,0:T(8,128)(2,1)}, u32[]{:S(2)}) copy-start(bf16[8,768,1024]{2,1,0:T(8,128)(2,1)} %gather_fusion.4) | copy-start | bytes 37748740
  291.1 8.4 %copy-start.8 = (f32[16]{0:T(128)S(1)}, f32[16]{0:T(128)}, u32[]{:S(2)}) copy-start(f32[16]{0:T(128)} %param.19) | copy-start | bytes 196
  291.1 9.0 %copy-start.9 = (s32[2]{0:T(128)S(1)}, s32[2]{0:T(128)}, u32[]{:S(2)}) copy-start(s32[2]{0:T(128)} %param.21) | copy-start | bytes 28
  291.1 9.0 %copy-start.2 = (f32[16]{0:T(128)S(1)}, f32[16]{0:T(128)}, u32[]{:S(2)}) copy-start(f32[16]{0:T(128)} %param.18) | copy-start | bytes 196
  291.1 166.3 %all-to-all-start = ((bf16[512,1,8,8,128]{4,3,2,1,0:T(8,128)(2,1)}), bf16[512,1,8,8,128]{4,3,2,1,0:T(8,128)(2,1)}, u32[]{:S(2)}, u32[]{:S(2)}) async-start(bf16[512,1,8,8,128]{4,3,2,1,0:T(8,128)(2,1)} %copy.28), calls=%async_computation | async-start | bytes 16777216 | tf_op jit(solution)/shard_map/all_to_all | solution.py:98
  299.4 370.2 %all-reduce.2.cloned.1.call-start = ((), (), s32[]{:S(2)}) async-start(), calls=%async_computation.2 | async-start | bytes 67108864 | tf_op jit(solution)/shard_map/psum | solution.py:121
  535.1 146.5 %copy-start.1 = (f32[1024]{0:T(1024)S(1)}, f32[1024]{0:T(1024)}, u32[]{:S(2)}) copy-start(f32[1024]{0:T(1024)} %param.15) | copy-start | bytes 12292
Sparse Core Ops, SparseCore 0:
  9.6 114.6 all-gather.1
  535.2 134.4 all-reduce.1
where the time goes:
time: 699 us; the launch traced here: 689 us
  waiting for transfers between devices  291 us (42%)
  local copies, waits for them, and re-layouts  209 us (30%)
  matrix products  103 us (15%)
  other arithmetic  61.5 us (9%)
  between operations  16 us (2%)
  starting transfers between devices  8.34 us (1%)
    all_to_all x1, waiting for transfers between devices, shards(): lax.all_to_all(tiles[:, None], ('grid', 'pw'), split_axis=0, concat_axis=...  155 us
    psum x1, waiting for transfers between devices, shards(): lax.psum(frequency_weights[:, None, None, None, None] * plane_waves[0][No...  135 us
    gather x5, local copies, waits for them, and re-layouts, shards(): jnp.take(unoccupied_blocks, orbital_block, axis=0)  76.1 us
    reshape x1, local copies, waits for them, and re-layouts, shards(): unoccupied_columns.reshape(block_count, unoccupied_block, width)  74.4 us
    dot_general x1, matrix products, shards(): jnp.einsum('jis,jic->sc', unoccupied_part, jnp.take(unoccupied_blocks, or...  42.5 us
    add x1, other arithmetic, combine_parts(): real_part = cosine[..., :width_x] + sine[..., width_x:]  34.5 us
    dot_general x1, matrix products, shards(): jnp.dot(response, row_table(NX), precision=lax.Precision.HIGHEST)  30 us
    mul x2, other arithmetic, shards(): frequency_weights[:, None, None, None, None] * plane_waves[0][None]  24.1 us
  transfers between devices with their start and end apart: 3, of which 2 were waited for; matrix products, arithmetic and copies ran while one was open for 26% of the time, Pallas kernels for 0%

commit v1 on v0

--- a/solution.py
+++ b/solution.py
@@ -2,7 +2,11 @@
 
 import jax
 import jax.numpy as jnp
+import ml_dtypes
+import numpy as np
 from jax import lax
+from jax.experimental import pallas as pl
+from jax.experimental.pallas import tpu as pltpu
 from jax.sharding import PartitionSpec as P
 
 NX = 64
@@ -42,7 +46,7 @@
     return (values * jnp.exp(-rates * time_point)[:, :, None]).astype(jnp.bfloat16)
 
 
-def shards(
+def general_shards(
     slab_orbitals,
     orbital_block,
     occupied_columns,
@@ -122,6 +126,351 @@
     return lax.dynamic_slice_in_dim(summed, moment, 1, 0)
 
 
+PAIR_CHUNKS = (1, 2, 1)
+DEPTH = 1024
+SPLIT_CALLS = 3
+GROUP = 16
+VMEM_LIMIT = 56 * 2**20
+AXES = ("grid", "tm", "pw")
+SWAP = [(0, 1), (1, 0)]
+
+
+def host_angles(number):
+    indices = np.arange(number)
+    return (indices[:, None] * indices[None, :] % number) * (2.0 * math.pi / number)
+
+
+def line_operator(lines):
+    angles = host_angles(lines)
+    table = np.concatenate([np.cos(angles), np.sin(angles)]) / math.sqrt(lines)
+    return table.astype(np.float32).astype(ml_dtypes.bfloat16)
+
+
+def row_operator(number):
+    angles = host_angles(number)
+    cosine, sine = np.cos(angles) / math.sqrt(number), np.sin(angles) / math.sqrt(number)
+    one = np.stack([np.concatenate([cosine, -sine], 1), np.concatenate([-sine, -cosine], 1)])
+    both = np.einsum("sxc,pq->spxqc", one, np.eye(2)).reshape(4 * number, 4 * number)
+    high = both.astype(np.float32).astype(ml_dtypes.bfloat16)
+    low = (both - high.astype(np.float64)).astype(np.float32).astype(ml_dtypes.bfloat16)
+    return high, low
+
+
+def expected(flops, read_and_written):
+    return pl.CostEstimate(flops=flops, bytes_accessed=read_and_written, transcendentals=0)
+
+
+def split_planes(columns, core, first, steps, previous):
+    count, planes, width = columns.shape
+    half = width // 2
+    pieces = [2 * pairs for pairs in PAIR_CHUNKS]
+    group = 256 // planes
+
+    def kernel(core_ref, in_ref, *rest):
+        out_refs = rest[-len(pieces) :]
+        rows = lax.broadcasted_iota(jnp.int32, (256, 256), 0)
+        cols = lax.broadcasted_iota(jnp.int32, (256, 256), 1)
+        order = jnp.where((rows % group) * planes + rows // group == cols, 1.0, 0.0)
+        order = order.astype(jnp.bfloat16)
+        for b in range(DEPTH // group):
+            part = in_ref[b * group : (b + 1) * group].reshape(256, half)
+            moved = jnp.dot(order, part, preferred_element_type=jnp.float32)
+            moved = moved.astype(jnp.bfloat16).reshape(planes, group, half)
+            start = 0
+            for out_ref, size in zip(out_refs, pieces):
+                out_ref[:, b * group : (b + 1) * group, :] = moved[start : start + size]
+                start += size
+
+    operands, extra, aliases = [core, columns], [], {}
+    if previous is not None:
+        operands += previous
+        extra = [pl.BlockSpec(memory_space=pl.ANY)] * len(pieces)
+        aliases = {2 + n: n for n in range(len(pieces))}
+    return pl.pallas_call(
+        kernel,
+        grid_spec=pltpu.PrefetchScalarGridSpec(
+            num_scalar_prefetch=1,
+            grid=(steps,),
+            in_specs=[pl.BlockSpec((DEPTH, planes, half), lambda i, core: (first + i, 0, core[0]))] + extra,
+            out_specs=[pl.BlockSpec((size, DEPTH, half), lambda i, core: (0, first + i, 0)) for size in pieces],
+        ),
+        out_shape=[jax.ShapeDtypeStruct((size, count, half), jnp.bfloat16) for size in pieces],
+        input_output_aliases=aliases,
+        compiler_params=pltpu.CompilerParams(vmem_limit_bytes=VMEM_LIMIT),
+        cost_estimate=expected(steps * DEPTH * planes * half * 512, steps * DEPTH * planes * half * 4),
+        name="split_planes",
+    )(*operands)
+
+
+def weigh(pieces, places, core, decays, previous):
+    occupied_decay, unoccupied_decay = decays
+    times, occupied_count = occupied_decay.shape
+    unoccupied_count = unoccupied_decay.shape[1]
+    flat = [entry for block in pieces for entry in block]
+    half = SLAB // 2
+    width = flat[0][0].shape[1]
+    occupied_block = occupied_count * width // (occupied_count + unoccupied_count)
+    unoccupied_block = width - occupied_block
+
+    def kernel(place_ref, core_ref, occ_ref, unocc_ref, *rest):
+        refs, (occ_out, unocc_out) = list(rest[: len(flat)]), rest[-2:]
+        for n, block in enumerate(pieces):
+            mine, refs = refs[: len(block)], refs[len(block) :]
+
+            @pl.when(pl.program_id(0) == n)
+            def _():
+                for ref, (array, other, start) in zip(mine, block):
+                    side = 1 - core_ref[0] if other else core_ref[0]
+                    at = pl.ds(pl.multiple_of(side * half + start, GROUP), array.shape[0])
+                    values = ref[...].astype(jnp.float32)
+                    for t in range(times):
+                        occ_out[t, at, :] = (values[:, :occupied_block] * occ_ref[t : t + 1, :]).astype(jnp.bfloat16)
+                        unocc_out[t, at, :] = (values[:, occupied_block:] * unocc_ref[t : t + 1, :]).astype(jnp.bfloat16)
+
+    operands = [places, core, occupied_decay, unoccupied_decay] + [entry[0] for entry in flat]
+    extra, aliases = [], {}
+    if previous is not None:
+        aliases = {len(operands): 0, len(operands) + 1: 1}
+        operands += previous
+        extra = [pl.BlockSpec(memory_space=pl.ANY)] * 2
+    elements = sum(entry[0].size for entry in flat)
+    return pl.pallas_call(
+        kernel,
+        grid_spec=pltpu.PrefetchScalarGridSpec(
+            num_scalar_prefetch=2,
+            grid=(len(pieces),),
+            in_specs=[
+                pl.BlockSpec((times, occupied_block), lambda n, place, core: (0, place[n])),
+                pl.BlockSpec((times, unoccupied_block), lambda n, place, core: (0, place[n])),
+            ]
+            + [pl.BlockSpec(entry[0].shape, lambda n, place, core: (0, 0)) for entry in flat]
+            + extra,
+            out_specs=[
+                pl.BlockSpec((times, 2 * half, occupied_block), lambda n, place, core: (0, 0, place[n])),
+                pl.BlockSpec((times, 2 * half, unoccupied_block), lambda n, place, core: (0, 0, place[n])),
+            ],
+        ),
+        out_shape=[
+            jax.ShapeDtypeStruct((times, 2 * half, occupied_count), jnp.bfloat16),
+            jax.ShapeDtypeStruct((times, 2 * half, unoccupied_count), jnp.bfloat16),
+        ],
+        input_output_aliases=aliases,
+        compiler_params=pltpu.CompilerParams(vmem_limit_bytes=VMEM_LIMIT),
+        cost_estimate=expected(elements * 2, elements * 6),
+        name="weigh",
+    )(*operands)
+
+
+def respond(weights, occupied, unoccupied, occupied_planes, unoccupied_planes, owners):
+    times, slab, occupied_count = occupied.shape
+    planes, unoccupied_count, width = unoccupied_planes.shape
+    lines = width // NX
+    grid_size, pw_size = owners
+    rows = slab // (grid_size * pw_size)
+    steps = unoccupied_count // DEPTH
+
+    def kernel(weight_ref, occ_ref, unocc_ref, occ_col_ref, unocc_col_ref, out_ref, occ_acc, unocc_acc):
+        step = pl.program_id(0)
+
+        @pl.when(step == 0)
+        def _():
+            unocc_acc[...] = jnp.zeros_like(unocc_acc)
+            left = occ_ref[...].reshape(times * slab, occupied_count)
+            for z in range(planes):
+                occ_acc[z] = jnp.dot(left, occ_col_ref[z], preferred_element_type=jnp.float32)
+
+        left = unocc_ref[...].reshape(times * slab, DEPTH)
+        for z in range(planes):
+            unocc_acc[z] += jnp.dot(left, unocc_col_ref[z], preferred_element_type=jnp.float32)
+
+        @pl.when(step == steps - 1)
+        def _():
+            for pair in range(planes // 2):
+                mixed = []
+                for z in (2 * pair, 2 * pair + 1):
+                    product = occ_acc[z] * unocc_acc[z]
+                    first, second = product[:slab], product[slab:]
+                    mixed.append([
+                        (weight_ref[f, 0] * first + weight_ref[f, 1] * second).astype(jnp.bfloat16)
+                        for f in range(times)
+                    ])
+                for f in range(times):
+                    even, odd = mixed[0][f], mixed[1][f]
+                    for y in range(lines):
+                        at = slice(y * NX, (y + 1) * NX)
+                        both = jnp.concatenate([even[:, at], odd[:, at]], axis=1)
+                        out_ref[:, f, :, pair, y] = both.reshape(grid_size, pw_size, rows, 2 * NX)
+
+    out_shape = (grid_size, times, pw_size, planes // 2, lines, rows, 2 * NX)
+    depth = occupied_count + unoccupied_count
+    return pl.pallas_call(
+        kernel,
+        grid=(steps,),
+        in_specs=[
+            pl.BlockSpec(memory_space=pltpu.SMEM),
+            pl.BlockSpec((times, slab, occupied_count), lambda k: (0, 0, 0)),
+            pl.BlockSpec((times, slab, DEPTH), lambda k: (0, 0, k)),
+            pl.BlockSpec((planes, occupied_count, width), lambda k: (0, 0, 0)),
+            pl.BlockSpec((planes, DEPTH, width), lambda k: (0, k, 0)),
+        ],
+        out_specs=pl.BlockSpec(out_shape, lambda k: (0,) * len(out_shape)),
+        out_shape=jax.ShapeDtypeStruct(out_shape, jnp.bfloat16),
+        scratch_shapes=[
+            pltpu.VMEM((planes, times * slab, width), jnp.float32),
+            pltpu.VMEM((planes, times * slab, width), jnp.float32),
+        ],
+        compiler_params=pltpu.CompilerParams(vmem_limit_bytes=VMEM_LIMIT),
+        cost_estimate=expected(2 * times * slab * depth * planes * width, 2 * depth * (times * slab + planes * width)),
+        name="respond",
+    )(weights, occupied, unoccupied, occupied_planes, unoccupied_planes)
+
+
+def transform(received, tables, previous, first_pair, total_planes):
+    sources, pw_size, pairs, lines, rows, width = received.shape
+    number = sources * lines
+    line_table, high_table, low_table = tables
+    pairs_of_pw = total_planes // (2 * pw_size)
+    together = 2
+    batch = 8
+
+    def kernel(line_ref, high_ref, low_ref, in_ref, *rest):
+        out_ref, sides_ref = rest[-2:]
+        images = jnp.swapaxes(in_ref[...].reshape(number, rows, width), 0, 1)
+        for first in range(0, rows, together):
+            group = range(first, first + together)
+            side_by_side = jnp.concatenate([images[r] for r in group], axis=1)
+            lined = jnp.dot(line_ref[...], side_by_side, preferred_element_type=jnp.float32)
+            for r in group:
+                at, lanes = slice(r * number, (r + 1) * number), slice((r - first) * width, (r - first + 1) * width)
+                sides_ref[at, :width] = lined[:number, lanes]
+                sides_ref[at, width:] = lined[number:, lanes]
+        for first in range(0, rows, batch):
+            sides = sides_ref[first * number : (first + batch) * number]
+            high = sides.astype(jnp.bfloat16)
+            low = (sides - high.astype(jnp.float32)).astype(jnp.bfloat16)
+            waves = jnp.dot(high, high_ref[...], preferred_element_type=jnp.float32)
+            waves += jnp.dot(low, high_ref[...], preferred_element_type=jnp.float32)
+            waves += jnp.dot(high, low_ref[...], preferred_element_type=jnp.float32)
+            for plane in range(2):
+                lanes = slice(plane * width, (plane + 1) * width)
+                out_ref[0, first : first + batch, plane] = waves[:, lanes].reshape(batch, number, width)
+
+    out_shape = (1, rows, total_planes, number, width)
+    whole = lambda p, j: (0, 0)
+    operands = [line_table, high_table, low_table, received]
+    in_specs = [
+        pl.BlockSpec(line_table.shape, whole),
+        pl.BlockSpec(high_table.shape, whole),
+        pl.BlockSpec(low_table.shape, whole),
+        pl.BlockSpec((sources, 1, 1, lines, rows, width), lambda p, j: (0, p, j, 0, 0, 0)),
+    ]
+    aliases = {}
+    if previous is not None:
+        aliases = {len(operands): 0}
+        operands.append(previous)
+        in_specs.append(pl.BlockSpec(memory_space=pl.ANY))
+    work = pw_size * pairs * rows * number
+    return pl.pallas_call(
+        kernel,
+        grid=(pw_size, pairs),
+        in_specs=in_specs,
+        out_specs=pl.BlockSpec(
+            (1, rows, 2, number, width), lambda p, j: (0, 0, p * pairs_of_pw + first_pair + j, 0, 0)
+        ),
+        out_shape=jax.ShapeDtypeStruct(out_shape, jnp.float32),
+        scratch_shapes=[pltpu.VMEM((rows * number, 2 * width), jnp.float32)],
+        input_output_aliases=aliases,
+        compiler_params=pltpu.CompilerParams(vmem_limit_bytes=VMEM_LIMIT),
+        cost_estimate=expected(work * 2 * width * (2 * number + 6 * width), work * width * 10),
+        name="transform",
+    )(*operands)
+
+
+def ring_places(number):
+    order = list(range(0, number, 2)) + list(range(number - 1, 0, -2))
+    onward = [(order[n], order[(n + 1) % number]) for n in range(number)]
+    back = [(to, source) for source, to in onward]
+    arrivals = np.zeros((number, number), np.int32)
+    for n, device in enumerate(order):
+        sequence = [n]
+        for hop in range(1, number // 2):
+            sequence += [n - hop, n + hop]
+        sequence.append(n + number // 2)
+        arrivals[device] = [order[m % number] for m in sequence]
+    return onward, back, arrivals
+
+
+def gather_weighed(mine, orbital_block, core, decays):
+    number = lax.axis_size("grid")
+    onward, back, arrivals = ring_places(number)
+    places = orbital_block[jnp.asarray(arrivals)[lax.axis_index("grid")]]
+    middle = mine.shape[0] // 2
+
+    def pair(rows, start):
+        return [(rows, 0, start), (lax.ppermute(rows, "tm", SWAP), 1, start)]
+
+    weighed = weigh([pair(mine, 0)], places[:1], core, decays, None)
+    up = down = mine
+    for hop in range(1, number // 2):
+        up, down = lax.ppermute(up, "grid", onward), lax.ppermute(down, "grid", back)
+        blocks = [pair(up, 0), pair(down, 0)]
+        weighed = weigh(blocks, places[2 * hop - 1 : 2 * hop + 1], core, decays, weighed)
+    up, down = lax.ppermute(up[:middle], "grid", onward), lax.ppermute(down[middle:], "grid", back)
+    blocks = [pair(up, 0) + pair(down, middle)]
+    return weigh(blocks, places[number - 1 :], core, decays, weighed)
+
+
+def shards(
+    slab_orbitals,
+    orbital_block,
+    occupied_columns,
+    unoccupied_columns,
+    occupied_gap,
+    unoccupied_gap,
+    time_table,
+    frequency_table,
+    time_weight,
+    time_index,
+    frequency_index,
+):
+    grid_size, tm_size, pw_size = (lax.axis_size(axis) for axis in AXES)
+    planes_local = occupied_columns.shape[1]
+    moment = lax.axis_index("tm").astype(jnp.int32)
+    core = moment.reshape(1)
+    half = SLAB // tm_size
+
+    rows = jnp.transpose(slab_orbitals[0])
+    mine = lax.dynamic_slice_in_dim(rows, moment * half, half, 0)
+
+    time_points = time_table[time_index]
+    frequency_weights = time_weight[time_index][None, :] * jnp.cos(
+        frequency_table[frequency_index][:, None] * time_points[None, :]
+    )
+    occupied_decay = jnp.exp(-occupied_gap[None, :] * time_points[:, None])
+    unoccupied_decay = jnp.exp(-unoccupied_gap[None, :] * time_points[:, None])
+
+    occupied, unoccupied = gather_weighed(mine, orbital_block, core, (occupied_decay, unoccupied_decay))
+    occupied_planes = split_planes(occupied_columns, core, 0, occupied_columns.shape[0] // DEPTH, None)
+    unoccupied_planes = None
+    steps = unoccupied_columns.shape[0] // DEPTH // SPLIT_CALLS
+    for call in range(SPLIT_CALLS):
+        unoccupied_planes = split_planes(unoccupied_columns, core, call * steps, steps, unoccupied_planes)
+
+    tables = (jnp.asarray(line_operator(NY)),) + tuple(jnp.asarray(t) for t in row_operator(NX))
+    result = None
+    first_pair = 0
+    for pairs, occupied_part, unoccupied_part in zip(PAIR_CHUNKS, occupied_planes, unoccupied_planes):
+        sent = respond(
+            -frequency_weights, occupied, unoccupied, occupied_part, unoccupied_part, (grid_size, pw_size)
+        )
+        sent = sent.reshape((-1,) + sent.shape[3:])
+        received = lax.all_to_all(sent, AXES, split_axis=0, concat_axis=0, tiled=True)
+        received = received.reshape((grid_size * tm_size, pw_size) + received.shape[1:])
+        result = transform(received, tables, result, first_pair, pw_size * planes_local)
+        first_pair += pairs
+    return result
+
+
 def solution(mesh):
     placed = (
         P("grid", None, None),
@@ -136,8 +485,11 @@
         P(),
         P(),
     )
+    rows = SLAB // (mesh.shape["grid"] * mesh.shape["pw"])
+    lanes = NX * NY // (mesh.shape["grid"] * mesh.shape["tm"])
+    fits = rows % GROUP == 0 and lanes % 128 == 0
     return jax.shard_map(
-        shards,
+        shards if fits else general_shards,
         mesh=mesh,
         in_specs=placed,
         out_specs=P("tm", ("grid", "pw"), None, None, None),

time: 699 us -> 229 us (0.33); the launches traced: 689 us -> 229 us
  waiting for transfers between devices: 291 us -> 75.9 us
  local copies, waits for them, and re-layouts: 209 us -> 9.46 us
  Pallas kernels: 0 us -> 115 us
  matrix products: 103 us -> 0 us
  other arithmetic: 61.5 us -> 4.21 us
  between operations: 16 us -> 0.23 us
  starting transfers between devices: 8.34 us -> 23.3 us
    psum x1 -> x0, waiting for transfers between devices: 135 us -> none  [shards(): lax.psum(frequency_weights[:, None, None, None, None] * plane_waves[0][No...]
    pallas_call x0 -> x15, Pallas kernels: none -> 115 us  [the longest x3 52.2 us: respond(): pl.pallas_call(kernel, grid=(steps,), in_specs=[pl.BlockSpec(memory_space...]
    all_to_all x1 -> x3, waiting for transfers between devices: 155 us -> 50.7 us  [shards(): lax.all_to_all(sent, AXES, split_axis=0, concat_axis=0, tiled=True)]
    dot_general x4 -> x0, matrix products: 103 us -> none  [the longest x1 42.5 us: shards(): jnp.einsum('jis,jic->sc', unoccupied_part, jnp.take(unoccupied_blocks, or...]
    reshape x3 -> x0, local copies, waits for them, and re-layouts: 87.9 us -> none  [the longest x1 74.4 us: shards(): unoccupied_columns.reshape(block_count, unoccupied_block, width)]
    gather x9 -> x4, local copies, waits for them, and re-layouts: 86.2 us -> 3.21 us  [the longest x1 1.29 us: shards(): time_points = time_table[time_index]]
    add x1 -> x0, other arithmetic: 34.5 us -> none  [combine_parts(): real_part = cosine[..., :width_x] + sine[..., width_x:]]
    mul x4 -> x0, other arithmetic: 25.4 us -> none  [the longest x2 24.1 us: shards(): frequency_weights[:, None, None, None, None] * plane_waves[0][None]]
  transfers between devices with their start and end apart: 3 -> 20, of which waited for: 2 -> 6; matrix products, arithmetic and copies ran while one was open for 26% -> 4% of each run, Pallas kernels for 0% -> 40%
where the time goes in v1:
time: 229 us
  Pallas kernels  115 us (50%)
  waiting for transfers between devices  75.9 us (33%)
  starting transfers between devices  23.3 us (10%)
  local copies, waits for them, and re-layouts  9.46 us (4%)
  other arithmetic  4.21 us (2%)
    pallas_call x3, Pallas kernels, respond(): pl.pallas_call(kernel, grid=(steps,), in_specs=[pl.BlockSpec(memory_space...  52.2 us
    all_to_all x3, waiting for transfers between devices, shards(): lax.all_to_all(sent, AXES, split_axis=0, concat_axis=0, tiled=True)  50.7 us
    pallas_call x4, Pallas kernels, split_planes(): pl.pallas_call(kernel, grid_spec=pltpu.PrefetchScalarGridSpec(num_scalar_...  25.6 us
    pallas_call x5, Pallas kernels, weigh(): pl.pallas_call(kernel, grid_spec=pltpu.PrefetchScalarGridSpec(num_scalar_...  19.7 us
    pallas_call x3, Pallas kernels, transform(): pl.pallas_call(kernel, grid=(pw_size, pairs), in_specs=in_specs, out_spec...  17.9 us
    ppermute x3, waiting for transfers between devices, gather_weighed(): lax.ppermute(up, 'grid', onward)  15.9 us
    all_to_all x3, starting transfers between devices, shards(): lax.all_to_all(sent, AXES, split_axis=0, concat_axis=0, tiled=True)  12.4 us
    ppermute x3, waiting for transfers between devices, gather_weighed(): lax.ppermute(down, 'grid', back)  9.27 us
  transfers between devices with their start and end apart: 20, of which 6 were waited for; matrix products, arithmetic and copies ran while one was open for 4% of the time, Pallas kernels for 40%

profile of v1, /device:TPU:0, one launch (start us, length us, event | category | flops | bytes accessed | tf_op | source)
XLA Modules:
  0.0 228.5 jit_solution(16838502031048070194)
XLA Ops:
  0.0 1.2 copy-done
  1.5 3.1 %collective-permute-start = (bf16[256,896]{1,0:T(8,128)(2,1)S(1)}, bf16[256,896]{1,0:T(8,128)(2,1)S(1)}, u32[]{:S(2)}, u32[]{:S(2)}) collective-permute-start(bf16[256,896]{1,0:T(8,128)(2,1)S(1)} %bitcast.22), channel_id=1, source_target_pairs={{0,8},{8,16},{16,24},{24,28},{28,20},{20,12},{12,4},{4,0},{1,9},{9... | collective-permute-start | bytes 1376264 | tf_op jit(solution)/shard_map/ppermute | solution.py:415
  6.1 1.3 gather_fusion.2
  7.4 7.7 %collective-permute-done.rest_0_ = bf16[256,896]{1,0:T(8,128)(2,1)S(1)} collective-permute-done((bf16[256,896]{1,0:T(8,128)(2,1)S(1)}, bf16[256,896]{1,0:T(8,128)(2,1)S(1)}, u32[]{:S(2)}, u32[]{:S(2)}) %collective-permute-start) | collective-permute-done | bytes 458784 | tf_op jit(solution)/shard_map/ppermute | solution.py:415
  15.0 1.8 collective-permute-start.1
  18.5 8.2 %collective-permute-done.1.rest_0_ = bf16[256,896]{1,0:T(8,128)(2,1)S(1)} collective-permute-done((bf16[256,896]{1,0:T(8,128)(2,1)S(1)}, bf16[256,896]{1,0:T(8,128)(2,1)S(1)}, u32[]{:S(2)}, u32[]{:S(2)}) %collective-permute-start.1) | collective-permute-done | bytes 458784 | tf_op jit(solution)/shard_map/ppermute | solution.py:415
  26.7 1.5 collective-permute-start.2
  28.2 6.7 %split_planes.5 = (bf16[2,6144,256]{2,1,0:T(8,128)(2,1)}, bf16[4,6144,256]{2,1,0:T(8,128)(2,1)}, bf16[2,6144,256]{2,1,0:T(8,128)(2,1)}) custom-call(s32[1]{0:T(128)} %bitcast.2.core_ref, bf16[6144,8,512]{2,1,0:T(8,128)(2,1)} %in_ref.7), custom_call_target="tpu_custom_call" | custom-call | flops 2147483648 | bytes 16777216 | tf_op jit(solution)/shard_map/split_planes/pallas_call | solution.py:189
  35.0 6.8 %split_planes.6 = (bf16[2,6144,256]{2,1,0:T(8,128)(2,1)}, bf16[4,6144,256]{2,1,0:T(8,128)(2,1)}, bf16[2,6144,256]{2,1,0:T(8,128)(2,1)}) custom-call(s32[1]{0:T(128)} %bitcast.2.core_ref, bf16[6144,8,512]{2,1,0:T(8,128)(2,1)} %in_ref.7, bf16[2,6144,256]{2,1,0:T(8,128)(2,1)} %get-tuple-element.38.rest_0_, ...), custom_call_target="tpu_custom_call", output_to_operand_aliasing={{0}: (2, {}), {1}: (3, {}), {2}: (4, {})} | custom-call | flops 2147483648 | bytes 16777216 | tf_op jit(solution)/shard_map/split_planes/pallas_call | solution.py:189
  46.2 9.3 %collective-permute-done.7.rest_2_ = bf16[256,896]{1,0:T(8,128)(2,1)S(1)} collective-permute-done((bf16[256,896]{1,0:T(8,128)(2,1)}, bf16[256,896]{1,0:T(8,128)(2,1)S(1)}, u32[]{:S(2)}, u32[]{:S(2)}) %collective-permute-start.7) | collective-permute-done | bytes 458784 | tf_op jit(solution)/shard_map/ppermute | solution.py:415
  55.5 1.6 collective-permute-start.3
  58.1 6.7 %split_planes.7 = (bf16[2,6144,256]{2,1,0:T(8,128)(2,1)}, bf16[4,6144,256]{2,1,0:T(8,128)(2,1)}, bf16[2,6144,256]{2,1,0:T(8,128)(2,1)}) custom-call(s32[1]{0:T(128)} %bitcast.2.core_ref, bf16[6144,8,512]{2,1,0:T(8,128)(2,1)} %in_ref.7, bf16[2,6144,256]{2,1,0:T(8,128)(2,1)} %get-tuple-element.41.rest_0_, ...), custom_call_target="tpu_custom_call", output_to_operand_aliasing={{0}: (2, {}), {1}: (3, {}), {2}: (4, {})} | custom-call | flops 2147483648 | bytes 16777216 | tf_op jit(solution)/shard_map/split_planes/pallas_call | solution.py:189
  66.0 5.3 %split_planes.4 = (bf16[2,1024,256]{2,1,0:T(8,128)(2,1)}, bf16[4,1024,256]{2,1,0:T(8,128)(2,1)}, bf16[2,1024,256]{2,1,0:T(8,128)(2,1)}) custom-call(s32[1]{0:T(128)} %bitcast.2.core_ref, bf16[1024,8,512]{2,1,0:T(8,128)(2,1)} %in_ref.4), custom_call_target="tpu_custom_call" | custom-call | flops 1073741824 | bytes 8388608 | tf_op jit(solution)/shard_map/split_planes/pallas_call | solution.py:189
  72.0 3.4 %weigh.5 = (bf16[2,512,1024]{2,1,0:T(8,128)(2,1)}, bf16[2,512,6144]{2,1,0:T(8,128)(2,1)}) custom-call(s32[1]{0:T(128)} %get-tuple-element.49.place_ref, s32[1]{0:T(128)} %bitcast.2.core_ref, f32[2,1024]{1,0:T(2,128)} %multiply_exponential_fusion.1.occ_ref, f32[2,6144]{1,0:T(2,128)} %multiply_exponential_fusion.unocc_ref, bf16[256,896]{1,0:T(8,128)(2,1)} %bitcast.25, ...), custom_call_target="tpu_custom_call" | custom-call | flops 917504 | bytes 2752512 | tf_op jit(solution)/shard_map/weigh/pallas_call | solution.py:237
  75.4 4.3 %weigh.6 = (bf16[2,512,1024]{2,1,0:T(8,128)(2,1)}, bf16[2,512,6144]{2,1,0:T(8,128)(2,1)}) custom-call(s32[2]{0:T(128)} %get-tuple-element.51.place_ref, s32[1]{0:T(128)} %bitcast.2.core_ref, f32[2,1024]{1,0:T(2,128)} %multiply_exponential_fusion.1.occ_ref, ...), custom_call_target="tpu_custom_call", output_to_operand_aliasing={{0}: (8, {}), {1}: (9, {})} | custom-call | flops 1835008 | bytes 5505024 | tf_op jit(solution)/shard_map/weigh/pallas_call | solution.py:237
  79.7 0.8 copy-done.15
  80.4 4.3 %weigh.7 = (bf16[2,512,1024]{2,1,0:T(8,128)(2,1)}, bf16[2,512,6144]{2,1,0:T(8,128)(2,1)}) custom-call(s32[2]{0:T(128)} %get-tuple-element.52.place_ref, s32[1]{0:T(128)} %bitcast.2.core_ref, f32[2,1024]{1,0:T(2,128)} %multiply_exponential_fusion.1.occ_ref, ...), custom_call_target="tpu_custom_call", output_to_operand_aliasing={{0}: (8, {}), {1}: (9, {})} | custom-call | flops 1835008 | bytes 5505024 | tf_op jit(solution)/shard_map/weigh/pallas_call | solution.py:237
  85.7 4.3 %weigh.8 = (bf16[2,512,1024]{2,1,0:T(8,128)(2,1)}, bf16[2,512,6144]{2,1,0:T(8,128)(2,1)}) custom-call(s32[2]{0:T(128)} %get-tuple-element.53.place_ref, s32[1]{0:T(128)} %bitcast.2.core_ref, f32[2,1024]{1,0:T(2,128)} %multiply_exponential_fusion.1.occ_ref, ...), custom_call_target="tpu_custom_call", output_to_operand_aliasing={{0}: (8, {}), {1}: (9, {})} | custom-call | flops 1835008 | bytes 5505024 | tf_op jit(solution)/shard_map/weigh/pallas_call | solution.py:237
  90.8 3.5 %weigh.9 = (bf16[2,512,1024]{2,1,0:T(8,128)(2,1)}, bf16[2,512,6144]{2,1,0:T(8,128)(2,1)}) custom-call(s32[1]{0:T(128)} %get-tuple-element.50.place_ref, s32[1]{0:T(128)} %bitcast.2.core_ref, f32[2,1024]{1,0:T(2,128)} %multiply_exponential_fusion.1.occ_ref, ...), custom_call_target="tpu_custom_call", output_to_operand_aliasing={{0}: (8, {}), {1}: (9, {})} | custom-call | flops 917504 | bytes 2752512 | tf_op jit(solution)/shard_map/weigh/pallas_call | solution.py:237
  94.2 14.8 %respond.5 = bf16[8,2,2,1,4,32,128]{6,5,4,3,2,1,0:T(8,128)(2,1)} custom-call(f32[2,2]{1,0:T(2,128)} %multiply_negate_fusion.weight_ref, bf16[2,512,1024]{2,1,0:T(8,128)(2,1)} %get-tuple-element.35.occ_ref, bf16[2,512,6144]{2,1,0:T(8,128)(2,1)} %get-tuple-element.36.unocc_ref, bf16[2,1024,256]{2,1,0:T(8,128)(2,1)} %get-tuple-element.47.occ_col_ref, ...), custom_call_target="tpu_custom_call" | custom-call | flops 7516192768 | bytes 22020096 | tf_op jit(solution)/shard_map/respond/pallas_call | solution.py:306
  109.0 5.1 %all-to-all-start.2 = ((bf16[32,1,4,32,128]{4,3,2,1,0:T(8,128)(2,1)}), bf16[32,1,4,32,128]{4,3,2,1,0:T(8,128)(2,1)S(1)}, u32[]{:S(2)}, u32[]{:S(2)}) async-start(bf16[32,1,4,32,128]{4,3,2,1,0:T(8,128)(2,1)} %bitcast.27), calls=%async_computation.2 | async-start | bytes 2097152 | tf_op jit(solution)/shard_map/all_to_all | solution.py:467
  114.1 22.6 %respond.4 = bf16[8,2,2,2,4,32,128]{6,5,4,3,2,1,0:T(8,128)(2,1)} custom-call(f32[2,2]{1,0:T(2,128)} %multiply_negate_fusion.weight_ref, bf16[2,512,1024]{2,1,0:T(8,128)(2,1)} %get-tuple-element.35.occ_ref, bf16[2,512,6144]{2,1,0:T(8,128)(2,1)} %get-tuple-element.36.unocc_ref, bf16[4,1024,256]{2,1,0:T(8,128)(2,1)} %get-tuple-element.45.occ_col_ref, ...), custom_call_target="tpu_custom_call" | custom-call | flops 15032385536 | bytes 29360128 | tf_op jit(solution)/shard_map/respond/pallas_call | solution.py:306
  136.7 3.4 %all-to-all-done.2 = bf16[32,1,4,32,128]{4,3,2,1,0:T(8,128)(2,1)S(1)} async-done(((bf16[32,1,4,32,128]{4,3,2,1,0:T(8,128)(2,1)}), bf16[32,1,4,32,128]{4,3,2,1,0:T(8,128)(2,1)S(1)}, u32[]{:S(2)}, u32[]{:S(2)}) %all-to-all-start.2) | async-done | bytes 1048608 | tf_op jit(solution)/shard_map/all_to_all | solution.py:467
  140.1 3.6 %all-to-all-start.1 = ((bf16[32,2,4,32,128]{4,3,2,1,0:T(8,128)(2,1)}), bf16[32,2,4,32,128]{4,3,2,1,0:T(8,128)(2,1)S(1)}, u32[]{:S(2)}, u32[]{:S(2)}) async-start(bf16[32,2,4,32,128]{4,3,2,1,0:T(8,128)(2,1)} %bitcast.21), calls=%async_computation.1 | async-start | bytes 4194304 | tf_op jit(solution)/shard_map/all_to_all | solution.py:467
  143.8 14.8 %respond.3 = bf16[8,2,2,1,4,32,128]{6,5,4,3,2,1,0:T(8,128)(2,1)} custom-call(f32[2,2]{1,0:T(2,128)} %multiply_negate_fusion.weight_ref, bf16[2,512,1024]{2,1,0:T(8,128)(2,1)} %get-tuple-element.35.occ_ref, bf16[2,512,6144]{2,1,0:T(8,128)(2,1)} %get-tuple-element.36.unocc_ref, bf16[2,1024,256]{2,1,0:T(8,128)(2,1)} %get-tuple-element.37.occ_col_ref, ...), custom_call_target="tpu_custom_call" | custom-call | flops 7516192768 | bytes 22020096 | tf_op jit(solution)/shard_map/respond/pallas_call | solution.py:306
  158.5 34.0 %all-to-all-done.1 = bf16[32,2,4,32,128]{4,3,2,1,0:T(8,128)(2,1)S(1)} async-done(((bf16[32,2,4,32,128]{4,3,2,1,0:T(8,128)(2,1)}), bf16[32,2,4,32,128]{4,3,2,1,0:T(8,128)(2,1)S(1)}, u32[]{:S(2)}, u32[]{:S(2)}) %all-to-all-start.1) | async-done | bytes 2097184 | tf_op jit(solution)/shard_map/all_to_all | solution.py:467
  192.5 3.7 %all-to-all-start = ((bf16[32,1,4,32,128]{4,3,2,1,0:T(8,128)(2,1)}), bf16[32,1,4,32,128]{4,3,2,1,0:T(8,128)(2,1)S(1)}, u32[]{:S(2)}, u32[]{:S(2)}) async-start(bf16[32,1,4,32,128]{4,3,2,1,0:T(8,128)(2,1)} %bitcast.26), calls=%async_computation | async-start | bytes 2097152 | tf_op jit(solution)/shard_map/all_to_all | solution.py:467
  196.2 5.0 %transform.3.rest_0_ = f32[1,32,16,64,128]{4,3,2,1,0:T(8,128)} custom-call(bf16[128,64]{1,0:T(8,128)(2,1)} %constant.33.clone.line_ref, bf16[256,256]{1,0:T(8,128)(2,1)} %constant.34.clone.high_ref, bf16[256,256]{1,0:T(8,128)(2,1)} %constant.35.clone.low_ref, bf16[16,2,1,4,32,128]{5,4,3,2,1,0:T(8,128)(2,1)} %bitcast.19), custom_call_target="tpu_custom_call" | custom-call | flops 939524096 | bytes 5242880 | tf_op jit(solution)/shard_map/transform/pallas_call | solution.py:373
  201.2 7.8 %transform.4.rest_0_ = f32[1,32,16,64,128]{4,3,2,1,0:T(8,128)} custom-call(bf16[128,64]{1,0:T(8,128)(2,1)} %constant.33.clone.line_ref, bf16[256,256]{1,0:T(8,128)(2,1)} %constant.34.clone.high_ref, bf16[256,256]{1,0:T(8,128)(2,1)} %constant.35.clone.low_ref, bf16[16,2,2,4,32,128]{5,4,3,2,1,0:T(8,128)(2,1)} %bitcast.18, ...), custom_call_target="tpu_custom_call", output_to_operand_aliasing={{}: (4, {})} | custom-call | flops 1879048192 | bytes 10485760 | tf_op jit(solution)/shard_map/transform/pallas_call | solution.py:373
  209.0 13.4 %all-to-all-done = bf16[32,1,4,32,128]{4,3,2,1,0:T(8,128)(2,1)S(1)} async-done(((bf16[32,1,4,32,128]{4,3,2,1,0:T(8,128)(2,1)}), bf16[32,1,4,32,128]{4,3,2,1,0:T(8,128)(2,1)S(1)}, u32[]{:S(2)}, u32[]{:S(2)}) %all-to-all-start) | async-done | bytes 1048608 | tf_op jit(solution)/shard_map/all_to_all | solution.py:467
  222.4 1.0 copy-done.7
  223.4 5.1 %transform.5 = f32[1,32,16,64,128]{4,3,2,1,0:T(8,128)} custom-call(bf16[128,64]{1,0:T(8,128)(2,1)} %constant.33.clone.line_ref, bf16[256,256]{1,0:T(8,128)(2,1)} %constant.34.clone.high_ref, bf16[256,256]{1,0:T(8,128)(2,1)} %constant.35.clone.low_ref, bf16[16,2,1,4,32,128]{5,4,3,2,1,0:T(8,128)(2,1)} %bitcast.20, ...), custom_call_target="tpu_custom_call", output_to_operand_aliasing={{}: (4, {})} | custom-call | flops 939524096 | bytes 5242880 | tf_op jit(solution)/shard_map/transform/pallas_call | solution.py:373
  (89 shorter events, 12.4 us)
Async XLA Ops:
  1.5 33.5 %copy-start.8 = (bf16[1,896,256]{1,2,0:T(8,128)(2,1)}, bf16[1,896,256]{1,2,0:T(8,128)(2,1)S(1)}, u32[]{:S(2)}) copy-start(bf16[1,896,256]{1,2,0:T(8,128)(2,1)S(1)} %copy.34) | copy-start | bytes 1376260
  1.5 13.5 %collective-permute-start = (bf16[256,896]{1,0:T(8,128)(2,1)S(1)}, bf16[256,896]{1,0:T(8,128)(2,1)S(1)}, u32[]{:S(2)}, u32[]{:S(2)}) collective-permute-start(bf16[256,896]{1,0:T(8,128)(2,1)S(1)} %bitcast.22), channel_id=1, source_target_pairs={{0,8},{8,16},{16,24},{24,28},{28,20},{20,12},{12,4},{4,0},{1,9},{9... | collective-permute-start | bytes 1376264 | tf_op jit(solution)/shard_map/ppermute | solution.py:415
  4.6 50.9 %collective-permute-start.16 = (bf16[256,896]{1,0:T(8,128)(2,1)S(1)}, bf16[256,896]{1,0:T(8,128)(2,1)S(1)}, u32[]{:S(2)}, u32[]{:S(2)}) collective-permute-start(bf16[256,896]{1,0:T(8,128)(2,1)S(1)} %bitcast.23), channel_id=1, source_target_pairs={{0,2},{2,0},{1,3},{3,1},{4,6},{6,4},{5,7},{7,5},{8,10},{10,8},{9,1... | collective-permute-start | bytes 1376264 | tf_op jit(solution)/shard_map/ppermute | solution.py:410
  4.6 13.7 %collective-permute-start.5 = (bf16[256,896]{1,0:T(8,128)(2,1)S(1)}, bf16[256,896]{1,0:T(8,128)(2,1)S(1)}, u32[]{:S(2)}, u32[]{:S(2)}) collective-permute-start(bf16[256,896]{1,0:T(8,128)(2,1)S(1)} %bitcast.24), channel_id=1, source_target_pairs={{8,0},{16,8},{24,16},{28,24},{20,28},{12,20},{4,12},{0,4},{9,1},{1... | collective-permute-start | bytes 1376264 | tf_op jit(solution)/shard_map/ppermute | solution.py:415
  15.0 26.8 %copy-start.12 = (bf16[256,896]{1,0:T(8,128)(2,1)}, bf16[256,896]{1,0:T(8,128)(2,1)S(1)}, u32[]{:S(2)}) copy-start(bf16[256,896]{1,0:T(8,128)(2,1)S(1)} %collective-permute-done.rest_0_) | copy-start | bytes 1376260
  15.0 11.7 %collective-permute-start.1 = (bf16[256,896]{1,0:T(8,128)(2,1)S(1)}, bf16[256,896]{1,0:T(8,128)(2,1)S(1)}, u32[]{:S(2)}, u32[]{:S(2)}) collective-permute-start(bf16[256,896]{1,0:T(8,128)(2,1)S(1)} %collective-permute-done.rest_0_), channel_id=1, source_target_pairs={{0,8},{8,16},{16,24},{24,28},{28,20},{20,12},{12,4},{4,0},{1,9},{9... | collective-permute-start | bytes 1376264 | tf_op jit(solution)/shard_map/ppermute | solution.py:415
  18.2 23.6 %copy-start.13 = (bf16[256,896]{1,0:T(8,128)(2,1)}, bf16[256,896]{1,0:T(8,128)(2,1)S(1)}, u32[]{:S(2)}) copy-start(bf16[256,896]{1,0:T(8,128)(2,1)S(1)} %collective-permute-done.5.rest_2_) | copy-start | bytes 1376260
  18.2 24.1 %collective-permute-start.6 = (bf16[256,896]{1,0:T(8,128)(2,1)S(1)}, bf16[256,896]{1,0:T(8,128)(2,1)}, u32[]{:S(2)}, u32[]{:S(2)}) collective-permute-start(bf16[256,896]{1,0:T(8,128)(2,1)S(1)} %collective-permute-done.5.rest_2_), channel_id=1, source_target_pairs={{8,0},{16,8},{24,16},{28,24},{20,28},{12,20},{4,12},{0,4},{9,1},{1... | collective-permute-start | bytes 1376264 | tf_op jit(solution)/shard_map/ppermute | solution.py:415
  26.7 15.6 %copy-start.14 = (bf16[256,896]{1,0:T(8,128)(2,1)}, bf16[256,896]{1,0:T(8,128)(2,1)S(1)}, u32[]{:S(2)}) copy-start(bf16[256,896]{1,0:T(8,128)(2,1)S(1)} %collective-permute-done.1.rest_0_) | copy-start | bytes 1376260
  26.7 15.6 %collective-permute-start.2 = (bf16[256,896]{1,0:T(8,128)(2,1)S(1)}, bf16[256,896]{1,0:T(8,128)(2,1)S(1)}, u32[]{:S(2)}, u32[]{:S(2)}) collective-permute-start(bf16[256,896]{1,0:T(8,128)(2,1)S(1)} %collective-permute-done.1.rest_0_), channel_id=1, source_target_pairs={{0,8},{8,16},{16,24},{24,28},{28,20},{20,12},{12,4},{4,0},{1,9},{9... | collective-permute-start | bytes 1376264 | tf_op jit(solution)/shard_map/ppermute | solution.py:415
  35.0 9.3 %copy-start.4 = (f32[16]{0:T(128)S(1)}, f32[16]{0:T(128)}, u32[]{:S(2)}) copy-start(f32[16]{0:T(128)} %param.22) | copy-start | bytes 196
  41.8 15.4 %collective-permute-start.14 = (bf16[256,896]{1,0:T(8,128)(2,1)S(1)}, bf16[256,896]{1,0:T(8,128)(2,1)}, u32[]{:S(2)}, u32[]{:S(2)}) collective-permute-start(bf16[256,896]{1,0:T(8,128)(2,1)S(1)} %collective-permute-done.rest_0_), channel_id=1, source_target_pairs={{0,2},{2,0},{1,3},{3,1},{4,6},{6,4},{5,7},{7,5},{8,10},{10,8},{9,1... | collective-permute-start | bytes 1376264 | tf_op jit(solution)/shard_map/ppermute | solution.py:410
  41.8 15.8 %collective-permute-start.15 = (bf16[256,896]{1,0:T(8,128)(2,1)S(1)}, bf16[256,896]{1,0:T(8,128)(2,1)}, u32[]{:S(2)}, u32[]{:S(2)}) collective-permute-start(bf16[256,896]{1,0:T(8,128)(2,1)S(1)} %collective-permute-done.5.rest_2_), channel_id=1, source_target_pairs={{0,2},{2,0},{1,3},{3,1},{4,6},{6,4},{5,7},{7,5},{8,10},{10,8},{9,1... | collective-permute-start | bytes 1376264 | tf_op jit(solution)/shard_map/ppermute | solution.py:410
  42.3 15.3 %collective-permute-start.12 = (bf16[256,896]{1,0:T(8,128)(2,1)S(1)}, bf16[256,896]{1,0:T(8,128)(2,1)}, u32[]{:S(2)}, u32[]{:S(2)}) collective-permute-start(bf16[256,896]{1,0:T(8,128)(2,1)S(1)} %collective-permute-done.1.rest_0_), channel_id=1, source_target_pairs={{0,2},{2,0},{1,3},{3,1},{4,6},{6,4},{5,7},{7,5},{8,10},{10,8},{9,1... | collective-permute-start | bytes 1376264 | tf_op jit(solution)/shard_map/ppermute | solution.py:410
  42.4 22.5 %copy-start.9 = (bf16[256,896]{1,0:T(8,128)(2,1)}, bf16[256,896]{1,0:T(8,128)(2,1)S(1)}, u32[]{:S(2)}) copy-start(bf16[256,896]{1,0:T(8,128)(2,1)S(1)} %collective-permute-done.2.rest_0_) | copy-start | bytes 1376260
  42.4 13.1 %collective-permute-start.7 = (bf16[256,896]{1,0:T(8,128)(2,1)}, bf16[256,896]{1,0:T(8,128)(2,1)S(1)}, u32[]{:S(2)}, u32[]{:S(2)}) collective-permute-start(bf16[256,896]{1,0:T(8,128)(2,1)} %collective-permute-done.6.rest_2_), channel_id=1, source_target_pairs={{8,0},{16,8},{24,16},{28,24},{20,28},{12,20},{4,12},{0,4},{9,1},{1... | collective-permute-start | bytes 1376264 | tf_op jit(solution)/shard_map/ppermute | solution.py:415
  55.5 9.4 %copy-start.10 = (bf16[256,896]{1,0:T(8,128)(2,1)}, bf16[256,896]{1,0:T(8,128)(2,1)S(1)}, u32[]{:S(2)}) copy-start(bf16[256,896]{1,0:T(8,128)(2,1)S(1)} %collective-permute-done.7.rest_2_) | copy-start | bytes 1376260
  55.5 24.2 %collective-permute-start.13 = (bf16[256,896]{1,0:T(8,128)(2,1)}, bf16[256,896]{1,0:T(8,128)(2,1)S(1)}, u32[]{:S(2)}, u32[]{:S(2)}) collective-permute-start(bf16[256,896]{1,0:T(8,128)(2,1)} %collective-permute-done.6.rest_2_), channel_id=1, source_target_pairs={{0,2},{2,0},{1,3},{3,1},{4,6},{6,4},{5,7},{7,5},{8,10},{10,8},{9,1... | collective-permute-start | bytes 1376264 | tf_op jit(solution)/shard_map/ppermute | solution.py:410
  55.5 9.3 %copy-start.11 = (bf16[256,896]{1,0:T(8,128)(2,1)}, bf16[256,896]{1,0:T(8,128)(2,1)S(1)}, u32[]{:S(2)}) copy-start(bf16[256,896]{1,0:T(8,128)(2,1)S(1)} %collective-permute-done.16.rest_1_) | copy-start | bytes 1376260
  55.5 10.0 %collective-permute-start.3 = (bf16[128,896]{1,0:T(8,128)(2,1)S(1)}, bf16[128,896]{1,0:T(8,128)(2,1)S(1)}, u32[]{:S(2)}, u32[]{:S(2)}) collective-permute-start(bf16[128,896]{1,0:T(8,128)(2,1)S(1)} %slice.36), channel_id=1, source_target_pairs={{0,8},{8,16},{16,24},{24,28},{28,20},{20,12},{12,4},{4,0},{1,9},{9... | collective-permute-start | bytes 688136 | tf_op jit(solution)/shard_map/ppermute | solution.py:418
  57.1 8.4 %collective-permute-start.8 = (bf16[128,896]{1,0:T(8,128)(2,1)S(1)}, bf16[128,896]{1,0:T(8,128)(2,1)S(1)}, u32[]{:S(2)}, u32[]{:S(2)}) collective-permute-start(bf16[128,896]{1,0:T(8,128)(2,1)S(1)} %slice.37), channel_id=1, source_target_pairs={{8,0},{16,8},{24,16},{28,24},{20,28},{12,20},{4,12},{0,4},{9,1},{1... | collective-permute-start | bytes 688136 | tf_op jit(solution)/shard_map/ppermute | solution.py:418
  57.6 27.1 %collective-permute-start.10 = (bf16[256,896]{1,0:T(8,128)(2,1)S(1)}, bf16[256,896]{1,0:T(8,128)(2,1)S(1)}, u32[]{:S(2)}, u32[]{:S(2)}) collective-permute-start(bf16[256,896]{1,0:T(8,128)(2,1)S(1)} %collective-permute-done.2.rest_0_), channel_id=1, source_target_pairs={{0,2},{2,0},{1,3},{3,1},{4,6},{6,4},{5,7},{7,5},{8,10},{10,8},{9,1... | collective-permute-start | bytes 1376264 | tf_op jit(solution)/shard_map/ppermute | solution.py:410
  57.6 27.2 %collective-permute-start.11 = (bf16[256,896]{1,0:T(8,128)(2,1)S(1)}, bf16[256,896]{1,0:T(8,128)(2,1)S(1)}, u32[]{:S(2)}, u32[]{:S(2)}) collective-permute-start(bf16[256,896]{1,0:T(8,128)(2,1)S(1)} %collective-permute-done.7.rest_2_), channel_id=1, source_target_pairs={{0,2},{2,0},{1,3},{3,1},{4,6},{6,4},{5,7},{7,5},{8,10},{10,8},{9,1... | collective-permute-start | bytes 1376264 | tf_op jit(solution)/shard_map/ppermute | solution.py:410
  65.5 14.2 %copy-start.18 = (bf16[128,896]{1,0:T(8,128)(2,1)}, bf16[128,896]{1,0:T(8,128)(2,1)S(1)}, u32[]{:S(2)}) copy-start(bf16[128,896]{1,0:T(8,128)(2,1)S(1)} %collective-permute-done.3.rest_0_) | copy-start | bytes 688132
  65.5 24.5 %collective-permute-start.4 = (bf16[128,896]{1,0:T(8,128)(2,1)S(1)}, bf16[128,896]{1,0:T(8,128)(2,1)S(1)}, u32[]{:S(2)}, u32[]{:S(2)}) collective-permute-start(bf16[128,896]{1,0:T(8,128)(2,1)S(1)} %collective-permute-done.3.rest_0_), channel_id=1, source_target_pairs={{0,2},{2,0},{1,3},{3,1},{4,6},{6,4},{5,7},{7,5},{8,10},{10,8},{9,1... | collective-permute-start | bytes 688136 | tf_op jit(solution)/shard_map/ppermute | solution.py:410
  65.5 14.1 %copy-start.19 = (bf16[128,896]{1,0:T(8,128)(2,1)}, bf16[128,896]{1,0:T(8,128)(2,1)S(1)}, u32[]{:S(2)}) copy-start(bf16[128,896]{1,0:T(8,128)(2,1)S(1)} %collective-permute-done.8.rest_2_) | copy-start | bytes 688132
  65.5 24.5 %collective-permute-start.9 = (bf16[128,896]{1,0:T(8,128)(2,1)S(1)}, bf16[128,896]{1,0:T(8,128)(2,1)S(1)}, u32[]{:S(2)}, u32[]{:S(2)}) collective-permute-start(bf16[128,896]{1,0:T(8,128)(2,1)S(1)} %collective-permute-done.8.rest_2_), channel_id=1, source_target_pairs={{0,2},{2,0},{1,3},{3,1},{4,6},{6,4},{5,7},{7,5},{8,10},{10,8},{9,1... | collective-permute-start | bytes 688136 | tf_op jit(solution)/shard_map/ppermute | solution.py:410
  109.0 31.1 %all-to-all-start.2 = ((bf16[32,1,4,32,128]{4,3,2,1,0:T(8,128)(2,1)}), bf16[32,1,4,32,128]{4,3,2,1,0:T(8,128)(2,1)S(1)}, u32[]{:S(2)}, u32[]{:S(2)}) async-start(bf16[32,1,4,32,128]{4,3,2,1,0:T(8,128)(2,1)} %bitcast.27), calls=%async_computation.2 | async-start | bytes 2097152 | tf_op jit(solution)/shard_map/all_to_all | solution.py:467
  140.1 18.4 %copy-start.6 = (bf16[32,1,4,32,128]{4,3,2,1,0:T(8,128)(2,1)}, bf16[32,1,4,32,128]{4,3,2,1,0:T(8,128)(2,1)S(1)}, u32[]{:S(2)}) copy-start(bf16[32,1,4,32,128]{4,3,2,1,0:T(8,128)(2,1)S(1)} %all-to-all-done.2) | copy-start | bytes 3145732
  140.1 52.4 %all-to-all-start.1 = ((bf16[32,2,4,32,128]{4,3,2,1,0:T(8,128)(2,1)}), bf16[32,2,4,32,128]{4,3,2,1,0:T(8,128)(2,1)S(1)}, u32[]{:S(2)}, u32[]{:S(2)}) async-start(bf16[32,2,4,32,128]{4,3,2,1,0:T(8,128)(2,1)} %bitcast.21), calls=%async_computation.1 | async-start | bytes 4194304 | tf_op jit(solution)/shard_map/all_to_all | solution.py:467
  192.5 8.7 %copy-start.5 = (bf16[32,2,4,32,128]{4,3,2,1,0:T(8,128)(2,1)}, bf16[32,2,4,32,128]{4,3,2,1,0:T(8,128)(2,1)S(1)}, u32[]{:S(2)}) copy-start(bf16[32,2,4,32,128]{4,3,2,1,0:T(8,128)(2,1)S(1)} %all-to-all-done.1) | copy-start | bytes 6291460
  192.5 29.9 %all-to-all-start = ((bf16[32,1,4,32,128]{4,3,2,1,0:T(8,128)(2,1)}), bf16[32,1,4,32,128]{4,3,2,1,0:T(8,128)(2,1)S(1)}, u32[]{:S(2)}, u32[]{:S(2)}) async-start(bf16[32,1,4,32,128]{4,3,2,1,0:T(8,128)(2,1)} %bitcast.26), calls=%async_computation | async-start | bytes 2097152 | tf_op jit(solution)/shard_map/all_to_all | solution.py:467
  (11 other events, 34.3 us)

commit v2 on v0

--- a/solution.py
+++ b/solution.py
@@ -2,7 +2,11 @@
 
 import jax
 import jax.numpy as jnp
+import ml_dtypes
+import numpy as np
 from jax import lax
+from jax.experimental import pallas as pl
+from jax.experimental.pallas import tpu as pltpu
 from jax.sharding import PartitionSpec as P
 
 NX = 64
@@ -42,7 +46,7 @@
     return (values * jnp.exp(-rates * time_point)[:, :, None]).astype(jnp.bfloat16)
 
 
-def shards(
+def general_shards(
     slab_orbitals,
     orbital_block,
     occupied_columns,
@@ -122,6 +126,376 @@
     return lax.dynamic_slice_in_dim(summed, moment, 1, 0)
 
 
+PARTS = 2
+TURN = 64
+GROUP = 16
+ABSORB_LIMIT = 32 * 2**20
+TRANSFORM_LIMIT = 24 * 2**20
+SMALL_LIMIT = 2**20
+AXES = ("grid", "tm", "pw")
+SWAP = [(0, 1), (1, 0)]
+TOKEN = jax.ShapeDtypeStruct((8, 128), jnp.float32)
+
+
+def host_angles(number):
+    indices = np.arange(number)
+    return (indices[:, None] * indices[None, :] % number) * (2.0 * math.pi / number)
+
+
+def line_operator(lines):
+    angles = host_angles(lines)
+    table = np.concatenate([np.cos(angles), np.sin(angles)]) / math.sqrt(lines)
+    return table.astype(np.float32).astype(ml_dtypes.bfloat16)
+
+
+def row_operator(number):
+    angles = host_angles(number)
+    cosine, sine = np.cos(angles) / math.sqrt(number), np.sin(angles) / math.sqrt(number)
+    one = np.stack([np.concatenate([cosine, -sine], 1), np.concatenate([-sine, -cosine], 1)])
+    both = np.einsum("sxc,pq->spxqc", one, np.eye(2)).reshape(4 * number, 4 * number)
+    high = both.astype(np.float32).astype(ml_dtypes.bfloat16)
+    low = (both - high.astype(np.float64)).astype(np.float32).astype(ml_dtypes.bfloat16)
+    return high, low
+
+
+def expected(flops, read_and_written):
+    return pl.CostEstimate(flops=flops, bytes_accessed=read_and_written, transcendentals=0)
+
+
+def hbm(array):
+    return pltpu.with_memory_space_constraint(array, pltpu.HBM)
+
+
+def take_planes(block_ref, out_ref, first):
+    for start in range(0, block_ref.shape[0], TURN):
+        at = slice(start, start + TURN)
+        out_ref[:, first + start : first + start + TURN] = jnp.swapaxes(block_ref[at], 0, 1)
+
+
+def mix_response(weight_ref, acc_ref, out_ref):
+    _, planes, _, width = acc_ref.shape
+    grid_size, times, pw_size, _, lines, rows, _ = out_ref.shape
+    points = grid_size * pw_size * rows
+    for pair in range(planes // 2):
+        mixed = []
+        for z in (2 * pair, 2 * pair + 1):
+            product = acc_ref[0, z] * acc_ref[1, z]
+            first, second = product[:points], product[points:]
+            mixed.append([
+                (weight_ref[f, 0] * first + weight_ref[f, 1] * second).astype(jnp.bfloat16) for f in range(times)
+            ])
+        for f in range(times):
+            even, odd = mixed[0][f], mixed[1][f]
+            for y in range(lines):
+                at = slice(y * NX, (y + 1) * NX)
+                both = jnp.concatenate([even[:, at], odd[:, at]], axis=1)
+                out_ref[:, f, :, pair, y] = both.reshape(grid_size, pw_size, rows, 2 * NX)
+
+
+def absorb(pieces, part, places, core, decays, columns, acc, finish, last):
+    occupied_decay, unoccupied_decay = decays
+    occupied_columns, unoccupied_columns = columns
+    times, occupied_count = occupied_decay.shape
+    unoccupied_count = unoccupied_decay.shape[1]
+    planes, lanes = occupied_columns.shape[1], occupied_columns.shape[2] // 2
+    flat = [entry for block in pieces for entry in block]
+    half, width = flat[0][0].shape
+    half //= PARTS
+    points = 2 * half
+    occupied_block = occupied_count * width // (occupied_count + unoccupied_count)
+    unoccupied_block = width - occupied_block
+    first_call = acc is None
+
+    def kernel(place_ref, core_ref, occ_ref, unocc_ref, occ_col, unocc_col, *rest):
+        refs, rest = rest[: len(flat)], rest[len(flat) :]
+        if not first_call:
+            rest = rest[1:]
+        weight_ref, acc_ref, last_ref, weighed, taken = rest
+        take_planes(occ_col, taken, 0)
+        take_planes(unocc_col, taken, occupied_block)
+        for n, block in enumerate(pieces):
+            mine, refs = refs[: len(block)], refs[len(block) :]
+
+            @pl.when(pl.program_id(0) == n)
+            def _():
+                for ref, (_, other) in zip(mine, block):
+                    side = 1 - core_ref[0] if other else core_ref[0]
+                    values = ref[...].astype(jnp.float32)
+                    for t in range(times):
+                        at = pl.ds(pl.multiple_of(t * points + side * half, half), half)
+                        for low, high, rates in ((0, occupied_block, occ_ref), (occupied_block, width, unocc_ref)):
+                            scaled = values[:, low:high] * rates[t : t + 1, :]
+                            weighed[at, low:high] = scaled.astype(jnp.bfloat16)
+
+        if first_call:
+
+            @pl.when(pl.program_id(0) == 0)
+            def _():
+                acc_ref[...] = jnp.zeros_like(acc_ref)
+
+        for z in range(planes):
+            for kind, at in enumerate((slice(0, occupied_block), slice(occupied_block, width))):
+                acc_ref[kind, z] += jnp.dot(weighed[:, at], taken[z, at], preferred_element_type=jnp.float32)
+
+        if last:
+
+            @pl.when(pl.program_id(0) == len(pieces) - 1)
+            def _():
+                mix_response(weight_ref, acc_ref, last_ref)
+
+        else:
+            last_ref[...] = jnp.zeros_like(last_ref)
+
+    total = (2, planes, times * points, lanes)
+    kept = pl.BlockSpec(memory_space=pltpu.VMEM)
+    operands = [places, core, occupied_decay, unoccupied_decay, hbm(occupied_columns), hbm(unoccupied_columns)]
+    operands += [entry[0] if part == 0 else hbm(entry[0]) for entry in flat]
+    in_specs = [
+        pl.BlockSpec((times, occupied_block), lambda n, place, core: (0, place[n])),
+        pl.BlockSpec((times, unoccupied_block), lambda n, place, core: (0, place[n])),
+        pl.BlockSpec((occupied_block, planes, lanes), lambda n, place, core: (place[n], 0, core[0])),
+        pl.BlockSpec((unoccupied_block, planes, lanes), lambda n, place, core: (place[n], 0, core[0])),
+    ] + [pl.BlockSpec((half, width), lambda n, place, core: (part, 0)) for entry in flat]
+    out_specs, out_shape, aliases = [kept], [pltpu.VMEM(total, jnp.float32)], {}
+    if not first_call:
+        aliases = {len(operands): 0}
+        operands.append(acc)
+        in_specs.append(kept)
+    weights, (grid_size, pw_size) = finish
+    operands.append(weights)
+    in_specs.append(pl.BlockSpec(memory_space=pltpu.SMEM))
+    if last:
+        rows = points // (grid_size * pw_size)
+        sent = (grid_size, times, pw_size, planes // 2, lanes // NX, rows, 2 * NX)
+        out_specs.append(pl.BlockSpec(sent, lambda n, place, core: (0,) * len(sent)))
+        out_shape.append(pltpu.HBM(sent, jnp.bfloat16))
+    else:
+        out_specs.append(pl.BlockSpec(TOKEN.shape, lambda n, place, core: (0, 0)))
+        out_shape.append(pltpu.VMEM(TOKEN.shape, TOKEN.dtype))
+    blocks = len(pieces)
+    return pl.pallas_call(
+        kernel,
+        grid_spec=pltpu.PrefetchScalarGridSpec(
+            num_scalar_prefetch=2,
+            grid=(blocks,),
+            in_specs=in_specs,
+            out_specs=out_specs,
+            scratch_shapes=[
+                pltpu.VMEM((times * points, width), jnp.bfloat16),
+                pltpu.VMEM((planes, width, lanes), jnp.bfloat16),
+            ],
+        ),
+        out_shape=out_shape,
+        input_output_aliases=aliases,
+        compiler_params=pltpu.CompilerParams(vmem_limit_bytes=ABSORB_LIMIT),
+        cost_estimate=expected(
+            blocks * 2 * times * points * width * planes * lanes, blocks * 2 * width * (points + planes * lanes)
+        ),
+        name="absorb",
+    )(*operands)
+
+
+def transform(received, tables, previous, part, total_rows):
+    sources, pw_size, pairs, lines, rows, width = received.shape
+    number = sources * lines
+    line_table, high_table, low_table = tables
+    total_planes = 2 * pw_size * pairs
+    together = 2
+    batch = 8
+
+    def kernel(line_ref, high_ref, low_ref, in_ref, *rest):
+        out_ref, sides_ref = rest[-2:]
+        images = jnp.swapaxes(in_ref[...].reshape(number, rows, width), 0, 1)
+        for first in range(0, rows, together):
+            group = range(first, first + together)
+            side_by_side = jnp.concatenate([images[r] for r in group], axis=1)
+            lined = jnp.dot(line_ref[...], side_by_side, preferred_element_type=jnp.float32)
+            for r in group:
+                at, lanes = slice(r * number, (r + 1) * number), slice((r - first) * width, (r - first + 1) * width)
+                sides_ref[at, :width] = lined[:number, lanes]
+                sides_ref[at, width:] = lined[number:, lanes]
+        for first in range(0, rows, batch):
+            sides = sides_ref[first * number : (first + batch) * number]
+            high = sides.astype(jnp.bfloat16)
+            low = (sides - high.astype(jnp.float32)).astype(jnp.bfloat16)
+            waves = jnp.dot(high, high_ref[...], preferred_element_type=jnp.float32)
+            waves += jnp.dot(low, high_ref[...], preferred_element_type=jnp.float32)
+            waves += jnp.dot(high, low_ref[...], preferred_element_type=jnp.float32)
+            for plane in range(2):
+                lanes = slice(plane * width, (plane + 1) * width)
+                out_ref[0, first : first + batch, plane] = waves[:, lanes].reshape(batch, number, width)
+
+    out_shape = (1, total_rows, total_planes, number, width)
+    whole = lambda p, j: (0, 0)
+    operands = [line_table, high_table, low_table, received]
+    in_specs = [
+        pl.BlockSpec(line_table.shape, whole),
+        pl.BlockSpec(high_table.shape, whole),
+        pl.BlockSpec(low_table.shape, whole),
+        pl.BlockSpec((sources, 1, 1, lines, rows, width), lambda p, j: (0, p, j, 0, 0, 0)),
+    ]
+    aliases = {}
+    if previous is not None:
+        aliases = {len(operands): 0}
+        operands.append(previous)
+        in_specs.append(pl.BlockSpec(memory_space=pl.ANY))
+    work = pw_size * pairs * rows * number
+    return pl.pallas_call(
+        kernel,
+        grid=(pw_size, pairs),
+        in_specs=in_specs,
+        out_specs=pl.BlockSpec(
+            (1, rows, 2, number, width), lambda p, j: (0, part, p * pairs + j, 0, 0)
+        ),
+        out_shape=jax.ShapeDtypeStruct(out_shape, jnp.float32),
+        scratch_shapes=[pltpu.VMEM((rows * number, 2 * width), jnp.float32)],
+        input_output_aliases=aliases,
+        compiler_params=pltpu.CompilerParams(vmem_limit_bytes=TRANSFORM_LIMIT),
+        cost_estimate=expected(work * 2 * width * (2 * number + 6 * width), work * width * 10),
+        name="transform",
+    )(*operands)
+
+
+def ring_places(number):
+    order = list(range(0, number, 2)) + list(range(number - 1, 0, -2))
+    onward = [(order[n], order[(n + 1) % number]) for n in range(number)]
+    back = [(to, source) for source, to in onward]
+    arrivals = np.zeros((number, number), np.int32)
+    for n, device in enumerate(order):
+        sequence = [n]
+        for hop in range(1, number // 2):
+            sequence += [n - hop, n + hop]
+        sequence.append(n + number // 2)
+        arrivals[device] = [order[m % number] for m in sequence]
+    return onward, back, arrivals
+
+
+def after(arrays, token):
+    count = len(arrays)
+    anywhere = pl.BlockSpec(memory_space=pl.ANY)
+    return pl.pallas_call(
+        lambda *refs: None,
+        in_specs=[anywhere] * count + [pl.BlockSpec(memory_space=pltpu.VMEM)],
+        out_specs=[anywhere] * count,
+        out_shape=[jax.ShapeDtypeStruct(array.shape, array.dtype) for array in arrays],
+        input_output_aliases={n: n for n in range(count)},
+        compiler_params=pltpu.CompilerParams(vmem_limit_bytes=SMALL_LIMIT),
+        name="after",
+    )(*arrays, pltpu.with_memory_space_constraint(token, pltpu.VMEM))
+
+
+def choose(core, first, second):
+    def kernel(core_ref, first_ref, second_ref, out_ref):
+        @pl.when(core_ref[0] == 0)
+        def _():
+            out_ref[...] = first_ref[...]
+
+        @pl.when(core_ref[0] != 0)
+        def _():
+            out_ref[...] = second_ref[...]
+
+    kept = pl.BlockSpec(memory_space=pltpu.VMEM)
+    return pl.pallas_call(
+        kernel,
+        in_specs=[pl.BlockSpec(memory_space=pltpu.SMEM), kept, kept],
+        out_specs=kept,
+        out_shape=pltpu.VMEM(first.shape, first.dtype),
+        compiler_params=pltpu.CompilerParams(vmem_limit_bytes=4 * SMALL_LIMIT),
+        name="choose",
+    )(core, first, second)
+
+
+def swapped(rows):
+    return [(rows, 0), (lax.ppermute(rows, "tm", SWAP), 1)]
+
+
+def pick(table, index):
+    here = index[..., None] == jnp.arange(table.shape[0], dtype=index.dtype)
+    return jnp.sum(jnp.where(here, table, jnp.zeros_like(table)), axis=-1)
+
+
+def gather_and_absorb(mine, core, places, ring, absorb_blocks):
+    number = lax.axis_size("grid")
+    onward, back = ring
+    blocks, every, acc = [swapped(mine)], [], None
+    up = down = mine
+    for hops in range(1, number // 2):
+        up, down = lax.ppermute(up, "grid", onward), lax.ppermute(down, "grid", back)
+        start = len(every)
+        every += blocks
+        acc, token = absorb_blocks(blocks, 0, places[start : len(every)], acc, False)
+        up, down = after([up, down], token)
+        blocks = [swapped(up), swapped(down)]
+    far = choose(core, up, down)
+    sides = list(enumerate((onward, back)))
+    far = [
+        lax.ppermute(far, ("grid", "tm"), [(2 * source + side, 2 * to + (side ^ flip)) for side, pairs in sides for source, to in pairs])
+        for flip in (0, 1)
+    ]
+    start = len(every)
+    every += blocks
+    acc, token = absorb_blocks(blocks, 0, places[start : len(every)], acc, False)
+    own, other = after(far, token)
+    blocks = [[(own, 0), (other, 1)]]
+    _, sent = absorb_blocks(blocks, 0, places[number - 1 :], acc, True)
+    return sent, every + blocks
+
+
+def shards(
+    slab_orbitals,
+    orbital_block,
+    occupied_columns,
+    unoccupied_columns,
+    occupied_gap,
+    unoccupied_gap,
+    time_table,
+    frequency_table,
+    time_weight,
+    time_index,
+    frequency_index,
+):
+    grid_size, tm_size, pw_size = (lax.axis_size(axis) for axis in AXES)
+    moment = lax.axis_index("tm").astype(jnp.int32)
+    core = moment.reshape(1)
+    owners = grid_size * pw_size
+    rows = SLAB // owners
+    part_rows = rows // PARTS
+
+    by_owner = jnp.transpose(slab_orbitals[0]).reshape(owners, PARTS, part_rows, -1)
+    by_owner = lax.dynamic_slice_in_dim(by_owner, moment * (owners // tm_size), owners // tm_size, 0)
+    onward, back, arrivals = ring_places(grid_size)
+    arrivals = jnp.asarray(arrivals)
+    mine_first = jnp.arange(grid_size)[:, None] == lax.axis_index("grid")
+    places = pick(orbital_block, jnp.sum(jnp.where(mine_first, arrivals, 0), axis=0))
+
+    time_points = pick(time_table, time_index)
+    frequency_weights = pick(time_weight, time_index)[None, :] * jnp.cos(
+        pick(frequency_table, frequency_index)[:, None] * time_points[None, :]
+    )
+    occupied_decay = jnp.exp(-occupied_gap[None, :] * time_points[:, None])
+    unoccupied_decay = jnp.exp(-unoccupied_gap[None, :] * time_points[:, None])
+
+    columns = (occupied_columns, unoccupied_columns)
+    finish = (-frequency_weights, (grid_size, pw_size))
+
+    def absorb_blocks(pieces, part, here, acc, last):
+        return absorb(pieces, part, here, core, (occupied_decay, unoccupied_decay), columns, acc, finish, last)
+
+    tables = (jnp.asarray(line_operator(NY)),) + tuple(jnp.asarray(t) for t in row_operator(NX))
+    mine = jnp.swapaxes(by_owner, 0, 1).reshape(SLAB // tm_size, -1)
+    result = None
+    for part in range(PARTS):
+        if part == 0:
+            sent, blocks = gather_and_absorb(mine, core, places, (onward, back), absorb_blocks)
+        else:
+            _, sent = absorb_blocks(blocks, part, places, None, True)
+        sent = sent.reshape((-1,) + sent.shape[3:])
+        received = lax.all_to_all(sent, AXES, split_axis=0, concat_axis=0, tiled=True)
+        received = received.reshape((grid_size * tm_size, pw_size) + received.shape[1:])
+        result = transform(received, tables, result, part, rows)
+    return result
+
+
 def solution(mesh):
     placed = (
         P("grid", None, None),
@@ -136,8 +510,11 @@
         P(),
         P(),
     )
+    rows = SLAB // (mesh.shape["grid"] * mesh.shape["pw"])
+    lanes = NX * NY // (mesh.shape["grid"] * mesh.shape["tm"])
+    fits = rows % (GROUP * PARTS) == 0 and lanes % 128 == 0
     return jax.shard_map(
-        shards,
+        shards if fits else general_shards,
         mesh=mesh,
         in_specs=placed,
         out_specs=P("tm", ("grid", "pw"), None, None, None),

time: 699 us -> 182 us (0.26); the launches traced: 689 us -> 181 us
  waiting for transfers between devices: 291 us -> 58.8 us
  local copies, waits for them, and re-layouts: 209 us -> 2.36 us
  matrix products: 103 us -> 0 us
  Pallas kernels: 0 us -> 95.7 us
  other arithmetic: 61.5 us -> 5.1 us
  between operations: 16 us -> 0.36 us
  starting transfers between devices: 8.34 us -> 19.2 us
    psum x1 -> x0, waiting for transfers between devices: 135 us -> none  [shards(): lax.psum(frequency_weights[:, None, None, None, None] * plane_waves[0][No...]
    dot_general x4 -> x0, matrix products: 103 us -> none  [the longest x1 42.5 us: shards(): jnp.einsum('jis,jic->sc', unoccupied_part, jnp.take(unoccupied_blocks, or...]
    all_to_all x1 -> x2, waiting for transfers between devices: 155 us -> 52.5 us  [shards(): lax.all_to_all(sent, AXES, split_axis=0, concat_axis=0, tiled=True)]
    pallas_call x0 -> x13, Pallas kernels: none -> 95.7 us  [the longest x6 78.2 us: absorb(): pl.pallas_call(kernel, grid_spec=pltpu.PrefetchScalarGridSpec(num_scalar_...]
    reshape x3 -> x0, local copies, waits for them, and re-layouts: 87.9 us -> none  [the longest x1 74.4 us: shards(): unoccupied_columns.reshape(block_count, unoccupied_block, width)]
    gather x9 -> x0, local copies, waits for them, and re-layouts: 86.2 us -> none  [the longest x5 76.1 us: shards(): jnp.take(unoccupied_blocks, orbital_block, axis=0)]
    add x1 -> x0, other arithmetic: 34.5 us -> none  [combine_parts(): real_part = cosine[..., :width_x] + sine[..., width_x:]]
    mul x4 -> x0, other arithmetic: 25.4 us -> none  [the longest x2 24.1 us: shards(): frequency_weights[:, None, None, None, None] * plane_waves[0][None]]
  transfers between devices with their start and end apart: 3 -> 17, of which waited for: 2 -> 8; matrix products, arithmetic and copies ran while one was open for 26% -> 3% of each run, Pallas kernels for 0% -> 43%
where the time goes in v2:
time: 182 us; the launch traced here: 181 us
  Pallas kernels  95.7 us (53%)
  waiting for transfers between devices  58.8 us (32%)
  starting transfers between devices  19.2 us (11%)
  other arithmetic  5.1 us (3%)
  local copies, waits for them, and re-layouts  2.36 us (1%)
    pallas_call x6, Pallas kernels, absorb(): pl.pallas_call(kernel, grid_spec=pltpu.PrefetchScalarGridSpec(num_scalar_...  78.2 us
    all_to_all x2, waiting for transfers between devices, shards(): lax.all_to_all(sent, AXES, split_axis=0, concat_axis=0, tiled=True)  52.5 us
    pallas_call x2, Pallas kernels, transform(): pl.pallas_call(kernel, grid=(pw_size, pairs), in_specs=in_specs, out_spec...  17.5 us
    all_to_all x2, starting transfers between devices, shards(): lax.all_to_all(sent, AXES, split_axis=0, concat_axis=0, tiled=True)  7.63 us
    ppermute x3, starting transfers between devices, gather_and_absorb(): lax.ppermute(down, 'grid', back)  3.95 us
  transfers between devices with their start and end apart: 17, of which 8 were waited for; matrix products, arithmetic and copies ran while one was open for 3% of the time, Pallas kernels for 43%

profile of v2, /device:TPU:0, one launch (start us, length us, event | category | flops | bytes accessed | tf_op | source)
XLA Modules:
  0.0 181.5 jit_solution(2631089721524978949)
XLA Ops:
  0.0 1.5 copy.32
  1.7 3.0 %collective-permute-start.2 = (bf16[256,896]{1,0:T(8,128)(2,1)S(1)}, bf16[256,896]{1,0:T(8,128)(2,1)S(1)}, u32[]{:S(2)}, u32[]{:S(2)}) collective-permute-start(bf16[256,896]{1,0:T(8,128)(2,1)S(1)} %bitcast.14), channel_id=1, source_target_pairs={{8,0},{16,8},{24,16},{28,24},{20,28},{12,20},{4,12},{0,4},{9,1},{1... | collective-permute-start | bytes 1376264 | tf_op jit(solution)/shard_map/ppermute | solution.py:423
  4.8 0.7 neg.12
  5.5 0.9 fusion
  6.4 0.9 select_reduce_fusion.2
  7.5 0.8 select_reduce_fusion.1
  8.3 0.7 neg.11
  9.0 0.8 select_reduce_fusion.place_ref
  9.8 0.6 fusion.1
  10.5 5.5 %absorb.6 = (f32[2,8,512,256]{3,2,1,0:T(8,128)S(1)}, f32[8,128]{1,0:T(8,128)S(1)}) custom-call(s32[1]{0:T(128)} %get-tuple-element.44.place_ref, s32[1]{0:T(128)} %bitcast.core_ref, f32[2,1024]{1,0:T(2,128)S(1)} %multiply_exponential_fusion.1.occ_ref, f32[2,6144]{1,0:T(2,128)S(1)} %multiply_exponential_fusion.unocc_ref, bf16[1024,8,512]{2,1,0:T(8,128)(2,1)} %occ_col.11, ...), custom_call_target="tpu_custom_call" | custom-call | flops 1879048192 | bytes 4128768 | tf_op jit(solution)/shard_map/absorb/pallas_call | solution.py:276
  16.1 0.6 collective-permute-done.1.refs_0_
  17.2 1.5 collective-permute-start.5
  19.3 9.4 %absorb.7 = (f32[2,8,512,256]{3,2,1,0:T(8,128)S(1)}, f32[8,128]{1,0:T(8,128)S(1)}) custom-call(s32[2]{0:T(128)S(1)} %get-tuple-element.47.place_ref, s32[1]{0:T(128)} %bitcast.core_ref, f32[2,1024]{1,0:T(2,128)S(1)} %multiply_exponential_fusion.1.occ_ref, f32[2,6144]{1,0:T(2,128)S(1)} %multiply_exponential_fusion.unocc_ref, ...), custom_call_target="tpu_custom_call", output_to_operand_aliasing={{0}: (10, {})} | custom-call | flops 3758096384 | bytes 8257536 | tf_op jit(solution)/shard_map/absorb/pallas_call | solution.py:276
  28.7 1.0 collective-permute-done.5.refs_0_
  29.8 1.5 collective-permute-done.6.refs_1_
  31.3 0.5 collective-permute-start.8
  31.8 1.6 collective-permute-start.9
  33.9 9.4 %absorb.8 = (f32[2,8,512,256]{3,2,1,0:T(8,128)S(1)}, f32[8,128]{1,0:T(8,128)S(1)}) custom-call(s32[2]{0:T(128)S(1)} %get-tuple-element.46.place_ref, s32[1]{0:T(128)} %bitcast.core_ref, f32[2,1024]{1,0:T(2,128)S(1)} %multiply_exponential_fusion.1.occ_ref, f32[2,6144]{1,0:T(2,128)S(1)} %multiply_exponential_fusion.unocc_ref, ...), custom_call_target="tpu_custom_call", output_to_operand_aliasing={{0}: (10, {})} | custom-call | flops 3758096384 | bytes 8257536 | tf_op jit(solution)/shard_map/absorb/pallas_call | solution.py:276
  43.3 1.0 collective-permute-done.9.refs_0_
  44.3 1.3 collective-permute-done.10.refs_1_
  46.2 1.3 collective-permute-start.14
  47.5 1.5 collective-permute-start.13
  49.0 9.4 %absorb.9 = (f32[2,8,512,256]{3,2,1,0:T(8,128)S(1)}, f32[8,128]{1,0:T(8,128)S(1)}) custom-call(s32[2]{0:T(128)S(1)} %get-tuple-element.45.place_ref, s32[1]{0:T(128)} %bitcast.core_ref, f32[2,1024]{1,0:T(2,128)S(1)} %multiply_exponential_fusion.1.occ_ref, f32[2,6144]{1,0:T(2,128)S(1)} %multiply_exponential_fusion.unocc_ref, ...), custom_call_target="tpu_custom_call", output_to_operand_aliasing={{0}: (10, {})} | custom-call | flops 3758096384 | bytes 8257536 | tf_op jit(solution)/shard_map/absorb/pallas_call | solution.py:276
  58.5 0.8 collective-permute-done.13.refs_0_
  59.3 7.6 %absorb.11 = (f32[2,8,512,256]{3,2,1,0:T(8,128)S(1)}, bf16[8,2,2,4,4,16,128]{6,5,4,3,2,1,0:T(8,128)(2,1)}) custom-call(s32[1]{0:T(128)} %get-tuple-element.43.place_ref, s32[1]{0:T(128)} %bitcast.core_ref, f32[2,1024]{1,0:T(2,128)S(1)} %multiply_exponential_fusion.1.occ_ref, ...), custom_call_target="tpu_custom_call", output_to_operand_aliasing={{0}: (8, {})} | custom-call | flops 1879048192 | bytes 4128768 | tf_op jit(solution)/shard_map/absorb/pallas_call | solution.py:276
  66.9 3.8 %all-to-all-start.1 = ((bf16[32,4,4,16,128]{4,3,2,1,0:T(8,128)(2,1)}), bf16[32,4,4,16,128]{4,3,2,1,0:T(8,128)(2,1)S(1)}, u32[]{:S(2)}, u32[]{:S(2)}) async-start(bf16[32,4,4,16,128]{4,3,2,1,0:T(8,128)(2,1)} %bitcast.20), calls=%async_computation.1 | async-start | bytes 4194304 | tf_op jit(solution)/shard_map/all_to_all | solution.py:493
  70.7 37.0 %absorb.10 = (f32[2,8,512,256]{3,2,1,0:T(8,128)}, bf16[8,2,2,4,4,16,128]{6,5,4,3,2,1,0:T(8,128)(2,1)}) custom-call(s32[8]{0:T(128)S(1)} %select_reduce_fusion.place_ref, s32[1]{0:T(128)} %bitcast.core_ref, f32[2,1024]{1,0:T(2,128)S(1)} %multiply_exponential_fusion.1.occ_ref, f32[2,6144]{1,0:T(2,128)S(1)} %multiply_exponential_fusion.unocc_ref, ...), custom_call_target="tpu_custom_call" | custom-call | flops 15032385536 | bytes 33030144 | tf_op jit(solution)/shard_map/absorb/pallas_call | solution.py:276
  107.7 11.7 %all-to-all-done.1 = bf16[32,4,4,16,128]{4,3,2,1,0:T(8,128)(2,1)S(1)} async-done(((bf16[32,4,4,16,128]{4,3,2,1,0:T(8,128)(2,1)}), bf16[32,4,4,16,128]{4,3,2,1,0:T(8,128)(2,1)S(1)}, u32[]{:S(2)}, u32[]{:S(2)}) %all-to-all-start.1) | async-done | bytes 2097184 | tf_op jit(solution)/shard_map/all_to_all | solution.py:493
  119.4 3.8 %all-to-all-start = ((bf16[32,4,4,16,128]{4,3,2,1,0:T(8,128)(2,1)}), bf16[32,4,4,16,128]{4,3,2,1,0:T(8,128)(2,1)}, u32[]{:S(2)}, u32[]{:S(2)}) async-start(bf16[32,4,4,16,128]{4,3,2,1,0:T(8,128)(2,1)} %bitcast.19), calls=%async_computation | async-start | bytes 4194304 | tf_op jit(solution)/shard_map/all_to_all | solution.py:493
  123.3 7.9 %transform.2.rest_0_ = f32[1,32,16,64,128]{4,3,2,1,0:T(8,128)} custom-call(bf16[128,64]{1,0:T(8,128)(2,1)S(1)} %copy-done.18, bf16[256,256]{1,0:T(8,128)(2,1)S(1)} %copy-done.17, bf16[256,256]{1,0:T(8,128)(2,1)S(1)} %copy-done.16, bf16[16,2,4,4,16,128]{5,4,3,2,1,0:T(8,128)(2,1)S(1)} %bitcast.13), custom_call_target="tpu_custom_call" | custom-call | flops 1879048192 | bytes 10485760 | tf_op jit(solution)/shard_map/transform/pallas_call | solution.py:343
  131.2 40.8 %all-to-all-done = bf16[32,4,4,16,128]{4,3,2,1,0:T(8,128)(2,1)} async-done(((bf16[32,4,4,16,128]{4,3,2,1,0:T(8,128)(2,1)}), bf16[32,4,4,16,128]{4,3,2,1,0:T(8,128)(2,1)}, u32[]{:S(2)}, u32[]{:S(2)}) %all-to-all-start) | async-done | bytes 2097184 | tf_op jit(solution)/shard_map/all_to_all | solution.py:493
  171.9 9.5 %transform.3 = f32[1,32,16,64,128]{4,3,2,1,0:T(8,128)} custom-call(bf16[128,64]{1,0:T(8,128)(2,1)S(1)} %copy-done.18, bf16[256,256]{1,0:T(8,128)(2,1)S(1)} %copy-done.17, bf16[256,256]{1,0:T(8,128)(2,1)S(1)} %copy-done.16, bf16[16,2,4,4,16,128]{5,4,3,2,1,0:T(8,128)(2,1)} %bitcast.7.in_ref, ...), custom_call_target="tpu_custom_call", output_to_operand_aliasing={{}: (4, {})} | custom-call | flops 1879048192 | bytes 10485760 | tf_op jit(solution)/shard_map/transform/pallas_call | solution.py:343
  (68 shorter events, 2.7 us)
Async XLA Ops:
  1.6 14.4 %copy-start.2 = (bf16[2,8,16,896]{3,2,1,0:T(8,128)(2,1)}, bf16[2,8,16,896]{3,2,1,0:T(8,128)(2,1)S(1)}, u32[]{:S(2)}) copy-start(bf16[2,8,16,896]{3,2,1,0:T(8,128)(2,1)S(1)} %copy.33) | copy-start | bytes 1376260
  1.7 14.4 %collective-permute-start.2 = (bf16[256,896]{1,0:T(8,128)(2,1)S(1)}, bf16[256,896]{1,0:T(8,128)(2,1)S(1)}, u32[]{:S(2)}, u32[]{:S(2)}) collective-permute-start(bf16[256,896]{1,0:T(8,128)(2,1)S(1)} %bitcast.14), channel_id=1, source_target_pairs={{8,0},{16,8},{24,16},{28,24},{20,28},{12,20},{4,12},{0,4},{9,1},{1... | collective-permute-start | bytes 1376264 | tf_op jit(solution)/shard_map/ppermute | solution.py:423
  4.7 12.0 %collective-permute-start.1 = (bf16[256,896]{1,0:T(8,128)(2,1)S(1)}, bf16[256,896]{1,0:T(8,128)(2,1)S(1)}, u32[]{:S(2)}, u32[]{:S(2)}) collective-permute-start(bf16[256,896]{1,0:T(8,128)(2,1)S(1)} %bitcast.15), channel_id=1, source_target_pairs={{0,8},{8,16},{16,24},{24,28},{28,20},{20,12},{12,4},{4,0},{1,9},{9... | collective-permute-start | bytes 1376264 | tf_op jit(solution)/shard_map/ppermute | solution.py:423
  4.8 5.7 %collective-permute-start = (bf16[256,896]{1,0:T(8,128)(2,1)S(1)}, bf16[256,896]{1,0:T(8,128)(2,1)S(1)}, u32[]{:S(2)}, u32[]{:S(2)}) collective-permute-start(bf16[256,896]{1,0:T(8,128)(2,1)S(1)} %bitcast.16), channel_id=1, source_target_pairs={{0,2},{2,0},{1,3},{3,1},{4,6},{6,4},{5,7},{7,5},{8,10},{10,8},{9,1... | collective-permute-start | bytes 1376264 | tf_op jit(solution)/shard_map/ppermute | solution.py:409
  16.7 12.1 %copy-start.3 = (bf16[256,896]{1,0:T(8,128)(2,1)}, bf16[256,896]{1,0:T(8,128)(2,1)S(1)}, u32[]{:S(2)}) copy-start(bf16[256,896]{1,0:T(8,128)(2,1)S(1)} %get-tuple-element.25.rest_2_.rest_4_) | copy-start | bytes 1376260
  16.7 12.1 %copy-start.4 = (bf16[256,896]{1,0:T(8,128)(2,1)}, bf16[256,896]{1,0:T(8,128)(2,1)S(1)}, u32[]{:S(2)}) copy-start(bf16[256,896]{1,0:T(8,128)(2,1)S(1)} %get-tuple-element.24.rest_0_.rest_2_) | copy-start | bytes 1376260
  16.7 2.6 %collective-permute-start.3 = (bf16[256,896]{1,0:T(8,128)(2,1)S(1)}, bf16[256,896]{1,0:T(8,128)(2,1)S(1)}, u32[]{:S(2)}, u32[]{:S(2)}) collective-permute-start(bf16[256,896]{1,0:T(8,128)(2,1)S(1)} %get-tuple-element.24.rest_0_.rest_2_), channel_id=1, source_target_pairs={{0,2},{2,0},{1,3},{3,1},{4,6},{6,4},{5,7},{7,5},{8,10},{10,8},{9,1... | collective-permute-start | bytes 1376264 | tf_op jit(solution)/shard_map/ppermute | solution.py:409
  16.7 2.6 %collective-permute-start.4 = (bf16[256,896]{1,0:T(8,128)(2,1)S(1)}, bf16[256,896]{1,0:T(8,128)(2,1)S(1)}, u32[]{:S(2)}, u32[]{:S(2)}) collective-permute-start(bf16[256,896]{1,0:T(8,128)(2,1)S(1)} %get-tuple-element.25.rest_2_.rest_4_), channel_id=1, source_target_pairs={{0,2},{2,0},{1,3},{3,1},{4,6},{6,4},{5,7},{7,5},{8,10},{10,8},{9,1... | collective-permute-start | bytes 1376264 | tf_op jit(solution)/shard_map/ppermute | solution.py:409
  17.2 12.6 %collective-permute-start.5 = (bf16[256,896]{1,0:T(8,128)(2,1)S(1)}, bf16[256,896]{1,0:T(8,128)(2,1)S(1)}, u32[]{:S(2)}, u32[]{:S(2)}) collective-permute-start(bf16[256,896]{1,0:T(8,128)(2,1)S(1)} %get-tuple-element.24.rest_0_.rest_2_), channel_id=1, source_target_pairs={{0,8},{8,16},{16,24},{24,28},{28,20},{20,12},{12,4},{4,0},{1,9},{9... | collective-permute-start | bytes 1376264 | tf_op jit(solution)/shard_map/ppermute | solution.py:423
  18.7 12.6 %collective-permute-start.6 = (bf16[256,896]{1,0:T(8,128)(2,1)S(1)}, bf16[256,896]{1,0:T(8,128)(2,1)S(1)}, u32[]{:S(2)}, u32[]{:S(2)}) collective-permute-start(bf16[256,896]{1,0:T(8,128)(2,1)S(1)} %get-tuple-element.25.rest_2_.rest_4_), channel_id=1, source_target_pairs={{8,0},{16,8},{24,16},{28,24},{20,28},{12,20},{4,12},{0,4},{9,1},{1... | collective-permute-start | bytes 1376264 | tf_op jit(solution)/shard_map/ppermute | solution.py:423
  19.3 9.5 %copy-start.11 = (bf16[256,896]{1,0:T(8,128)(2,1)}, bf16[256,896]{1,0:T(8,128)(2,1)S(1)}, u32[]{:S(2)}) copy-start(bf16[256,896]{1,0:T(8,128)(2,1)S(1)} %collective-permute-done.4.rest_3_.rest_5_) | copy-start | bytes 1376260
  31.3 12.0 %copy-start.5 = (bf16[256,896]{1,0:T(8,128)(2,1)}, bf16[256,896]{1,0:T(8,128)(2,1)S(1)}, u32[]{:S(2)}) copy-start(bf16[256,896]{1,0:T(8,128)(2,1)S(1)} %get-tuple-element.28.rest_0_.rest_6_) | copy-start | bytes 1376260
  31.3 12.0 %copy-start.7 = (bf16[256,896]{1,0:T(8,128)(2,1)}, bf16[256,896]{1,0:T(8,128)(2,1)S(1)}, u32[]{:S(2)}) copy-start(bf16[256,896]{1,0:T(8,128)(2,1)S(1)} %get-tuple-element.29.rest_2_.rest_8_) | copy-start | bytes 1376260
  31.3 2.5 %collective-permute-start.7 = (bf16[256,896]{1,0:T(8,128)(2,1)S(1)}, bf16[256,896]{1,0:T(8,128)(2,1)S(1)}, u32[]{:S(2)}, u32[]{:S(2)}) collective-permute-start(bf16[256,896]{1,0:T(8,128)(2,1)S(1)} %get-tuple-element.28.rest_0_.rest_6_), channel_id=1, source_target_pairs={{0,2},{2,0},{1,3},{3,1},{4,6},{6,4},{5,7},{7,5},{8,10},{10,8},{9,1... | collective-permute-start | bytes 1376264 | tf_op jit(solution)/shard_map/ppermute | solution.py:409
  31.3 2.5 %collective-permute-start.8 = (bf16[256,896]{1,0:T(8,128)(2,1)S(1)}, bf16[256,896]{1,0:T(8,128)(2,1)S(1)}, u32[]{:S(2)}, u32[]{:S(2)}) collective-permute-start(bf16[256,896]{1,0:T(8,128)(2,1)S(1)} %get-tuple-element.29.rest_2_.rest_8_), channel_id=1, source_target_pairs={{0,2},{2,0},{1,3},{3,1},{4,6},{6,4},{5,7},{7,5},{8,10},{10,8},{9,1... | collective-permute-start | bytes 1376264 | tf_op jit(solution)/shard_map/ppermute | solution.py:409
  31.8 12.5 %collective-permute-start.9 = (bf16[256,896]{1,0:T(8,128)(2,1)S(1)}, bf16[256,896]{1,0:T(8,128)(2,1)S(1)}, u32[]{:S(2)}, u32[]{:S(2)}) collective-permute-start(bf16[256,896]{1,0:T(8,128)(2,1)S(1)} %get-tuple-element.28.rest_0_.rest_6_), channel_id=1, source_target_pairs={{0,8},{8,16},{16,24},{24,28},{28,20},{20,12},{12,4},{4,0},{1,9},{9... | collective-permute-start | bytes 1376264 | tf_op jit(solution)/shard_map/ppermute | solution.py:423
  33.4 12.2 %collective-permute-start.10 = (bf16[256,896]{1,0:T(8,128)(2,1)S(1)}, bf16[256,896]{1,0:T(8,128)(2,1)S(1)}, u32[]{:S(2)}, u32[]{:S(2)}) collective-permute-start(bf16[256,896]{1,0:T(8,128)(2,1)S(1)} %get-tuple-element.29.rest_2_.rest_8_), channel_id=1, source_target_pairs={{8,0},{16,8},{24,16},{28,24},{20,28},{12,20},{4,12},{0,4},{9,1},{1... | collective-permute-start | bytes 1376264 | tf_op jit(solution)/shard_map/ppermute | solution.py:423
  33.8 9.5 %copy-start.12 = (bf16[256,896]{1,0:T(8,128)(2,1)}, bf16[256,896]{1,0:T(8,128)(2,1)S(1)}, u32[]{:S(2)}) copy-start(bf16[256,896]{1,0:T(8,128)(2,1)S(1)} %collective-permute-done.7.rest_1_.rest_7_) | copy-start | bytes 1376260
  33.9 9.5 %copy-start.13 = (bf16[256,896]{1,0:T(8,128)(2,1)}, bf16[256,896]{1,0:T(8,128)(2,1)S(1)}, u32[]{:S(2)}) copy-start(bf16[256,896]{1,0:T(8,128)(2,1)S(1)} %collective-permute-done.8.rest_3_.rest_9_) | copy-start | bytes 1376260
  45.6 12.8 %copy-start = (bf16[256,896]{1,0:T(8,128)(2,1)}, bf16[256,896]{1,0:T(8,128)(2,1)S(1)}, u32[]{:S(2)}) copy-start(bf16[256,896]{1,0:T(8,128)(2,1)S(1)} %get-tuple-element.32.first_ref.rest_0_.rest_10_) | copy-start | bytes 1376260
  45.6 12.8 %copy-start.1 = (bf16[256,896]{1,0:T(8,128)(2,1)}, bf16[256,896]{1,0:T(8,128)(2,1)S(1)}, u32[]{:S(2)}) copy-start(bf16[256,896]{1,0:T(8,128)(2,1)S(1)} %get-tuple-element.33.second_ref.rest_2_.rest_12_) | copy-start | bytes 1376260
  45.6 3.4 %collective-permute-start.11 = (bf16[256,896]{1,0:T(8,128)(2,1)S(1)}, bf16[256,896]{1,0:T(8,128)(2,1)S(1)}, u32[]{:S(2)}, u32[]{:S(2)}) collective-permute-start(bf16[256,896]{1,0:T(8,128)(2,1)S(1)} %get-tuple-element.32.first_ref.rest_0_.rest_10_), channel_id=1, source_target_pairs={{0,2},{2,0},{1,3},{3,1},{4,6},{6,4},{5,7},{7,5},{8,10},{10,8},{9,1... | collective-permute-start | bytes 1376264 | tf_op jit(solution)/shard_map/ppermute | solution.py:409
  45.6 3.4 %collective-permute-start.12 = (bf16[256,896]{1,0:T(8,128)(2,1)S(1)}, bf16[256,896]{1,0:T(8,128)(2,1)S(1)}, u32[]{:S(2)}, u32[]{:S(2)}) collective-permute-start(bf16[256,896]{1,0:T(8,128)(2,1)S(1)} %get-tuple-element.33.second_ref.rest_2_.rest_12_), channel_id=1, source_target_pairs={{0,2},{2,0},{1,3},{3,1},{4,6},{6,4},{5,7},{7,5},{8,10},{10,8},{9,1... | collective-permute-start | bytes 1376264 | tf_op jit(solution)/shard_map/ppermute | solution.py:409
  46.2 12.3 %collective-permute-start.14 = (bf16[256,896]{1,0:T(8,128)(2,1)S(1)}, bf16[256,896]{1,0:T(8,128)(2,1)S(1)}, u32[]{:S(2)}, u32[]{:S(2)}) collective-permute-start(bf16[256,896]{1,0:T(8,128)(2,1)S(1)} %choose.1), channel_id=1, source_target_pairs={{0,10},{8,18},{16,26},{24,30},{28,22},{20,14},{12,6},{4,2},{10,0},... | collective-permute-start | bytes 1376264 | tf_op jit(solution)/shard_map/ppermute | solution.py:432
  47.5 11.8 %collective-permute-start.13 = (bf16[256,896]{1,0:T(8,128)(2,1)S(1)}, bf16[256,896]{1,0:T(8,128)(2,1)S(1)}, u32[]{:S(2)}, u32[]{:S(2)}) collective-permute-start(bf16[256,896]{1,0:T(8,128)(2,1)S(1)} %choose.1), channel_id=1, source_target_pairs={{0,8},{8,16},{16,24},{24,28},{28,20},{20,12},{12,4},{4,0},{10,2},{... | collective-permute-start | bytes 1376264 | tf_op jit(solution)/shard_map/ppermute | solution.py:432
  49.0 9.5 %copy-start.14 = (bf16[256,896]{1,0:T(8,128)(2,1)}, bf16[256,896]{1,0:T(8,128)(2,1)S(1)}, u32[]{:S(2)}) copy-start(bf16[256,896]{1,0:T(8,128)(2,1)S(1)} %collective-permute-done.11.rest_1_.rest_11_) | copy-start | bytes 1376260
  49.0 9.5 %copy-start.15 = (bf16[256,896]{1,0:T(8,128)(2,1)}, bf16[256,896]{1,0:T(8,128)(2,1)S(1)}, u32[]{:S(2)}) copy-start(bf16[256,896]{1,0:T(8,128)(2,1)S(1)} %collective-permute-done.12.rest_3_.rest_13_) | copy-start | bytes 1376260
  66.9 52.6 %all-to-all-start.1 = ((bf16[32,4,4,16,128]{4,3,2,1,0:T(8,128)(2,1)}), bf16[32,4,4,16,128]{4,3,2,1,0:T(8,128)(2,1)S(1)}, u32[]{:S(2)}, u32[]{:S(2)}) async-start(bf16[32,4,4,16,128]{4,3,2,1,0:T(8,128)(2,1)} %bitcast.20), calls=%async_computation.1 | async-start | bytes 4194304 | tf_op jit(solution)/shard_map/all_to_all | solution.py:493
  70.7 52.5 %copy-start.16 = (bf16[256,256]{1,0:T(8,128)(2,1)S(1)}, bf16[256,256]{1,0:T(8,128)(2,1)}, u32[]{:S(2)}) copy-start(bf16[256,256]{1,0:T(8,128)(2,1)} %constant.31.clone.low_ref) | copy-start | bytes 393220
  70.7 52.5 %copy-start.17 = (bf16[256,256]{1,0:T(8,128)(2,1)S(1)}, bf16[256,256]{1,0:T(8,128)(2,1)}, u32[]{:S(2)}) copy-start(bf16[256,256]{1,0:T(8,128)(2,1)} %constant.30.clone.high_ref) | copy-start | bytes 393220
  70.7 52.5 %copy-start.18 = (bf16[128,64]{1,0:T(8,128)(2,1)S(1)}, bf16[128,64]{1,0:T(8,128)(2,1)}, u32[]{:S(2)}) copy-start(bf16[128,64]{1,0:T(8,128)(2,1)} %constant.29.clone.line_ref) | copy-start | bytes 49156
  119.4 52.5 %all-to-all-start = ((bf16[32,4,4,16,128]{4,3,2,1,0:T(8,128)(2,1)}), bf16[32,4,4,16,128]{4,3,2,1,0:T(8,128)(2,1)}, u32[]{:S(2)}, u32[]{:S(2)}) async-start(bf16[32,4,4,16,128]{4,3,2,1,0:T(8,128)(2,1)} %bitcast.19), calls=%async_computation | async-start | bytes 4194304 | tf_op jit(solution)/shard_map/all_to_all | solution.py:493
  (4 other events, 30.1 us)

commit v3 on v2

--- a/solution.py
+++ b/solution.py
@@ -127,6 +127,7 @@
 
 
 PARTS = 2
+EXCHANGES = ((0, 0, 4), (1, 0, 4))
 TURN = 64
 GROUP = 16
 ABSORB_LIMIT = 32 * 2**20
@@ -166,10 +167,11 @@
     return pltpu.with_memory_space_constraint(array, pltpu.HBM)
 
 
-def take_planes(block_ref, out_ref, first):
+def take_planes(block_ref, out_ref, row, first):
+    planes = out_ref.shape[0]
     for start in range(0, block_ref.shape[0], TURN):
-        at = slice(start, start + TURN)
-        out_ref[:, first + start : first + start + TURN] = jnp.swapaxes(block_ref[at], 0, 1)
+        turned = jnp.swapaxes(block_ref[start : start + TURN], 0, 1)
+        out_ref[:, row + start : row + start + TURN] = turned[first : first + planes]
 
 
 def mix_response(weight_ref, acc_ref, out_ref):
@@ -192,15 +194,16 @@
                 out_ref[:, f, :, pair, y] = both.reshape(grid_size, pw_size, rows, 2 * NX)
 
 
-def absorb(pieces, part, places, core, decays, columns, acc, finish, last):
+def absorb(pieces, exchange, places, core, decays, columns, acc, finish, last):
     occupied_decay, unoccupied_decay = decays
     occupied_columns, unoccupied_columns = columns
     times, occupied_count = occupied_decay.shape
     unoccupied_count = unoccupied_decay.shape[1]
-    planes, lanes = occupied_columns.shape[1], occupied_columns.shape[2] // 2
+    part, first_pair, pairs = exchange
+    planes, planes_local, lanes = 2 * pairs, occupied_columns.shape[1], occupied_columns.shape[2] // 2
     flat = [entry for block in pieces for entry in block]
-    half, width = flat[0][0].shape
-    half //= PARTS
+    width = flat[0][0].shape[1]
+    half = SLAB // 2 // PARTS
     points = 2 * half
     occupied_block = occupied_count * width // (occupied_count + unoccupied_count)
     unoccupied_block = width - occupied_block
@@ -211,8 +214,8 @@
         if not first_call:
             rest = rest[1:]
         weight_ref, acc_ref, last_ref, weighed, taken = rest
-        take_planes(occ_col, taken, 0)
-        take_planes(unocc_col, taken, occupied_block)
+        take_planes(occ_col, taken, 0, 2 * first_pair)
+        take_planes(unocc_col, taken, occupied_block, 2 * first_pair)
         for n, block in enumerate(pieces):
             mine, refs = refs[: len(block)], refs[len(block) :]
 
@@ -249,12 +252,12 @@
     total = (2, planes, times * points, lanes)
     kept = pl.BlockSpec(memory_space=pltpu.VMEM)
     operands = [places, core, occupied_decay, unoccupied_decay, hbm(occupied_columns), hbm(unoccupied_columns)]
-    operands += [entry[0] if part == 0 else hbm(entry[0]) for entry in flat]
+    operands += [hbm(entry[0]) if first_call and last else entry[0] for entry in flat]
     in_specs = [
         pl.BlockSpec((times, occupied_block), lambda n, place, core: (0, place[n])),
         pl.BlockSpec((times, unoccupied_block), lambda n, place, core: (0, place[n])),
-        pl.BlockSpec((occupied_block, planes, lanes), lambda n, place, core: (place[n], 0, core[0])),
-        pl.BlockSpec((unoccupied_block, planes, lanes), lambda n, place, core: (place[n], 0, core[0])),
+        pl.BlockSpec((occupied_block, planes_local, lanes), lambda n, place, core: (place[n], 0, core[0])),
+        pl.BlockSpec((unoccupied_block, planes_local, lanes), lambda n, place, core: (place[n], 0, core[0])),
     ] + [pl.BlockSpec((half, width), lambda n, place, core: (part, 0)) for entry in flat]
     out_specs, out_shape, aliases = [kept], [pltpu.VMEM(total, jnp.float32)], {}
     if not first_call:
@@ -289,33 +292,33 @@
         input_output_aliases=aliases,
         compiler_params=pltpu.CompilerParams(vmem_limit_bytes=ABSORB_LIMIT),
         cost_estimate=expected(
-            blocks * 2 * times * points * width * planes * lanes, blocks * 2 * width * (points + planes * lanes)
+            blocks * 2 * times * points * width * planes * lanes, blocks * 2 * width * (points + planes_local * lanes)
         ),
         name="absorb",
     )(*operands)
 
 
-def transform(received, tables, previous, part, total_rows):
+def transform(received, tables, previous, exchange, total_rows, total_pairs):
     sources, pw_size, pairs, lines, rows, width = received.shape
     number = sources * lines
     line_table, high_table, low_table = tables
-    total_planes = 2 * pw_size * pairs
+    part, first_pair, _ = exchange
+    step = 2 if first_pair % 2 == 0 and pairs % 2 == 0 and total_pairs % 2 == 0 else 1
     together = 2
-    batch = 8
 
     def kernel(line_ref, high_ref, low_ref, in_ref, *rest):
         out_ref, sides_ref = rest[-2:]
-        images = jnp.swapaxes(in_ref[...].reshape(number, rows, width), 0, 1)
-        for first in range(0, rows, together):
-            group = range(first, first + together)
-            side_by_side = jnp.concatenate([images[r] for r in group], axis=1)
-            lined = jnp.dot(line_ref[...], side_by_side, preferred_element_type=jnp.float32)
-            for r in group:
-                at, lanes = slice(r * number, (r + 1) * number), slice((r - first) * width, (r - first + 1) * width)
-                sides_ref[at, :width] = lined[:number, lanes]
-                sides_ref[at, width:] = lined[number:, lanes]
-        for first in range(0, rows, batch):
-            sides = sides_ref[first * number : (first + batch) * number]
+        for pair in range(step):
+            images = jnp.swapaxes(in_ref[:, 0, pair].reshape(number, rows, width), 0, 1)
+            for first in range(0, rows, together):
+                group = range(first, first + together)
+                side_by_side = jnp.concatenate([images[r] for r in group], axis=1)
+                lined = jnp.dot(line_ref[...], side_by_side, preferred_element_type=jnp.float32)
+                for r in group:
+                    at, lanes = slice(r * number, (r + 1) * number), slice((r - first) * width, (r - first + 1) * width)
+                    sides_ref[at, :width] = lined[:number, lanes]
+                    sides_ref[at, width:] = lined[number:, lanes]
+            sides = sides_ref[...]
             high = sides.astype(jnp.bfloat16)
             low = (sides - high.astype(jnp.float32)).astype(jnp.bfloat16)
             waves = jnp.dot(high, high_ref[...], preferred_element_type=jnp.float32)
@@ -323,16 +326,16 @@
             waves += jnp.dot(high, low_ref[...], preferred_element_type=jnp.float32)
             for plane in range(2):
                 lanes = slice(plane * width, (plane + 1) * width)
-                out_ref[0, first : first + batch, plane] = waves[:, lanes].reshape(batch, number, width)
-
-    out_shape = (1, total_rows, total_planes, number, width)
+                out_ref[0, :, 2 * pair + plane] = waves[:, lanes].reshape(rows, number, width)
+
+    out_shape = (1, total_rows, 2 * pw_size * total_pairs, number, width)
     whole = lambda p, j: (0, 0)
     operands = [line_table, high_table, low_table, received]
     in_specs = [
         pl.BlockSpec(line_table.shape, whole),
         pl.BlockSpec(high_table.shape, whole),
         pl.BlockSpec(low_table.shape, whole),
-        pl.BlockSpec((sources, 1, 1, lines, rows, width), lambda p, j: (0, p, j, 0, 0, 0)),
+        pl.BlockSpec((sources, 1, step, lines, rows, width), lambda p, j: (0, p, j, 0, 0, 0)),
     ]
     aliases = {}
     if previous is not None:
@@ -342,10 +345,10 @@
     work = pw_size * pairs * rows * number
     return pl.pallas_call(
         kernel,
-        grid=(pw_size, pairs),
+        grid=(pw_size, pairs // step),
         in_specs=in_specs,
         out_specs=pl.BlockSpec(
-            (1, rows, 2, number, width), lambda p, j: (0, part, p * pairs + j, 0, 0)
+            (1, rows, 2 * step, number, width), lambda p, j: (0, part, (p * total_pairs + first_pair) // step + j, 0, 0)
         ),
         out_shape=jax.ShapeDtypeStruct(out_shape, jnp.float32),
         scratch_shapes=[pltpu.VMEM((rows * number, 2 * width), jnp.float32)],
@@ -385,21 +388,23 @@
 
 
 def choose(core, first, second):
-    def kernel(core_ref, first_ref, second_ref, out_ref):
-        @pl.when(core_ref[0] == 0)
-        def _():
-            out_ref[...] = first_ref[...]
-
-        @pl.when(core_ref[0] != 0)
-        def _():
-            out_ref[...] = second_ref[...]
+    shape, dtype = first.shape, first.dtype
+    some = (shape[0] // PARTS, shape[1])
+
+    def kernel(core_ref, first_ref, second_ref, out_ref, some_ref):
+        for core_index, ref in enumerate((first_ref, second_ref)):
+
+            @pl.when(core_ref[0] == core_index)
+            def _():
+                out_ref[...] = ref[...]
+                some_ref[...] = ref[: some[0]]
 
     kept = pl.BlockSpec(memory_space=pltpu.VMEM)
     return pl.pallas_call(
         kernel,
         in_specs=[pl.BlockSpec(memory_space=pltpu.SMEM), kept, kept],
-        out_specs=kept,
-        out_shape=pltpu.VMEM(first.shape, first.dtype),
+        out_specs=[kept, kept],
+        out_shape=[pltpu.VMEM(shape, dtype), pltpu.VMEM(some, dtype)],
         compiler_params=pltpu.CompilerParams(vmem_limit_bytes=4 * SMALL_LIMIT),
         name="choose",
     )(core, first, second)
@@ -423,22 +428,24 @@
         up, down = lax.ppermute(up, "grid", onward), lax.ppermute(down, "grid", back)
         start = len(every)
         every += blocks
-        acc, token = absorb_blocks(blocks, 0, places[start : len(every)], acc, False)
+        acc, token = absorb_blocks(blocks, EXCHANGES[0], places[start : len(every)], acc, False)
         up, down = after([up, down], token)
         blocks = [swapped(up), swapped(down)]
-    far = choose(core, up, down)
+    far, some = choose(core, up, down)
     sides = list(enumerate((onward, back)))
-    far = [
-        lax.ppermute(far, ("grid", "tm"), [(2 * source + side, 2 * to + (side ^ flip)) for side, pairs in sides for source, to in pairs])
-        for flip in (0, 1)
+    own, other = [
+        lax.ppermute(
+            rows, ("grid", "tm"), [(2 * source + side, 2 * to + (side ^ flip)) for side, pairs in sides for source, to in pairs]
+        )
+        for rows, flip in ((far, 0), (some, 1))
     ]
     start = len(every)
     every += blocks
-    acc, token = absorb_blocks(blocks, 0, places[start : len(every)], acc, False)
-    own, other = after(far, token)
+    acc, token = absorb_blocks(blocks, EXCHANGES[0], places[start : len(every)], acc, False)
+    own, other = after([own, other], token)
     blocks = [[(own, 0), (other, 1)]]
-    _, sent = absorb_blocks(blocks, 0, places[number - 1 :], acc, True)
-    return sent, every + blocks
+    _, sent = absorb_blocks(blocks, EXCHANGES[0], places[number - 1 :], acc, True)
+    return sent, every + blocks, every + [swapped(own)]
 
 
 def shards(
@@ -478,21 +485,21 @@
     columns = (occupied_columns, unoccupied_columns)
     finish = (-frequency_weights, (grid_size, pw_size))
 
-    def absorb_blocks(pieces, part, here, acc, last):
-        return absorb(pieces, part, here, core, (occupied_decay, unoccupied_decay), columns, acc, finish, last)
+    def absorb_blocks(pieces, exchange, here, acc, last):
+        return absorb(pieces, exchange, here, core, (occupied_decay, unoccupied_decay), columns, acc, finish, last)
 
     tables = (jnp.asarray(line_operator(NY)),) + tuple(jnp.asarray(t) for t in row_operator(NX))
     mine = jnp.swapaxes(by_owner, 0, 1).reshape(SLAB // tm_size, -1)
     result = None
-    for part in range(PARTS):
-        if part == 0:
-            sent, blocks = gather_and_absorb(mine, core, places, (onward, back), absorb_blocks)
+    for exchange in EXCHANGES:
+        if exchange == EXCHANGES[0]:
+            sent, *blocks = gather_and_absorb(mine, core, places, (onward, back), absorb_blocks)
         else:
-            _, sent = absorb_blocks(blocks, part, places, None, True)
+            _, sent = absorb_blocks(blocks[exchange[0]], exchange, places, None, True)
         sent = sent.reshape((-1,) + sent.shape[3:])
         received = lax.all_to_all(sent, AXES, split_axis=0, concat_axis=0, tiled=True)
         received = received.reshape((grid_size * tm_size, pw_size) + received.shape[1:])
-        result = transform(received, tables, result, part, rows)
+        result = transform(received, tables, result, exchange, rows, occupied_columns.shape[1] // 2)
     return result
 
 

time: 182 us -> 179 us (0.984)
  Pallas kernels: 95.7 us -> 92.7 us
    pallas_call x2, Pallas kernels: 17.5 us -> 14.5 us  [transform(): pl.pallas_call(kernel, grid=(pw_size, pairs // step), in_specs=in_specs,...]
    ppermute x7 -> x8, waiting for transfers between devices: 0.02 us -> 1.87 us  [swapped(): return [(rows, 0), (lax.ppermute(rows, 'tm', SWAP), 1)]]
  transfers between devices with their start and end apart: 17 -> 18, of which waited for: 8 -> 9; matrix products, arithmetic and copies ran while one was open for 3% -> 3% of each run, Pallas kernels for 43% -> 43%
where the time goes in v3:
time: 179 us; the launch traced here: 178 us
  Pallas kernels  92.7 us (52%)
  waiting for transfers between devices  58.1 us (32%)
  starting transfers between devices  18.6 us (10%)
  other arithmetic  5.1 us (3%)
  local copies, waits for them, and re-layouts  3.11 us (2%)
    pallas_call x6, Pallas kernels, absorb(): pl.pallas_call(kernel, grid_spec=pltpu.PrefetchScalarGridSpec(num_scalar_...  78.2 us
    all_to_all x2, waiting for transfers between devices, shards(): lax.all_to_all(sent, AXES, split_axis=0, concat_axis=0, tiled=True)  50.8 us
    pallas_call x2, Pallas kernels, transform(): pl.pallas_call(kernel, grid=(pw_size, pairs // step), in_specs=in_specs,...  14.5 us
    all_to_all x2, starting transfers between devices, shards(): lax.all_to_all(sent, AXES, split_axis=0, concat_axis=0, tiled=True)  7.96 us
    ppermute x3, starting transfers between devices, gather_and_absorb(): lax.ppermute(down, 'grid', back)  4.05 us
  transfers between devices with their start and end apart: 18, of which 9 were waited for; matrix products, arithmetic and copies ran while one was open for 3% of the time, Pallas kernels for 43%

profile of v3, /device:TPU:0, one launch (start us, length us, event | category | flops | bytes accessed | tf_op | source)
XLA Modules:
  0.0 178.0 jit_solution(2904330493701308077)
XLA Ops:
  0.0 1.5 copy.32
  1.7 3.0 %collective-permute-start.2 = (bf16[256,896]{1,0:T(8,128)(2,1)S(1)}, bf16[256,896]{1,0:T(8,128)(2,1)S(1)}, u32[]{:S(2)}, u32[]{:S(2)}) collective-permute-start(bf16[256,896]{1,0:T(8,128)(2,1)S(1)} %bitcast.14), channel_id=1, source_target_pairs={{8,0},{16,8},{24,16},{28,24},{20,28},{12,20},{4,12},{0,4},{9,1},{1... | collective-permute-start | bytes 1376264 | tf_op jit(solution)/shard_map/ppermute | solution.py:428
  4.8 0.7 neg.12
  5.5 0.9 fusion
  6.4 0.9 select_reduce_fusion.2
  7.5 0.8 select_reduce_fusion.1
  8.3 0.7 neg.11
  9.0 0.8 select_reduce_fusion.place_ref
  9.8 0.6 fusion.1
  10.5 5.4 %absorb.6 = (f32[2,8,512,256]{3,2,1,0:T(8,128)S(1)}, f32[8,128]{1,0:T(8,128)S(1)}) custom-call(s32[1]{0:T(128)} %get-tuple-element.48.place_ref, s32[1]{0:T(128)} %bitcast.core_ref, f32[2,1024]{1,0:T(2,128)S(1)} %multiply_exponential_fusion.1.occ_ref, f32[2,6144]{1,0:T(2,128)S(1)} %multiply_exponential_fusion.unocc_ref, bf16[1024,8,512]{2,1,0:T(8,128)(2,1)} %occ_col.11, ...), custom_call_target="tpu_custom_call" | custom-call | flops 1879048192 | bytes 4128768 | tf_op jit(solution)/shard_map/absorb/pallas_call | solution.py:279
  15.9 0.7 collective-permute-done.1.refs_0_
  17.2 1.4 collective-permute-start.5
  18.6 0.6 collective-permute-start.6
  19.3 9.4 %absorb.7 = (f32[2,8,512,256]{3,2,1,0:T(8,128)S(1)}, f32[8,128]{1,0:T(8,128)S(1)}) custom-call(s32[2]{0:T(128)S(1)} %get-tuple-element.51.place_ref, s32[1]{0:T(128)} %bitcast.core_ref, f32[2,1024]{1,0:T(2,128)S(1)} %multiply_exponential_fusion.1.occ_ref, f32[2,6144]{1,0:T(2,128)S(1)} %multiply_exponential_fusion.unocc_ref, ...), custom_call_target="tpu_custom_call", output_to_operand_aliasing={{0}: (10, {})} | custom-call | flops 3758096384 | bytes 8257536 | tf_op jit(solution)/shard_map/absorb/pallas_call | solution.py:279
  28.7 0.9 collective-permute-done.5.refs_0_
  29.7 1.5 collective-permute-done.6.refs_1_
  31.7 1.6 collective-permute-start.9
  33.8 9.4 %absorb.8 = (f32[2,8,512,256]{3,2,1,0:T(8,128)S(1)}, f32[8,128]{1,0:T(8,128)S(1)}) custom-call(s32[2]{0:T(128)S(1)} %get-tuple-element.50.place_ref, s32[1]{0:T(128)} %bitcast.core_ref, f32[2,1024]{1,0:T(2,128)S(1)} %multiply_exponential_fusion.1.occ_ref, f32[2,6144]{1,0:T(2,128)S(1)} %multiply_exponential_fusion.unocc_ref, ...), custom_call_target="tpu_custom_call", output_to_operand_aliasing={{0}: (10, {})} | custom-call | flops 3758096384 | bytes 8257536 | tf_op jit(solution)/shard_map/absorb/pallas_call | solution.py:279
  43.2 1.0 collective-permute-done.9.refs_0_
  44.2 1.3 collective-permute-done.10.refs_1_
  46.1 1.8 %collective-permute-start.13 = (bf16[256,896]{1,0:T(8,128)(2,1)S(1)}, bf16[256,896]{1,0:T(8,128)(2,1)S(1)}, u32[]{:S(2)}, u32[]{:S(2)}) collective-permute-start(bf16[256,896]{1,0:T(8,128)(2,1)S(1)} %get-tuple-element.36), channel_id=1, source_target_pairs={{0,8},{8,16},{16,24},{24,28},{28,20},{20,12},{12,4},{4,0},{10,2},{... | collective-permute-start | bytes 1376264 | tf_op jit(solution)/shard_map/ppermute | solution.py:437
  48.0 9.4 %absorb.9 = (f32[2,8,512,256]{3,2,1,0:T(8,128)S(1)}, f32[8,128]{1,0:T(8,128)S(1)}) custom-call(s32[2]{0:T(128)S(1)} %get-tuple-element.49.place_ref, s32[1]{0:T(128)} %bitcast.core_ref, f32[2,1024]{1,0:T(2,128)S(1)} %multiply_exponential_fusion.1.occ_ref, f32[2,6144]{1,0:T(2,128)S(1)} %multiply_exponential_fusion.unocc_ref, ...), custom_call_target="tpu_custom_call", output_to_operand_aliasing={{0}: (10, {})} | custom-call | flops 3758096384 | bytes 8257536 | tf_op jit(solution)/shard_map/absorb/pallas_call | solution.py:279
  57.5 7.6 %absorb.11 = (f32[2,8,512,256]{3,2,1,0:T(8,128)S(1)}, bf16[8,2,2,4,4,16,128]{6,5,4,3,2,1,0:T(8,128)(2,1)}) custom-call(s32[1]{0:T(128)} %get-tuple-element.47.place_ref, s32[1]{0:T(128)} %bitcast.core_ref, f32[2,1024]{1,0:T(2,128)S(1)} %multiply_exponential_fusion.1.occ_ref, ...), custom_call_target="tpu_custom_call", output_to_operand_aliasing={{0}: (8, {})} | custom-call | flops 1879048192 | bytes 4128768 | tf_op jit(solution)/shard_map/absorb/pallas_call | solution.py:279
  65.1 4.1 %all-to-all-start.1 = ((bf16[32,4,4,16,128]{4,3,2,1,0:T(8,128)(2,1)}), bf16[32,4,4,16,128]{4,3,2,1,0:T(8,128)(2,1)S(1)}, u32[]{:S(2)}, u32[]{:S(2)}) async-start(bf16[32,4,4,16,128]{4,3,2,1,0:T(8,128)(2,1)} %bitcast.19), calls=%async_computation.1 | async-start | bytes 4194304 | tf_op jit(solution)/shard_map/all_to_all | solution.py:500
  69.4 1.8 collective-permute-done.15.rest_15_
  71.2 0.8 copy-done.18
  71.9 37.0 %absorb.10 = (f32[2,8,512,256]{3,2,1,0:T(8,128)}, bf16[8,2,2,4,4,16,128]{6,5,4,3,2,1,0:T(8,128)(2,1)}) custom-call(s32[8]{0:T(128)S(1)} %select_reduce_fusion.place_ref, s32[1]{0:T(128)} %bitcast.core_ref, f32[2,1024]{1,0:T(2,128)S(1)} %multiply_exponential_fusion.1.occ_ref, f32[2,6144]{1,0:T(2,128)S(1)} %multiply_exponential_fusion.unocc_ref, ...), custom_call_target="tpu_custom_call" | custom-call | flops 15032385536 | bytes 33030144 | tf_op jit(solution)/shard_map/absorb/pallas_call | solution.py:279
  108.9 8.8 %all-to-all-done.1 = bf16[32,4,4,16,128]{4,3,2,1,0:T(8,128)(2,1)S(1)} async-done(((bf16[32,4,4,16,128]{4,3,2,1,0:T(8,128)(2,1)}), bf16[32,4,4,16,128]{4,3,2,1,0:T(8,128)(2,1)S(1)}, u32[]{:S(2)}, u32[]{:S(2)}) %all-to-all-start.1) | async-done | bytes 2097184 | tf_op jit(solution)/shard_map/all_to_all | solution.py:500
  117.7 3.8 %all-to-all-start = ((bf16[32,4,4,16,128]{4,3,2,1,0:T(8,128)(2,1)}), bf16[32,4,4,16,128]{4,3,2,1,0:T(8,128)(2,1)}, u32[]{:S(2)}, u32[]{:S(2)}) async-start(bf16[32,4,4,16,128]{4,3,2,1,0:T(8,128)(2,1)} %bitcast.20), calls=%async_computation | async-start | bytes 4194304 | tf_op jit(solution)/shard_map/all_to_all | solution.py:500
  121.6 6.7 %transform.2.rest_0_ = f32[1,32,16,64,128]{4,3,2,1,0:T(8,128)} custom-call(bf16[128,64]{1,0:T(8,128)(2,1)S(1)} %copy-done.17, bf16[256,256]{1,0:T(8,128)(2,1)S(1)} %copy-done.16, bf16[256,256]{1,0:T(8,128)(2,1)S(1)} %copy-done.15, bf16[16,2,4,4,16,128]{5,4,3,2,1,0:T(8,128)(2,1)S(1)} %bitcast.13), custom_call_target="tpu_custom_call" | custom-call | flops 1879048192 | bytes 10485760 | tf_op jit(solution)/shard_map/transform/pallas_call | solution.py:346
  128.3 41.9 %all-to-all-done = bf16[32,4,4,16,128]{4,3,2,1,0:T(8,128)(2,1)} async-done(((bf16[32,4,4,16,128]{4,3,2,1,0:T(8,128)(2,1)}), bf16[32,4,4,16,128]{4,3,2,1,0:T(8,128)(2,1)}, u32[]{:S(2)}, u32[]{:S(2)}) %all-to-all-start) | async-done | bytes 2097184 | tf_op jit(solution)/shard_map/all_to_all | solution.py:500
  170.3 7.7 %transform.3 = f32[1,32,16,64,128]{4,3,2,1,0:T(8,128)} custom-call(bf16[128,64]{1,0:T(8,128)(2,1)S(1)} %copy-done.17, bf16[256,256]{1,0:T(8,128)(2,1)S(1)} %copy-done.16, bf16[256,256]{1,0:T(8,128)(2,1)S(1)} %copy-done.15, bf16[16,2,4,4,16,128]{5,4,3,2,1,0:T(8,128)(2,1)} %bitcast.7.in_ref, ...), custom_call_target="tpu_custom_call", output_to_operand_aliasing={{}: (4, {})} | custom-call | flops 1879048192 | bytes 10485760 | tf_op jit(solution)/shard_map/transform/pallas_call | solution.py:346
  (70 shorter events, 2.9 us)
Async XLA Ops:
  1.6 14.3 %copy-start.2 = (bf16[2,8,16,896]{3,2,1,0:T(8,128)(2,1)}, bf16[2,8,16,896]{3,2,1,0:T(8,128)(2,1)S(1)}, u32[]{:S(2)}) copy-start(bf16[2,8,16,896]{3,2,1,0:T(8,128)(2,1)S(1)} %copy.33) | copy-start | bytes 1376260
  1.7 14.3 %collective-permute-start.2 = (bf16[256,896]{1,0:T(8,128)(2,1)S(1)}, bf16[256,896]{1,0:T(8,128)(2,1)S(1)}, u32[]{:S(2)}, u32[]{:S(2)}) collective-permute-start(bf16[256,896]{1,0:T(8,128)(2,1)S(1)} %bitcast.14), channel_id=1, source_target_pairs={{8,0},{16,8},{24,16},{28,24},{20,28},{12,20},{4,12},{0,4},{9,1},{1... | collective-permute-start | bytes 1376264 | tf_op jit(solution)/shard_map/ppermute | solution.py:428
  4.7 12.0 %collective-permute-start.1 = (bf16[256,896]{1,0:T(8,128)(2,1)S(1)}, bf16[256,896]{1,0:T(8,128)(2,1)S(1)}, u32[]{:S(2)}, u32[]{:S(2)}) collective-permute-start(bf16[256,896]{1,0:T(8,128)(2,1)S(1)} %bitcast.15), channel_id=1, source_target_pairs={{0,8},{8,16},{16,24},{24,28},{28,20},{20,12},{12,4},{4,0},{1,9},{9... | collective-permute-start | bytes 1376264 | tf_op jit(solution)/shard_map/ppermute | solution.py:428
  4.8 5.7 %collective-permute-start = (bf16[256,896]{1,0:T(8,128)(2,1)S(1)}, bf16[256,896]{1,0:T(8,128)(2,1)S(1)}, u32[]{:S(2)}, u32[]{:S(2)}) collective-permute-start(bf16[256,896]{1,0:T(8,128)(2,1)S(1)} %bitcast.16), channel_id=1, source_target_pairs={{0,2},{2,0},{1,3},{3,1},{4,6},{6,4},{5,7},{7,5},{8,10},{10,8},{9,1... | collective-permute-start | bytes 1376264 | tf_op jit(solution)/shard_map/ppermute | solution.py:414
  16.7 12.1 %copy-start.4 = (bf16[256,896]{1,0:T(8,128)(2,1)}, bf16[256,896]{1,0:T(8,128)(2,1)S(1)}, u32[]{:S(2)}) copy-start(bf16[256,896]{1,0:T(8,128)(2,1)S(1)} %get-tuple-element.27.rest_2_.rest_4_) | copy-start | bytes 1376260
  16.7 12.1 %copy-start.5 = (bf16[256,896]{1,0:T(8,128)(2,1)}, bf16[256,896]{1,0:T(8,128)(2,1)S(1)}, u32[]{:S(2)}) copy-start(bf16[256,896]{1,0:T(8,128)(2,1)S(1)} %get-tuple-element.26.rest_0_.rest_2_) | copy-start | bytes 1376260
  16.7 2.6 %collective-permute-start.3 = (bf16[256,896]{1,0:T(8,128)(2,1)S(1)}, bf16[256,896]{1,0:T(8,128)(2,1)S(1)}, u32[]{:S(2)}, u32[]{:S(2)}) collective-permute-start(bf16[256,896]{1,0:T(8,128)(2,1)S(1)} %get-tuple-element.26.rest_0_.rest_2_), channel_id=1, source_target_pairs={{0,2},{2,0},{1,3},{3,1},{4,6},{6,4},{5,7},{7,5},{8,10},{10,8},{9,1... | collective-permute-start | bytes 1376264 | tf_op jit(solution)/shard_map/ppermute | solution.py:414
  16.7 2.6 %collective-permute-start.4 = (bf16[256,896]{1,0:T(8,128)(2,1)S(1)}, bf16[256,896]{1,0:T(8,128)(2,1)S(1)}, u32[]{:S(2)}, u32[]{:S(2)}) collective-permute-start(bf16[256,896]{1,0:T(8,128)(2,1)S(1)} %get-tuple-element.27.rest_2_.rest_4_), channel_id=1, source_target_pairs={{0,2},{2,0},{1,3},{3,1},{4,6},{6,4},{5,7},{7,5},{8,10},{10,8},{9,1... | collective-permute-start | bytes 1376264 | tf_op jit(solution)/shard_map/ppermute | solution.py:414
  17.2 12.5 %collective-permute-start.5 = (bf16[256,896]{1,0:T(8,128)(2,1)S(1)}, bf16[256,896]{1,0:T(8,128)(2,1)S(1)}, u32[]{:S(2)}, u32[]{:S(2)}) collective-permute-start(bf16[256,896]{1,0:T(8,128)(2,1)S(1)} %get-tuple-element.26.rest_0_.rest_2_), channel_id=1, source_target_pairs={{0,8},{8,16},{16,24},{24,28},{28,20},{20,12},{12,4},{4,0},{1,9},{9... | collective-permute-start | bytes 1376264 | tf_op jit(solution)/shard_map/ppermute | solution.py:428
  18.6 12.6 %collective-permute-start.6 = (bf16[256,896]{1,0:T(8,128)(2,1)S(1)}, bf16[256,896]{1,0:T(8,128)(2,1)S(1)}, u32[]{:S(2)}, u32[]{:S(2)}) collective-permute-start(bf16[256,896]{1,0:T(8,128)(2,1)S(1)} %get-tuple-element.27.rest_2_.rest_4_), channel_id=1, source_target_pairs={{8,0},{16,8},{24,16},{28,24},{20,28},{12,20},{4,12},{0,4},{9,1},{1... | collective-permute-start | bytes 1376264 | tf_op jit(solution)/shard_map/ppermute | solution.py:428
  19.3 9.5 %copy-start.10 = (bf16[256,896]{1,0:T(8,128)(2,1)}, bf16[256,896]{1,0:T(8,128)(2,1)S(1)}, u32[]{:S(2)}) copy-start(bf16[256,896]{1,0:T(8,128)(2,1)S(1)} %collective-permute-done.4.rest_3_.rest_5_) | copy-start | bytes 1376260
  31.2 12.0 %copy-start.6 = (bf16[256,896]{1,0:T(8,128)(2,1)}, bf16[256,896]{1,0:T(8,128)(2,1)S(1)}, u32[]{:S(2)}) copy-start(bf16[256,896]{1,0:T(8,128)(2,1)S(1)} %get-tuple-element.30.rest_0_.rest_6_) | copy-start | bytes 1376260
  31.2 12.0 %copy-start.7 = (bf16[256,896]{1,0:T(8,128)(2,1)}, bf16[256,896]{1,0:T(8,128)(2,1)S(1)}, u32[]{:S(2)}) copy-start(bf16[256,896]{1,0:T(8,128)(2,1)S(1)} %get-tuple-element.31.rest_2_.rest_8_) | copy-start | bytes 1376260
  31.2 2.5 %collective-permute-start.7 = (bf16[256,896]{1,0:T(8,128)(2,1)S(1)}, bf16[256,896]{1,0:T(8,128)(2,1)S(1)}, u32[]{:S(2)}, u32[]{:S(2)}) collective-permute-start(bf16[256,896]{1,0:T(8,128)(2,1)S(1)} %get-tuple-element.30.rest_0_.rest_6_), channel_id=1, source_target_pairs={{0,2},{2,0},{1,3},{3,1},{4,6},{6,4},{5,7},{7,5},{8,10},{10,8},{9,1... | collective-permute-start | bytes 1376264 | tf_op jit(solution)/shard_map/ppermute | solution.py:414
  31.2 2.5 %collective-permute-start.8 = (bf16[256,896]{1,0:T(8,128)(2,1)S(1)}, bf16[256,896]{1,0:T(8,128)(2,1)S(1)}, u32[]{:S(2)}, u32[]{:S(2)}) collective-permute-start(bf16[256,896]{1,0:T(8,128)(2,1)S(1)} %get-tuple-element.31.rest_2_.rest_8_), channel_id=1, source_target_pairs={{0,2},{2,0},{1,3},{3,1},{4,6},{6,4},{5,7},{7,5},{8,10},{10,8},{9,1... | collective-permute-start | bytes 1376264 | tf_op jit(solution)/shard_map/ppermute | solution.py:414
  31.7 12.5 %collective-permute-start.9 = (bf16[256,896]{1,0:T(8,128)(2,1)S(1)}, bf16[256,896]{1,0:T(8,128)(2,1)S(1)}, u32[]{:S(2)}, u32[]{:S(2)}) collective-permute-start(bf16[256,896]{1,0:T(8,128)(2,1)S(1)} %get-tuple-element.30.rest_0_.rest_6_), channel_id=1, source_target_pairs={{0,8},{8,16},{16,24},{24,28},{28,20},{20,12},{12,4},{4,0},{1,9},{9... | collective-permute-start | bytes 1376264 | tf_op jit(solution)/shard_map/ppermute | solution.py:428
  33.3 12.2 %collective-permute-start.10 = (bf16[256,896]{1,0:T(8,128)(2,1)S(1)}, bf16[256,896]{1,0:T(8,128)(2,1)S(1)}, u32[]{:S(2)}, u32[]{:S(2)}) collective-permute-start(bf16[256,896]{1,0:T(8,128)(2,1)S(1)} %get-tuple-element.31.rest_2_.rest_8_), channel_id=1, source_target_pairs={{8,0},{16,8},{24,16},{28,24},{20,28},{12,20},{4,12},{0,4},{9,1},{1... | collective-permute-start | bytes 1376264 | tf_op jit(solution)/shard_map/ppermute | solution.py:428
  33.7 9.5 %copy-start.12 = (bf16[256,896]{1,0:T(8,128)(2,1)}, bf16[256,896]{1,0:T(8,128)(2,1)S(1)}, u32[]{:S(2)}) copy-start(bf16[256,896]{1,0:T(8,128)(2,1)S(1)} %collective-permute-done.8.rest_3_.rest_9_) | copy-start | bytes 1376260
  45.5 11.9 %copy-start = (bf16[256,896]{1,0:T(8,128)(2,1)}, bf16[256,896]{1,0:T(8,128)(2,1)S(1)}, u32[]{:S(2)}) copy-start(bf16[256,896]{1,0:T(8,128)(2,1)S(1)} %get-tuple-element.34.first_ref.rest_0_.rest_10_) | copy-start | bytes 1376260
  45.5 11.9 %copy-start.1 = (bf16[256,896]{1,0:T(8,128)(2,1)}, bf16[256,896]{1,0:T(8,128)(2,1)S(1)}, u32[]{:S(2)}) copy-start(bf16[256,896]{1,0:T(8,128)(2,1)S(1)} %get-tuple-element.35.second_ref.rest_2_.rest_12_) | copy-start | bytes 1376260
  45.5 2.4 %collective-permute-start.11 = (bf16[256,896]{1,0:T(8,128)(2,1)S(1)}, bf16[256,896]{1,0:T(8,128)(2,1)S(1)}, u32[]{:S(2)}, u32[]{:S(2)}) collective-permute-start(bf16[256,896]{1,0:T(8,128)(2,1)S(1)} %get-tuple-element.34.first_ref.rest_0_.rest_10_), channel_id=1, source_target_pairs={{0,2},{2,0},{1,3},{3,1},{4,6},{6,4},{5,7},{7,5},{8,10},{10,8},{9,1... | collective-permute-start | bytes 1376264 | tf_op jit(solution)/shard_map/ppermute | solution.py:414
  45.5 2.5 %collective-permute-start.12 = (bf16[256,896]{1,0:T(8,128)(2,1)S(1)}, bf16[256,896]{1,0:T(8,128)(2,1)S(1)}, u32[]{:S(2)}, u32[]{:S(2)}) collective-permute-start(bf16[256,896]{1,0:T(8,128)(2,1)S(1)} %get-tuple-element.35.second_ref.rest_2_.rest_12_), channel_id=1, source_target_pairs={{0,2},{2,0},{1,3},{3,1},{4,6},{6,4},{5,7},{7,5},{8,10},{10,8},{9,1... | collective-permute-start | bytes 1376264 | tf_op jit(solution)/shard_map/ppermute | solution.py:414
  46.1 11.4 %collective-permute-start.13 = (bf16[256,896]{1,0:T(8,128)(2,1)S(1)}, bf16[256,896]{1,0:T(8,128)(2,1)S(1)}, u32[]{:S(2)}, u32[]{:S(2)}) collective-permute-start(bf16[256,896]{1,0:T(8,128)(2,1)S(1)} %get-tuple-element.36), channel_id=1, source_target_pairs={{0,8},{8,16},{16,24},{24,28},{28,20},{20,12},{12,4},{4,0},{10,2},{... | collective-permute-start | bytes 1376264 | tf_op jit(solution)/shard_map/ppermute | solution.py:437
  47.9 9.5 %collective-permute-start.14 = (bf16[128,896]{1,0:T(8,128)(2,1)S(1)}, bf16[128,896]{1,0:T(8,128)(2,1)S(1)}, u32[]{:S(2)}, u32[]{:S(2)}) collective-permute-start(bf16[128,896]{1,0:T(8,128)(2,1)S(1)} %get-tuple-element.37), channel_id=1, source_target_pairs={{0,10},{8,18},{16,26},{24,30},{28,22},{20,14},{12,6},{4,2},{10,0},... | collective-permute-start | bytes 688136 | tf_op jit(solution)/shard_map/ppermute | solution.py:437
  47.9 9.5 %copy-start.13 = (bf16[256,896]{1,0:T(8,128)(2,1)}, bf16[256,896]{1,0:T(8,128)(2,1)S(1)}, u32[]{:S(2)}) copy-start(bf16[256,896]{1,0:T(8,128)(2,1)S(1)} %collective-permute-done.11.rest_1_.rest_11_) | copy-start | bytes 1376260
  57.5 11.8 %copy-start.3 = (bf16[256,896]{1,0:T(8,128)(2,1)}, bf16[256,896]{1,0:T(8,128)(2,1)S(1)}, u32[]{:S(2)}) copy-start(bf16[256,896]{1,0:T(8,128)(2,1)S(1)} %get-tuple-element.40.rest_14_.rest_0_) | copy-start | bytes 1376260
  65.1 52.7 %all-to-all-start.1 = ((bf16[32,4,4,16,128]{4,3,2,1,0:T(8,128)(2,1)}), bf16[32,4,4,16,128]{4,3,2,1,0:T(8,128)(2,1)S(1)}, u32[]{:S(2)}, u32[]{:S(2)}) async-start(bf16[32,4,4,16,128]{4,3,2,1,0:T(8,128)(2,1)} %bitcast.19), calls=%async_computation.1 | async-start | bytes 4194304 | tf_op jit(solution)/shard_map/all_to_all | solution.py:500
  69.2 52.3 %copy-start.15 = (bf16[256,256]{1,0:T(8,128)(2,1)S(1)}, bf16[256,256]{1,0:T(8,128)(2,1)}, u32[]{:S(2)}) copy-start(bf16[256,256]{1,0:T(8,128)(2,1)} %constant.31.clone.low_ref) | copy-start | bytes 393220
  69.2 52.3 %copy-start.16 = (bf16[256,256]{1,0:T(8,128)(2,1)S(1)}, bf16[256,256]{1,0:T(8,128)(2,1)}, u32[]{:S(2)}) copy-start(bf16[256,256]{1,0:T(8,128)(2,1)} %constant.30.clone.high_ref) | copy-start | bytes 393220
  69.3 52.3 %copy-start.17 = (bf16[128,64]{1,0:T(8,128)(2,1)S(1)}, bf16[128,64]{1,0:T(8,128)(2,1)}, u32[]{:S(2)}) copy-start(bf16[128,64]{1,0:T(8,128)(2,1)} %constant.29.clone.line_ref) | copy-start | bytes 49156
  69.3 1.9 %collective-permute-start.15 = (bf16[256,896]{1,0:T(8,128)(2,1)S(1)}, bf16[256,896]{1,0:T(8,128)(2,1)S(1)}, u32[]{:S(2)}, u32[]{:S(2)}) collective-permute-start(bf16[256,896]{1,0:T(8,128)(2,1)S(1)} %get-tuple-element.40.rest_14_.rest_0_), channel_id=1, source_target_pairs={{0,2},{2,0},{1,3},{3,1},{4,6},{6,4},{5,7},{7,5},{8,10},{10,8},{9,1... | collective-permute-start | bytes 1376264 | tf_op jit(solution)/shard_map/ppermute | solution.py:414
  117.7 52.5 %all-to-all-start = ((bf16[32,4,4,16,128]{4,3,2,1,0:T(8,128)(2,1)}), bf16[32,4,4,16,128]{4,3,2,1,0:T(8,128)(2,1)}, u32[]{:S(2)}, u32[]{:S(2)}) async-start(bf16[32,4,4,16,128]{4,3,2,1,0:T(8,128)(2,1)} %bitcast.20), calls=%async_computation | async-start | bytes 4194304 | tf_op jit(solution)/shard_map/all_to_all | solution.py:500
  (5 other events, 34.5 us)

commit v4 on v3

--- a/solution.py
+++ b/solution.py
@@ -128,9 +128,11 @@
 
 PARTS = 2
 EXCHANGES = ((0, 0, 4), (1, 0, 4))
+AHEAD = 1
 TURN = 64
 GROUP = 16
-ABSORB_LIMIT = 32 * 2**20
+ABSORB_LIMIT = 16 * 2**20
+WHOLE_LIMIT = 28 * 2**20
 TRANSFORM_LIMIT = 24 * 2**20
 SMALL_LIMIT = 2**20
 AXES = ("grid", "tm", "pw")
@@ -172,6 +174,45 @@
     for start in range(0, block_ref.shape[0], TURN):
         turned = jnp.swapaxes(block_ref[start : start + TURN], 0, 1)
         out_ref[:, row + start : row + start + TURN] = turned[first : first + planes]
+
+
+def column_specs(columns, blocks, start):
+    return [
+        pl.BlockSpec(
+            (array.shape[0] // blocks, array.shape[1], array.shape[2] // 2), lambda n, place, core: (place[start + n], 0, core[0])
+        )
+        for array in columns
+    ]
+
+
+def prepare(places, start, core, small, columns, exchange):
+    _, first_pair, pairs = exchange
+    blocks = places.shape[0]
+    count = blocks - start
+    occupied_block = columns[0].shape[0] // blocks
+    width = occupied_block + columns[1].shape[0] // blocks
+    shape = (count, 2 * pairs, width, columns[0].shape[2] // 2)
+
+    def kernel(place_ref, core_ref, *refs):
+        occ_col, unocc_col, ready_ref, token_ref = refs[len(small) :]
+        here = ready_ref.at[pl.program_id(0)]
+        take_planes(occ_col, here, 0, 2 * first_pair)
+        take_planes(unocc_col, here, occupied_block, 2 * first_pair)
+        token_ref[...] = jnp.zeros_like(token_ref)
+
+    return pl.pallas_call(
+        kernel,
+        grid_spec=pltpu.PrefetchScalarGridSpec(
+            num_scalar_prefetch=2,
+            grid=(count,),
+            in_specs=[pl.BlockSpec(memory_space=pltpu.SMEM)] * len(small) + column_specs(columns, blocks, start),
+            out_specs=[pl.BlockSpec(memory_space=pltpu.VMEM), pl.BlockSpec(TOKEN.shape, lambda n, place, core: (0, 0))],
+        ),
+        out_shape=[pltpu.VMEM(shape, jnp.bfloat16), pltpu.VMEM(TOKEN.shape, TOKEN.dtype)],
+        compiler_params=pltpu.CompilerParams(vmem_limit_bytes=16 * SMALL_LIMIT),
+        cost_estimate=expected(0, 2 * math.prod(shape)),
+        name="prepare",
+    )(places, core, *small, *[hbm(array) for array in columns])
 
 
 def mix_response(weight_ref, acc_ref, out_ref):
@@ -194,11 +235,11 @@
                 out_ref[:, f, :, pair, y] = both.reshape(grid_size, pw_size, rows, 2 * NX)
 
 
-def absorb(pieces, exchange, places, core, decays, columns, acc, finish, last):
-    occupied_decay, unoccupied_decay = decays
+def absorb(pieces, exchange, places, start, core, decays, columns, ready, acc, finish, last):
+    time_points, occupied_gap, unoccupied_gap = decays
     occupied_columns, unoccupied_columns = columns
-    times, occupied_count = occupied_decay.shape
-    unoccupied_count = unoccupied_decay.shape[1]
+    times, occupied_count = time_points.shape[0], occupied_gap.shape[0]
+    unoccupied_count = unoccupied_gap.shape[0]
     part, first_pair, pairs = exchange
     planes, planes_local, lanes = 2 * pairs, occupied_columns.shape[1], occupied_columns.shape[2] // 2
     flat = [entry for block in pieces for entry in block]
@@ -208,14 +249,23 @@
     occupied_block = occupied_count * width // (occupied_count + unoccupied_count)
     unoccupied_block = width - occupied_block
     first_call = acc is None
-
-    def kernel(place_ref, core_ref, occ_ref, unocc_ref, occ_col, unocc_col, *rest):
+    blocks = len(pieces)
+
+    def kernel(place_ref, core_ref, time_ref, occ_ref, unocc_ref, *rest):
+        col_refs, rest = rest[: 2 if ready is None else 1], rest[2 if ready is None else 1 :]
         refs, rest = rest[: len(flat)], rest[len(flat) :]
         if not first_call:
             rest = rest[1:]
-        weight_ref, acc_ref, last_ref, weighed, taken = rest
-        take_planes(occ_col, taken, 0, 2 * first_pair)
-        take_planes(unocc_col, taken, occupied_block, 2 * first_pair)
+        weight_ref, acc_ref, last_ref, weighed, *taken = rest
+        if ready is None:
+            (taken,) = taken
+            take_planes(col_refs[0], taken, 0, 2 * first_pair)
+            take_planes(col_refs[1], taken, occupied_block, 2 * first_pair)
+        else:
+            taken = col_refs[0].at[ready[1] + pl.program_id(0)]
+        factors = [
+            [jnp.exp(-ref[...] * time_ref[t]) for ref in (occ_ref, unocc_ref)] for t in range(times)
+        ]
         for n, block in enumerate(pieces):
             mine, refs = refs[: len(block)], refs[len(block) :]
 
@@ -226,11 +276,10 @@
                     values = ref[...].astype(jnp.float32)
                     for t in range(times):
                         at = pl.ds(pl.multiple_of(t * points + side * half, half), half)
-                        for low, high, rates in ((0, occupied_block, occ_ref), (occupied_block, width, unocc_ref)):
-                            scaled = values[:, low:high] * rates[t : t + 1, :]
-                            weighed[at, low:high] = scaled.astype(jnp.bfloat16)
-
-        if first_call:
+                        for low, high, factor in ((0, occupied_block, factors[t][0]), (occupied_block, width, factors[t][1])):
+                            weighed[at, low:high] = (values[:, low:high] * factor).astype(jnp.bfloat16)
+
+        if first_call and blocks > 1:
 
             @pl.when(pl.program_id(0) == 0)
             def _():
@@ -238,7 +287,11 @@
 
         for z in range(planes):
             for kind, at in enumerate((slice(0, occupied_block), slice(occupied_block, width))):
-                acc_ref[kind, z] += jnp.dot(weighed[:, at], taken[z, at], preferred_element_type=jnp.float32)
+                part_sum = jnp.dot(weighed[:, at], taken[z, at], preferred_element_type=jnp.float32)
+                if first_call and blocks == 1:
+                    acc_ref[kind, z] = part_sum
+                else:
+                    acc_ref[kind, z] += part_sum
 
         if last:
 
@@ -251,13 +304,19 @@
 
     total = (2, planes, times * points, lanes)
     kept = pl.BlockSpec(memory_space=pltpu.VMEM)
-    operands = [places, core, occupied_decay, unoccupied_decay, hbm(occupied_columns), hbm(unoccupied_columns)]
+    operands = [places, core, time_points, occupied_gap.reshape(1, -1), unoccupied_gap.reshape(1, -1)]
+    if ready is None:
+        operands += [hbm(occupied_columns), hbm(unoccupied_columns)]
+        column_in = column_specs(columns, places.shape[0], start)
+    else:
+        operands.append(pltpu.with_memory_space_constraint(ready[0], pltpu.VMEM))
+        column_in = [kept]
     operands += [hbm(entry[0]) if first_call and last else entry[0] for entry in flat]
     in_specs = [
-        pl.BlockSpec((times, occupied_block), lambda n, place, core: (0, place[n])),
-        pl.BlockSpec((times, unoccupied_block), lambda n, place, core: (0, place[n])),
-        pl.BlockSpec((occupied_block, planes_local, lanes), lambda n, place, core: (place[n], 0, core[0])),
-        pl.BlockSpec((unoccupied_block, planes_local, lanes), lambda n, place, core: (place[n], 0, core[0])),
+        pl.BlockSpec(memory_space=pltpu.SMEM),
+        pl.BlockSpec((1, occupied_block), lambda n, place, core: (0, place[start + n])),
+        pl.BlockSpec((1, unoccupied_block), lambda n, place, core: (0, place[start + n])),
+        *column_in,
     ] + [pl.BlockSpec((half, width), lambda n, place, core: (part, 0)) for entry in flat]
     out_specs, out_shape, aliases = [kept], [pltpu.VMEM(total, jnp.float32)], {}
     if not first_call:
@@ -275,7 +334,6 @@
     else:
         out_specs.append(pl.BlockSpec(TOKEN.shape, lambda n, place, core: (0, 0)))
         out_shape.append(pltpu.VMEM(TOKEN.shape, TOKEN.dtype))
-    blocks = len(pieces)
     return pl.pallas_call(
         kernel,
         grid_spec=pltpu.PrefetchScalarGridSpec(
@@ -285,12 +343,12 @@
             out_specs=out_specs,
             scratch_shapes=[
                 pltpu.VMEM((times * points, width), jnp.bfloat16),
-                pltpu.VMEM((planes, width, lanes), jnp.bfloat16),
-            ],
+            ]
+            + ([pltpu.VMEM((planes, width, lanes), jnp.bfloat16)] if ready is None else []),
         ),
         out_shape=out_shape,
         input_output_aliases=aliases,
-        compiler_params=pltpu.CompilerParams(vmem_limit_bytes=ABSORB_LIMIT),
+        compiler_params=pltpu.CompilerParams(vmem_limit_bytes=WHOLE_LIMIT if first_call and last else ABSORB_LIMIT),
         cost_estimate=expected(
             blocks * 2 * times * points * width * planes * lanes, blocks * 2 * width * (points + planes_local * lanes)
         ),
@@ -373,18 +431,18 @@
     return onward, back, arrivals
 
 
-def after(arrays, token):
+def after(arrays, *tokens):
     count = len(arrays)
     anywhere = pl.BlockSpec(memory_space=pl.ANY)
     return pl.pallas_call(
         lambda *refs: None,
-        in_specs=[anywhere] * count + [pl.BlockSpec(memory_space=pltpu.VMEM)],
+        in_specs=[anywhere] * count + [pl.BlockSpec(memory_space=pltpu.VMEM)] * len(tokens),
         out_specs=[anywhere] * count,
         out_shape=[jax.ShapeDtypeStruct(array.shape, array.dtype) for array in arrays],
         input_output_aliases={n: n for n in range(count)},
         compiler_params=pltpu.CompilerParams(vmem_limit_bytes=SMALL_LIMIT),
         name="after",
-    )(*arrays, pltpu.with_memory_space_constraint(token, pltpu.VMEM))
+    )(*arrays, *[pltpu.with_memory_space_constraint(token, pltpu.VMEM) for token in tokens])
 
 
 def choose(core, first, second):
@@ -419,17 +477,20 @@
     return jnp.sum(jnp.where(here, table, jnp.zeros_like(table)), axis=-1)
 
 
-def gather_and_absorb(mine, core, places, ring, absorb_blocks):
+def gather_and_absorb(mine, core, places, ring, columns, small, absorb_blocks):
     number = lax.axis_size("grid")
     onward, back = ring
     blocks, every, acc = [swapped(mine)], [], None
+    ready, token = prepare(places, number - AHEAD, core, small, columns, EXCHANGES[0])
+    tokens = [token]
     up = down = mine
     for hops in range(1, number // 2):
         up, down = lax.ppermute(up, "grid", onward), lax.ppermute(down, "grid", back)
         start = len(every)
         every += blocks
-        acc, token = absorb_blocks(blocks, EXCHANGES[0], places[start : len(every)], acc, False)
-        up, down = after([up, down], token)
+        acc, token = absorb_blocks(blocks, EXCHANGES[0], start, None, acc, False)
+        up, down = after([up, down], token, *tokens)
+        tokens = []
         blocks = [swapped(up), swapped(down)]
     far, some = choose(core, up, down)
     sides = list(enumerate((onward, back)))
@@ -441,10 +502,12 @@
     ]
     start = len(every)
     every += blocks
-    acc, token = absorb_blocks(blocks, EXCHANGES[0], places[start : len(every)], acc, False)
+    acc, token = absorb_blocks(
+        blocks, EXCHANGES[0], start, (ready, 0) if AHEAD > len(blocks) else None, acc, False
+    )
     own, other = after([own, other], token)
     blocks = [[(own, 0), (other, 1)]]
-    _, sent = absorb_blocks(blocks, EXCHANGES[0], places[number - 1 :], acc, True)
+    _, sent = absorb_blocks(blocks, EXCHANGES[0], number - 1, (ready, AHEAD - 1), acc, True)
     return sent, every + blocks, every + [swapped(own)]
 
 
@@ -479,23 +542,22 @@
     frequency_weights = pick(time_weight, time_index)[None, :] * jnp.cos(
         pick(frequency_table, frequency_index)[:, None] * time_points[None, :]
     )
-    occupied_decay = jnp.exp(-occupied_gap[None, :] * time_points[:, None])
-    unoccupied_decay = jnp.exp(-unoccupied_gap[None, :] * time_points[:, None])
 
     columns = (occupied_columns, unoccupied_columns)
     finish = (-frequency_weights, (grid_size, pw_size))
 
-    def absorb_blocks(pieces, exchange, here, acc, last):
-        return absorb(pieces, exchange, here, core, (occupied_decay, unoccupied_decay), columns, acc, finish, last)
+    def absorb_blocks(pieces, exchange, start, ready, acc, last):
+        decays = (time_points, occupied_gap, unoccupied_gap)
+        return absorb(pieces, exchange, places, start, core, decays, columns, ready, acc, finish, last)
 
     tables = (jnp.asarray(line_operator(NY)),) + tuple(jnp.asarray(t) for t in row_operator(NX))
     mine = jnp.swapaxes(by_owner, 0, 1).reshape(SLAB // tm_size, -1)
     result = None
     for exchange in EXCHANGES:
         if exchange == EXCHANGES[0]:
-            sent, *blocks = gather_and_absorb(mine, core, places, (onward, back), absorb_blocks)
+            sent, *blocks = gather_and_absorb(mine, core, places, (onward, back), columns, (time_points, finish[0]), absorb_blocks)
         else:
-            _, sent = absorb_blocks(blocks[exchange[0]], exchange, places, None, True)
+            _, sent = absorb_blocks(blocks[exchange[0]], exchange, 0, None, None, True)
         sent = sent.reshape((-1,) + sent.shape[3:])
         received = lax.all_to_all(sent, AXES, split_axis=0, concat_axis=0, tiled=True)
         received = received.reshape((grid_size * tm_size, pw_size) + received.shape[1:])

time: 179 us -> 177 us (0.989)
  Pallas kernels: 92.7 us -> 95.4 us
  other arithmetic: 5.1 us -> 2.66 us
    pallas_call x0 -> x1, Pallas kernels: none -> 3.49 us  [prepare(): pl.pallas_call(kernel, grid_spec=pltpu.PrefetchScalarGridSpec(num_scalar_...]
  transfers between devices with their start and end apart: 18 -> 18, of which waited for: 9 -> 9; matrix products, arithmetic and copies ran while one was open for 3% -> 2% of each run, Pallas kernels for 43% -> 46%
where the time goes in v4:
time: 177 us
  Pallas kernels  95.4 us (54%)
  waiting for transfers between devices  57.3 us (32%)
  starting transfers between devices  18.8 us (11%)
  other arithmetic  2.66 us (2%)
  local copies, waits for them, and re-layouts  2.47 us (1%)
    pallas_call x6, Pallas kernels, absorb(): pl.pallas_call(kernel, grid_spec=pltpu.PrefetchScalarGridSpec(num_scalar_...  77.3 us
    all_to_all x2, waiting for transfers between devices, shards(): lax.all_to_all(sent, AXES, split_axis=0, concat_axis=0, tiled=True)  50.7 us
    pallas_call x2, Pallas kernels, transform(): pl.pallas_call(kernel, grid=(pw_size, pairs // step), in_specs=in_specs,...  14.5 us
    all_to_all x2, starting transfers between devices, shards(): lax.all_to_all(sent, AXES, split_axis=0, concat_axis=0, tiled=True)  7.97 us
    ppermute x3, starting transfers between devices, gather_and_absorb(): lax.ppermute(down, 'grid', back)  3.62 us
    ppermute x3, starting transfers between devices, gather_and_absorb(): lax.ppermute(up, 'grid', onward)  3.58 us
  transfers between devices with their start and end apart: 18, of which 9 were waited for; matrix products, arithmetic and copies ran while one was open for 2% of the time, Pallas kernels for 46%

profile of v4, /device:TPU:0, one launch (start us, length us, event | category | flops | bytes accessed | tf_op | source)
XLA Modules:
  0.0 177.0 jit_solution(7086791922462816647)
XLA Ops:
  0.0 1.5 copy.32
  1.7 3.0 %collective-permute-start.2 = (bf16[256,896]{1,0:T(8,128)(2,1)S(1)}, bf16[256,896]{1,0:T(8,128)(2,1)S(1)}, u32[]{:S(2)}, u32[]{:S(2)}) collective-permute-start(bf16[256,896]{1,0:T(8,128)(2,1)S(1)} %bitcast.16), channel_id=1, source_target_pairs={{8,0},{16,8},{24,16},{28,24},{20,28},{12,20},{4,12},{0,4},{9,1},{1... | collective-permute-start | bytes 1376264 | tf_op jit(solution)/shard_map/ppermute | solution.py:488
  4.8 0.8 select_reduce_fusion.1
  5.6 0.9 select_reduce_fusion.2
  6.5 0.8 select_reduce_fusion.place_ref
  7.5 3.5 %prepare.1 = (bf16[1,8,896,256]{3,2,1,0:T(8,128)(2,1)S(1)}, f32[8,128]{1,0:T(8,128)S(1)}) custom-call(s32[8]{0:T(128)S(1)} %select_reduce_fusion.place_ref, s32[1]{0:T(128)} %bitcast.core_ref, f32[2]{0:T(128)S(1)} %get-tuple-element.50.time_ref.refs_0_, f32[2,2]{1,0:T(2,128)S(1)} %multiply_negate_fusion.rest_4_.refs_1_.rest_7_.rest_18_, ...), custom_call_target="tpu_custom_call" | custom-call | bytes 3670016 | tf_op jit(solution)/shard_map/prepare/pallas_call | solution.py:203
  11.0 5.3 %absorb.6 = (f32[2,8,512,256]{3,2,1,0:T(8,128)S(1)}, f32[8,128]{1,0:T(8,128)S(1)}) custom-call(s32[8]{0:T(128)S(1)} %select_reduce_fusion.place_ref, s32[1]{0:T(128)} %bitcast.core_ref, f32[2]{0:T(128)S(1)} %get-tuple-element.50.time_ref.refs_0_, f32[1,1024]{1,0:T(1,128)S(1)} %bitcast.27, f32[1,6144]{1,0:T(1,128)S(1)} %bitcast.21, ...), custom_call_target="tpu_custom_call" | custom-call | flops 1879048192 | bytes 4128768 | tf_op jit(solution)/shard_map/absorb/pallas_call | solution.py:337
  16.7 0.3 collective-permute-start.3
  17.2 1.9 %collective-permute-start.5 = (bf16[256,896]{1,0:T(8,128)(2,1)S(1)}, bf16[256,896]{1,0:T(8,128)(2,1)S(1)}, u32[]{:S(2)}, u32[]{:S(2)}) collective-permute-start(bf16[256,896]{1,0:T(8,128)(2,1)S(1)} %get-tuple-element.29.rest_2_.rest_4_), channel_id=1, source_target_pairs={{0,8},{8,16},{16,24},{24,28},{28,20},{20,12},{12,4},{4,0},{1,9},{9... | collective-permute-start | bytes 1376264 | tf_op jit(solution)/shard_map/ppermute | solution.py:488
  19.2 9.7 %absorb.7 = (f32[2,8,512,256]{3,2,1,0:T(8,128)S(1)}, f32[8,128]{1,0:T(8,128)S(1)}) custom-call(s32[8]{0:T(128)S(1)} %select_reduce_fusion.place_ref, s32[1]{0:T(128)} %bitcast.core_ref, f32[2]{0:T(128)S(1)} %get-tuple-element.50.time_ref.refs_0_, f32[1,1024]{1,0:T(1,128)S(1)} %bitcast.28, f32[1,6144]{1,0:T(1,128)S(1)} %bitcast.22, ...), custom_call_target="tpu_custom_call", output_to_operand_aliasing={{0}: (11, {})} | custom-call | flops 3758096384 | bytes 8257536 | tf_op jit(solution)/shard_map/absorb/pallas_call | solution.py:337
  29.0 1.1 collective-permute-done.5.refs_0_
  30.1 1.5 collective-permute-done.6.refs_1_
  31.6 0.5 collective-permute-start.8
  32.1 1.6 collective-permute-start.9
  33.7 0.4 collective-permute-start.10
  34.2 9.7 %absorb.8 = (f32[2,8,512,256]{3,2,1,0:T(8,128)S(1)}, f32[8,128]{1,0:T(8,128)S(1)}) custom-call(s32[8]{0:T(128)S(1)} %select_reduce_fusion.place_ref, s32[1]{0:T(128)} %bitcast.core_ref, f32[2]{0:T(128)S(1)} %get-tuple-element.50.time_ref.refs_0_, f32[1,1024]{1,0:T(1,128)S(1)} %bitcast.29, f32[1,6144]{1,0:T(1,128)S(1)} %bitcast.23, ...), custom_call_target="tpu_custom_call", output_to_operand_aliasing={{0}: (11, {})} | custom-call | flops 3758096384 | bytes 8257536 | tf_op jit(solution)/shard_map/absorb/pallas_call | solution.py:337
  44.0 0.7 collective-permute-done.9.refs_0_
  44.6 1.3 collective-permute-done.10.refs_1_
  46.0 0.5 collective-permute-start.12
  46.5 1.8 %collective-permute-start.13 = (bf16[256,896]{1,0:T(8,128)(2,1)S(1)}, bf16[256,896]{1,0:T(8,128)(2,1)S(1)}, u32[]{:S(2)}, u32[]{:S(2)}) collective-permute-start(bf16[256,896]{1,0:T(8,128)(2,1)S(1)} %get-tuple-element.39), channel_id=1, source_target_pairs={{0,8},{8,16},{16,24},{24,28},{28,20},{20,12},{12,4},{4,0},{10,2},{... | collective-permute-start | bytes 1376264 | tf_op jit(solution)/shard_map/ppermute | solution.py:498
  48.4 9.7 %absorb.9 = (f32[2,8,512,256]{3,2,1,0:T(8,128)S(1)}, f32[8,128]{1,0:T(8,128)S(1)}) custom-call(s32[8]{0:T(128)S(1)} %select_reduce_fusion.place_ref, s32[1]{0:T(128)} %bitcast.core_ref, f32[2]{0:T(128)S(1)} %get-tuple-element.50.time_ref.refs_0_, f32[1,1024]{1,0:T(1,128)S(1)} %bitcast.30, f32[1,6144]{1,0:T(1,128)S(1)} %bitcast.24, ...), custom_call_target="tpu_custom_call", output_to_operand_aliasing={{0}: (11, {})} | custom-call | flops 3758096384 | bytes 8257536 | tf_op jit(solution)/shard_map/absorb/pallas_call | solution.py:337
  58.2 5.8 %absorb.11 = (f32[2,8,512,256]{3,2,1,0:T(8,128)S(1)}, bf16[8,2,2,4,4,16,128]{6,5,4,3,2,1,0:T(8,128)(2,1)}) custom-call(s32[8]{0:T(128)S(1)} %select_reduce_fusion.place_ref, s32[1]{0:T(128)} %bitcast.core_ref, f32[2]{0:T(128)S(1)} %get-tuple-element.50.time_ref.refs_0_, f32[1,1024]{1,0:T(1,128)S(1)} %bitcast.31, ...), custom_call_target="tpu_custom_call", output_to_operand_aliasing={{0}: (8, {})} | custom-call | flops 1879048192 | bytes 4128768 | tf_op jit(solution)/shard_map/absorb/pallas_call | solution.py:337
  64.0 3.9 %all-to-all-start.1 = ((bf16[32,4,4,16,128]{4,3,2,1,0:T(8,128)(2,1)}), bf16[32,4,4,16,128]{4,3,2,1,0:T(8,128)(2,1)S(1)}, u32[]{:S(2)}, u32[]{:S(2)}) async-start(bf16[32,4,4,16,128]{4,3,2,1,0:T(8,128)(2,1)} %bitcast.33), calls=%async_computation.1 | async-start | bytes 4194304 | tf_op jit(solution)/shard_map/all_to_all | solution.py:562
  68.0 0.3 collective-permute-start.15
  68.4 1.6 collective-permute-done.15.rest_17_
  69.9 0.8 copy-done.20
  70.7 37.0 %absorb.10 = (f32[2,8,512,256]{3,2,1,0:T(8,128)}, bf16[8,2,2,4,4,16,128]{6,5,4,3,2,1,0:T(8,128)(2,1)}) custom-call(s32[8]{0:T(128)S(1)} %select_reduce_fusion.place_ref, s32[1]{0:T(128)} %bitcast.core_ref, f32[2]{0:T(128)S(1)} %get-tuple-element.50.time_ref.refs_0_, f32[1,1024]{1,0:T(1,128)S(1)} %bitcast.32, f32[1,6144]{1,0:T(1,128)S(1)} %bitcast.26, ...), custom_call_target="tpu_custom_call" | custom-call | flops 15032385536 | bytes 33030144 | tf_op jit(solution)/shard_map/absorb/pallas_call | solution.py:337
  107.7 9.0 %all-to-all-done.1 = bf16[32,4,4,16,128]{4,3,2,1,0:T(8,128)(2,1)S(1)} async-done(((bf16[32,4,4,16,128]{4,3,2,1,0:T(8,128)(2,1)}), bf16[32,4,4,16,128]{4,3,2,1,0:T(8,128)(2,1)S(1)}, u32[]{:S(2)}, u32[]{:S(2)}) %all-to-all-start.1) | async-done | bytes 2097184 | tf_op jit(solution)/shard_map/all_to_all | solution.py:562
  116.7 4.0 %all-to-all-start = ((bf16[32,4,4,16,128]{4,3,2,1,0:T(8,128)(2,1)}), bf16[32,4,4,16,128]{4,3,2,1,0:T(8,128)(2,1)}, u32[]{:S(2)}, u32[]{:S(2)}) async-start(bf16[32,4,4,16,128]{4,3,2,1,0:T(8,128)(2,1)} %bitcast.34), calls=%async_computation | async-start | bytes 4194304 | tf_op jit(solution)/shard_map/all_to_all | solution.py:562
  120.8 6.8 %transform.2.rest_0_ = f32[1,32,16,64,128]{4,3,2,1,0:T(8,128)} custom-call(bf16[128,64]{1,0:T(8,128)(2,1)S(1)} %copy-done.19, bf16[256,256]{1,0:T(8,128)(2,1)S(1)} %copy-done.17, bf16[256,256]{1,0:T(8,128)(2,1)S(1)} %copy-done.16, bf16[16,2,4,4,16,128]{5,4,3,2,1,0:T(8,128)(2,1)S(1)} %bitcast.15), custom_call_target="tpu_custom_call" | custom-call | flops 1879048192 | bytes 10485760 | tf_op jit(solution)/shard_map/transform/pallas_call | solution.py:404
  127.6 41.7 %all-to-all-done = bf16[32,4,4,16,128]{4,3,2,1,0:T(8,128)(2,1)} async-done(((bf16[32,4,4,16,128]{4,3,2,1,0:T(8,128)(2,1)}), bf16[32,4,4,16,128]{4,3,2,1,0:T(8,128)(2,1)}, u32[]{:S(2)}, u32[]{:S(2)}) %all-to-all-start) | async-done | bytes 2097184 | tf_op jit(solution)/shard_map/all_to_all | solution.py:562
  169.2 7.8 %transform.3 = f32[1,32,16,64,128]{4,3,2,1,0:T(8,128)} custom-call(bf16[128,64]{1,0:T(8,128)(2,1)S(1)} %copy-done.19, bf16[256,256]{1,0:T(8,128)(2,1)S(1)} %copy-done.17, bf16[256,256]{1,0:T(8,128)(2,1)S(1)} %copy-done.16, bf16[16,2,4,4,16,128]{5,4,3,2,1,0:T(8,128)(2,1)} %bitcast.9.in_ref, ...), custom_call_target="tpu_custom_call", output_to_operand_aliasing={{}: (4, {})} | custom-call | flops 1879048192 | bytes 10485760 | tf_op jit(solution)/shard_map/transform/pallas_call | solution.py:404
  (68 shorter events, 1.2 us)
Async XLA Ops:
  1.7 14.7 %collective-permute-start.2 = (bf16[256,896]{1,0:T(8,128)(2,1)S(1)}, bf16[256,896]{1,0:T(8,128)(2,1)S(1)}, u32[]{:S(2)}, u32[]{:S(2)}) collective-permute-start(bf16[256,896]{1,0:T(8,128)(2,1)S(1)} %bitcast.16), channel_id=1, source_target_pairs={{8,0},{16,8},{24,16},{28,24},{20,28},{12,20},{4,12},{0,4},{9,1},{1... | collective-permute-start | bytes 1376264 | tf_op jit(solution)/shard_map/ppermute | solution.py:488
  4.7 12.0 %collective-permute-start.1 = (bf16[256,896]{1,0:T(8,128)(2,1)S(1)}, bf16[256,896]{1,0:T(8,128)(2,1)S(1)}, u32[]{:S(2)}, u32[]{:S(2)}) collective-permute-start(bf16[256,896]{1,0:T(8,128)(2,1)S(1)} %bitcast.17), channel_id=1, source_target_pairs={{0,8},{8,16},{16,24},{24,28},{28,20},{20,12},{12,4},{4,0},{1,9},{9... | collective-permute-start | bytes 1376264 | tf_op jit(solution)/shard_map/ppermute | solution.py:488
  4.8 6.2 %collective-permute-start = (bf16[256,896]{1,0:T(8,128)(2,1)S(1)}, bf16[256,896]{1,0:T(8,128)(2,1)S(1)}, u32[]{:S(2)}, u32[]{:S(2)}) collective-permute-start(bf16[256,896]{1,0:T(8,128)(2,1)S(1)} %bitcast.18), channel_id=1, source_target_pairs={{0,2},{2,0},{1,3},{3,1},{4,6},{6,4},{5,7},{7,5},{8,10},{10,8},{9,1... | collective-permute-start | bytes 1376264 | tf_op jit(solution)/shard_map/ppermute | solution.py:472
  16.7 12.3 %copy-start.4 = (bf16[256,896]{1,0:T(8,128)(2,1)}, bf16[256,896]{1,0:T(8,128)(2,1)S(1)}, u32[]{:S(2)}) copy-start(bf16[256,896]{1,0:T(8,128)(2,1)S(1)} %get-tuple-element.30.rest_4_.rest_6_) | copy-start | bytes 1376260
  16.7 12.3 %copy-start.5 = (bf16[256,896]{1,0:T(8,128)(2,1)}, bf16[256,896]{1,0:T(8,128)(2,1)S(1)}, u32[]{:S(2)}) copy-start(bf16[256,896]{1,0:T(8,128)(2,1)S(1)} %get-tuple-element.29.rest_2_.rest_4_) | copy-start | bytes 1376260
  16.7 2.5 %collective-permute-start.3 = (bf16[256,896]{1,0:T(8,128)(2,1)S(1)}, bf16[256,896]{1,0:T(8,128)(2,1)S(1)}, u32[]{:S(2)}, u32[]{:S(2)}) collective-permute-start(bf16[256,896]{1,0:T(8,128)(2,1)S(1)} %get-tuple-element.29.rest_2_.rest_4_), channel_id=1, source_target_pairs={{0,2},{2,0},{1,3},{3,1},{4,6},{6,4},{5,7},{7,5},{8,10},{10,8},{9,1... | collective-permute-start | bytes 1376264 | tf_op jit(solution)/shard_map/ppermute | solution.py:472
  17.0 2.2 %collective-permute-start.4 = (bf16[256,896]{1,0:T(8,128)(2,1)S(1)}, bf16[256,896]{1,0:T(8,128)(2,1)S(1)}, u32[]{:S(2)}, u32[]{:S(2)}) collective-permute-start(bf16[256,896]{1,0:T(8,128)(2,1)S(1)} %get-tuple-element.30.rest_4_.rest_6_), channel_id=1, source_target_pairs={{0,2},{2,0},{1,3},{3,1},{4,6},{6,4},{5,7},{7,5},{8,10},{10,8},{9,1... | collective-permute-start | bytes 1376264 | tf_op jit(solution)/shard_map/ppermute | solution.py:472
  17.2 12.9 %collective-permute-start.5 = (bf16[256,896]{1,0:T(8,128)(2,1)S(1)}, bf16[256,896]{1,0:T(8,128)(2,1)S(1)}, u32[]{:S(2)}, u32[]{:S(2)}) collective-permute-start(bf16[256,896]{1,0:T(8,128)(2,1)S(1)} %get-tuple-element.29.rest_2_.rest_4_), channel_id=1, source_target_pairs={{0,8},{8,16},{16,24},{24,28},{28,20},{20,12},{12,4},{4,0},{1,9},{9... | collective-permute-start | bytes 1376264 | tf_op jit(solution)/shard_map/ppermute | solution.py:488
  19.0 12.6 %collective-permute-start.6 = (bf16[256,896]{1,0:T(8,128)(2,1)S(1)}, bf16[256,896]{1,0:T(8,128)(2,1)S(1)}, u32[]{:S(2)}, u32[]{:S(2)}) collective-permute-start(bf16[256,896]{1,0:T(8,128)(2,1)S(1)} %get-tuple-element.30.rest_4_.rest_6_), channel_id=1, source_target_pairs={{8,0},{16,8},{24,16},{28,24},{20,28},{12,20},{4,12},{0,4},{9,1},{1... | collective-permute-start | bytes 1376264 | tf_op jit(solution)/shard_map/ppermute | solution.py:488
  19.2 9.8 %copy-start.10 = (bf16[256,896]{1,0:T(8,128)(2,1)}, bf16[256,896]{1,0:T(8,128)(2,1)S(1)}, u32[]{:S(2)}) copy-start(bf16[256,896]{1,0:T(8,128)(2,1)S(1)} %collective-permute-done.4.rest_5_.rest_7_) | copy-start | bytes 1376260
  31.6 12.3 %copy-start.6 = (bf16[256,896]{1,0:T(8,128)(2,1)}, bf16[256,896]{1,0:T(8,128)(2,1)S(1)}, u32[]{:S(2)}) copy-start(bf16[256,896]{1,0:T(8,128)(2,1)S(1)} %get-tuple-element.33.rest_2_.rest_8_) | copy-start | bytes 1376260
  31.6 12.3 %copy-start.7 = (bf16[256,896]{1,0:T(8,128)(2,1)}, bf16[256,896]{1,0:T(8,128)(2,1)S(1)}, u32[]{:S(2)}) copy-start(bf16[256,896]{1,0:T(8,128)(2,1)S(1)} %get-tuple-element.34.rest_4_.rest_10_) | copy-start | bytes 1376260
  31.6 2.5 %collective-permute-start.7 = (bf16[256,896]{1,0:T(8,128)(2,1)S(1)}, bf16[256,896]{1,0:T(8,128)(2,1)S(1)}, u32[]{:S(2)}, u32[]{:S(2)}) collective-permute-start(bf16[256,896]{1,0:T(8,128)(2,1)S(1)} %get-tuple-element.33.rest_2_.rest_8_), channel_id=1, source_target_pairs={{0,2},{2,0},{1,3},{3,1},{4,6},{6,4},{5,7},{7,5},{8,10},{10,8},{9,1... | collective-permute-start | bytes 1376264 | tf_op jit(solution)/shard_map/ppermute | solution.py:472
  31.6 2.5 %collective-permute-start.8 = (bf16[256,896]{1,0:T(8,128)(2,1)S(1)}, bf16[256,896]{1,0:T(8,128)(2,1)S(1)}, u32[]{:S(2)}, u32[]{:S(2)}) collective-permute-start(bf16[256,896]{1,0:T(8,128)(2,1)S(1)} %get-tuple-element.34.rest_4_.rest_10_), channel_id=1, source_target_pairs={{0,2},{2,0},{1,3},{3,1},{4,6},{6,4},{5,7},{7,5},{8,10},{10,8},{9,1... | collective-permute-start | bytes 1376264 | tf_op jit(solution)/shard_map/ppermute | solution.py:472
  32.1 12.5 %collective-permute-start.9 = (bf16[256,896]{1,0:T(8,128)(2,1)S(1)}, bf16[256,896]{1,0:T(8,128)(2,1)S(1)}, u32[]{:S(2)}, u32[]{:S(2)}) collective-permute-start(bf16[256,896]{1,0:T(8,128)(2,1)S(1)} %get-tuple-element.33.rest_2_.rest_8_), channel_id=1, source_target_pairs={{0,8},{8,16},{16,24},{24,28},{28,20},{20,12},{12,4},{4,0},{1,9},{9... | collective-permute-start | bytes 1376264 | tf_op jit(solution)/shard_map/ppermute | solution.py:488
  33.7 12.2 %collective-permute-start.10 = (bf16[256,896]{1,0:T(8,128)(2,1)S(1)}, bf16[256,896]{1,0:T(8,128)(2,1)S(1)}, u32[]{:S(2)}, u32[]{:S(2)}) collective-permute-start(bf16[256,896]{1,0:T(8,128)(2,1)S(1)} %get-tuple-element.34.rest_4_.rest_10_), channel_id=1, source_target_pairs={{8,0},{16,8},{24,16},{28,24},{20,28},{12,20},{4,12},{0,4},{9,1},{1... | collective-permute-start | bytes 1376264 | tf_op jit(solution)/shard_map/ppermute | solution.py:488
  34.2 9.8 %copy-start.11 = (bf16[256,896]{1,0:T(8,128)(2,1)}, bf16[256,896]{1,0:T(8,128)(2,1)S(1)}, u32[]{:S(2)}) copy-start(bf16[256,896]{1,0:T(8,128)(2,1)S(1)} %collective-permute-done.7.rest_3_.rest_9_) | copy-start | bytes 1376260
  34.2 9.8 %copy-start.12 = (bf16[256,896]{1,0:T(8,128)(2,1)}, bf16[256,896]{1,0:T(8,128)(2,1)S(1)}, u32[]{:S(2)}) copy-start(bf16[256,896]{1,0:T(8,128)(2,1)S(1)} %collective-permute-done.8.rest_5_.rest_11_) | copy-start | bytes 1376260
  45.9 12.2 %copy-start = (bf16[256,896]{1,0:T(8,128)(2,1)}, bf16[256,896]{1,0:T(8,128)(2,1)S(1)}, u32[]{:S(2)}) copy-start(bf16[256,896]{1,0:T(8,128)(2,1)S(1)} %get-tuple-element.37.first_ref.rest_2_.rest_12_) | copy-start | bytes 1376260
  45.9 12.2 %copy-start.1 = (bf16[256,896]{1,0:T(8,128)(2,1)}, bf16[256,896]{1,0:T(8,128)(2,1)S(1)}, u32[]{:S(2)}) copy-start(bf16[256,896]{1,0:T(8,128)(2,1)S(1)} %get-tuple-element.38.second_ref.rest_4_.rest_14_) | copy-start | bytes 1376260
  45.9 2.4 %collective-permute-start.11 = (bf16[256,896]{1,0:T(8,128)(2,1)S(1)}, bf16[256,896]{1,0:T(8,128)(2,1)S(1)}, u32[]{:S(2)}, u32[]{:S(2)}) collective-permute-start(bf16[256,896]{1,0:T(8,128)(2,1)S(1)} %get-tuple-element.37.first_ref.rest_2_.rest_12_), channel_id=1, source_target_pairs={{0,2},{2,0},{1,3},{3,1},{4,6},{6,4},{5,7},{7,5},{8,10},{10,8},{9,1... | collective-permute-start | bytes 1376264 | tf_op jit(solution)/shard_map/ppermute | solution.py:472
  46.0 2.5 %collective-permute-start.12 = (bf16[256,896]{1,0:T(8,128)(2,1)S(1)}, bf16[256,896]{1,0:T(8,128)(2,1)S(1)}, u32[]{:S(2)}, u32[]{:S(2)}) collective-permute-start(bf16[256,896]{1,0:T(8,128)(2,1)S(1)} %get-tuple-element.38.second_ref.rest_4_.rest_14_), channel_id=1, source_target_pairs={{0,2},{2,0},{1,3},{3,1},{4,6},{6,4},{5,7},{7,5},{8,10},{10,8},{9,1... | collective-permute-start | bytes 1376264 | tf_op jit(solution)/shard_map/ppermute | solution.py:472
  46.5 11.7 %collective-permute-start.13 = (bf16[256,896]{1,0:T(8,128)(2,1)S(1)}, bf16[256,896]{1,0:T(8,128)(2,1)S(1)}, u32[]{:S(2)}, u32[]{:S(2)}) collective-permute-start(bf16[256,896]{1,0:T(8,128)(2,1)S(1)} %get-tuple-element.39), channel_id=1, source_target_pairs={{0,8},{8,16},{16,24},{24,28},{28,20},{20,12},{12,4},{4,0},{10,2},{... | collective-permute-start | bytes 1376264 | tf_op jit(solution)/shard_map/ppermute | solution.py:498
  48.3 9.8 %collective-permute-start.14 = (bf16[128,896]{1,0:T(8,128)(2,1)S(1)}, bf16[128,896]{1,0:T(8,128)(2,1)S(1)}, u32[]{:S(2)}, u32[]{:S(2)}) collective-permute-start(bf16[128,896]{1,0:T(8,128)(2,1)S(1)} %get-tuple-element.40), channel_id=1, source_target_pairs={{0,10},{8,18},{16,26},{24,30},{28,22},{20,14},{12,6},{4,2},{10,0},... | collective-permute-start | bytes 688136 | tf_op jit(solution)/shard_map/ppermute | solution.py:498
  48.3 9.8 %copy-start.13 = (bf16[256,896]{1,0:T(8,128)(2,1)}, bf16[256,896]{1,0:T(8,128)(2,1)S(1)}, u32[]{:S(2)}) copy-start(bf16[256,896]{1,0:T(8,128)(2,1)S(1)} %collective-permute-done.11.rest_3_.rest_13_) | copy-start | bytes 1376260
  58.2 9.8 %copy-start.3 = (bf16[256,896]{1,0:T(8,128)(2,1)}, bf16[256,896]{1,0:T(8,128)(2,1)S(1)}, u32[]{:S(2)}) copy-start(bf16[256,896]{1,0:T(8,128)(2,1)S(1)} %get-tuple-element.43.rest_16_.rest_1_) | copy-start | bytes 1376260
  64.0 52.7 %all-to-all-start.1 = ((bf16[32,4,4,16,128]{4,3,2,1,0:T(8,128)(2,1)}), bf16[32,4,4,16,128]{4,3,2,1,0:T(8,128)(2,1)S(1)}, u32[]{:S(2)}, u32[]{:S(2)}) async-start(bf16[32,4,4,16,128]{4,3,2,1,0:T(8,128)(2,1)} %bitcast.33), calls=%async_computation.1 | async-start | bytes 4194304 | tf_op jit(solution)/shard_map/all_to_all | solution.py:562
  68.0 52.8 %copy-start.16 = (bf16[256,256]{1,0:T(8,128)(2,1)S(1)}, bf16[256,256]{1,0:T(8,128)(2,1)}, u32[]{:S(2)}) copy-start(bf16[256,256]{1,0:T(8,128)(2,1)} %constant.31.clone.low_ref) | copy-start | bytes 393220
  68.0 52.8 %copy-start.17 = (bf16[256,256]{1,0:T(8,128)(2,1)S(1)}, bf16[256,256]{1,0:T(8,128)(2,1)}, u32[]{:S(2)}) copy-start(bf16[256,256]{1,0:T(8,128)(2,1)} %constant.30.clone.high_ref) | copy-start | bytes 393220
  68.0 52.8 %copy-start.19 = (bf16[128,64]{1,0:T(8,128)(2,1)S(1)}, bf16[128,64]{1,0:T(8,128)(2,1)}, u32[]{:S(2)}) copy-start(bf16[128,64]{1,0:T(8,128)(2,1)} %constant.29.clone.line_ref) | copy-start | bytes 49156
  68.0 1.9 %collective-permute-start.15 = (bf16[256,896]{1,0:T(8,128)(2,1)S(1)}, bf16[256,896]{1,0:T(8,128)(2,1)S(1)}, u32[]{:S(2)}, u32[]{:S(2)}) collective-permute-start(bf16[256,896]{1,0:T(8,128)(2,1)S(1)} %get-tuple-element.43.rest_16_.rest_1_), channel_id=1, source_target_pairs={{0,2},{2,0},{1,3},{3,1},{4,6},{6,4},{5,7},{7,5},{8,10},{10,8},{9,1... | collective-permute-start | bytes 1376264 | tf_op jit(solution)/shard_map/ppermute | solution.py:472
  116.7 52.5 %all-to-all-start = ((bf16[32,4,4,16,128]{4,3,2,1,0:T(8,128)(2,1)}), bf16[32,4,4,16,128]{4,3,2,1,0:T(8,128)(2,1)}, u32[]{:S(2)}, u32[]{:S(2)}) async-start(bf16[32,4,4,16,128]{4,3,2,1,0:T(8,128)(2,1)} %bitcast.34), calls=%async_computation | async-start | bytes 4194304 | tf_op jit(solution)/shard_map/all_to_all | solution.py:562
  (7 other events, 42.1 us)

commit v5 on v4

--- a/solution.py
+++ b/solution.py
@@ -285,8 +285,8 @@
             def _():
                 acc_ref[...] = jnp.zeros_like(acc_ref)
 
-        for z in range(planes):
-            for kind, at in enumerate((slice(0, occupied_block), slice(occupied_block, width))):
+        for kind, at in enumerate((slice(0, occupied_block), slice(occupied_block, width))):
+            for z in range(planes):
                 part_sum = jnp.dot(weighed[:, at], taken[z, at], preferred_element_type=jnp.float32)
                 if first_call and blocks == 1:
                     acc_ref[kind, z] = part_sum

time: 177 us -> 177 us (level)
  no operation moved by 1% of the time
where the time goes in v5:
time: 177 us
  Pallas kernels  95 us (54%)
  waiting for transfers between devices  57.4 us (32%)
  starting transfers between devices  18.8 us (11%)
  other arithmetic  2.66 us (2%)
  local copies, waits for them, and re-layouts  2.47 us (1%)
    pallas_call x6, Pallas kernels, absorb(): pl.pallas_call(kernel, grid_spec=pltpu.PrefetchScalarGridSpec(num_scalar_...  76.9 us
    all_to_all x2, waiting for transfers between devices, shards(): lax.all_to_all(sent, AXES, split_axis=0, concat_axis=0, tiled=True)  50.7 us
    pallas_call x2, Pallas kernels, transform(): pl.pallas_call(kernel, grid=(pw_size, pairs // step), in_specs=in_specs,...  14.5 us
    all_to_all x2, starting transfers between devices, shards(): lax.all_to_all(sent, AXES, split_axis=0, concat_axis=0, tiled=True)  7.96 us
    ppermute x3, starting transfers between devices, gather_and_absorb(): lax.ppermute(down, 'grid', back)  3.63 us
    ppermute x3, starting transfers between devices, gather_and_absorb(): lax.ppermute(up, 'grid', onward)  3.57 us
  transfers between devices with their start and end apart: 18, of which 9 were waited for; matrix products, arithmetic and copies ran while one was open for 2% of the time, Pallas kernels for 46%

profile of v5, /device:TPU:0, one launch (start us, length us, event | category | flops | bytes accessed | tf_op | source)
XLA Modules:
  0.0 176.7 jit_solution(7463097834028430832)
XLA Ops:
  0.0 1.5 copy.32
  1.7 3.0 %collective-permute-start.2 = (bf16[256,896]{1,0:T(8,128)(2,1)S(1)}, bf16[256,896]{1,0:T(8,128)(2,1)S(1)}, u32[]{:S(2)}, u32[]{:S(2)}) collective-permute-start(bf16[256,896]{1,0:T(8,128)(2,1)S(1)} %bitcast.16), channel_id=1, source_target_pairs={{8,0},{16,8},{24,16},{28,24},{20,28},{12,20},{4,12},{0,4},{9,1},{1... | collective-permute-start | bytes 1376264 | tf_op jit(solution)/shard_map/ppermute | solution.py:488
  4.8 0.8 select_reduce_fusion.1
  5.6 0.9 select_reduce_fusion.2
  6.5 0.8 select_reduce_fusion.place_ref
  7.5 3.5 %prepare.1 = (bf16[1,8,896,256]{3,2,1,0:T(8,128)(2,1)S(1)}, f32[8,128]{1,0:T(8,128)S(1)}) custom-call(s32[8]{0:T(128)S(1)} %select_reduce_fusion.place_ref, s32[1]{0:T(128)} %bitcast.core_ref, f32[2]{0:T(128)S(1)} %get-tuple-element.50.time_ref.refs_0_, f32[2,2]{1,0:T(2,128)S(1)} %multiply_negate_fusion.rest_4_.refs_1_.rest_7_.rest_18_, ...), custom_call_target="tpu_custom_call" | custom-call | bytes 3670016 | tf_op jit(solution)/shard_map/prepare/pallas_call | solution.py:203
  11.0 5.3 %absorb.6 = (f32[2,8,512,256]{3,2,1,0:T(8,128)S(1)}, f32[8,128]{1,0:T(8,128)S(1)}) custom-call(s32[8]{0:T(128)S(1)} %select_reduce_fusion.place_ref, s32[1]{0:T(128)} %bitcast.core_ref, f32[2]{0:T(128)S(1)} %get-tuple-element.50.time_ref.refs_0_, f32[1,1024]{1,0:T(1,128)S(1)} %bitcast.27, f32[1,6144]{1,0:T(1,128)S(1)} %bitcast.21, ...), custom_call_target="tpu_custom_call" | custom-call | flops 1879048192 | bytes 4128768 | tf_op jit(solution)/shard_map/absorb/pallas_call | solution.py:337
  16.7 0.3 collective-permute-start.3
  17.2 1.9 %collective-permute-start.5 = (bf16[256,896]{1,0:T(8,128)(2,1)S(1)}, bf16[256,896]{1,0:T(8,128)(2,1)S(1)}, u32[]{:S(2)}, u32[]{:S(2)}) collective-permute-start(bf16[256,896]{1,0:T(8,128)(2,1)S(1)} %get-tuple-element.29.rest_2_.rest_4_), channel_id=1, source_target_pairs={{0,8},{8,16},{16,24},{24,28},{28,20},{20,12},{12,4},{4,0},{1,9},{9... | collective-permute-start | bytes 1376264 | tf_op jit(solution)/shard_map/ppermute | solution.py:488
  19.2 9.7 %absorb.7 = (f32[2,8,512,256]{3,2,1,0:T(8,128)S(1)}, f32[8,128]{1,0:T(8,128)S(1)}) custom-call(s32[8]{0:T(128)S(1)} %select_reduce_fusion.place_ref, s32[1]{0:T(128)} %bitcast.core_ref, f32[2]{0:T(128)S(1)} %get-tuple-element.50.time_ref.refs_0_, f32[1,1024]{1,0:T(1,128)S(1)} %bitcast.28, f32[1,6144]{1,0:T(1,128)S(1)} %bitcast.22, ...), custom_call_target="tpu_custom_call", output_to_operand_aliasing={{0}: (11, {})} | custom-call | flops 3758096384 | bytes 8257536 | tf_op jit(solution)/shard_map/absorb/pallas_call | solution.py:337
  28.9 1.2 collective-permute-done.5.refs_0_
  30.1 1.5 collective-permute-done.6.refs_1_
  31.6 0.5 collective-permute-start.8
  32.1 1.6 collective-permute-start.9
  33.7 0.4 collective-permute-start.10
  34.2 9.7 %absorb.8 = (f32[2,8,512,256]{3,2,1,0:T(8,128)S(1)}, f32[8,128]{1,0:T(8,128)S(1)}) custom-call(s32[8]{0:T(128)S(1)} %select_reduce_fusion.place_ref, s32[1]{0:T(128)} %bitcast.core_ref, f32[2]{0:T(128)S(1)} %get-tuple-element.50.time_ref.refs_0_, f32[1,1024]{1,0:T(1,128)S(1)} %bitcast.29, f32[1,6144]{1,0:T(1,128)S(1)} %bitcast.23, ...), custom_call_target="tpu_custom_call", output_to_operand_aliasing={{0}: (11, {})} | custom-call | flops 3758096384 | bytes 8257536 | tf_op jit(solution)/shard_map/absorb/pallas_call | solution.py:337
  43.9 0.7 collective-permute-done.9.refs_0_
  44.6 1.3 collective-permute-done.10.refs_1_
  45.9 0.5 collective-permute-start.12
  46.5 1.8 %collective-permute-start.13 = (bf16[256,896]{1,0:T(8,128)(2,1)S(1)}, bf16[256,896]{1,0:T(8,128)(2,1)S(1)}, u32[]{:S(2)}, u32[]{:S(2)}) collective-permute-start(bf16[256,896]{1,0:T(8,128)(2,1)S(1)} %get-tuple-element.39), channel_id=1, source_target_pairs={{0,8},{8,16},{16,24},{24,28},{28,20},{20,12},{12,4},{4,0},{10,2},{... | collective-permute-start | bytes 1376264 | tf_op jit(solution)/shard_map/ppermute | solution.py:498
  48.4 9.7 %absorb.9 = (f32[2,8,512,256]{3,2,1,0:T(8,128)S(1)}, f32[8,128]{1,0:T(8,128)S(1)}) custom-call(s32[8]{0:T(128)S(1)} %select_reduce_fusion.place_ref, s32[1]{0:T(128)} %bitcast.core_ref, f32[2]{0:T(128)S(1)} %get-tuple-element.50.time_ref.refs_0_, f32[1,1024]{1,0:T(1,128)S(1)} %bitcast.30, f32[1,6144]{1,0:T(1,128)S(1)} %bitcast.24, ...), custom_call_target="tpu_custom_call", output_to_operand_aliasing={{0}: (11, {})} | custom-call | flops 3758096384 | bytes 8257536 | tf_op jit(solution)/shard_map/absorb/pallas_call | solution.py:337
  58.2 5.6 %absorb.11 = (f32[2,8,512,256]{3,2,1,0:T(8,128)S(1)}, bf16[8,2,2,4,4,16,128]{6,5,4,3,2,1,0:T(8,128)(2,1)}) custom-call(s32[8]{0:T(128)S(1)} %select_reduce_fusion.place_ref, s32[1]{0:T(128)} %bitcast.core_ref, f32[2]{0:T(128)S(1)} %get-tuple-element.50.time_ref.refs_0_, f32[1,1024]{1,0:T(1,128)S(1)} %bitcast.31, ...), custom_call_target="tpu_custom_call", output_to_operand_aliasing={{0}: (8, {})} | custom-call | flops 1879048192 | bytes 4128768 | tf_op jit(solution)/shard_map/absorb/pallas_call | solution.py:337
  63.7 3.9 %all-to-all-start.1 = ((bf16[32,4,4,16,128]{4,3,2,1,0:T(8,128)(2,1)}), bf16[32,4,4,16,128]{4,3,2,1,0:T(8,128)(2,1)S(1)}, u32[]{:S(2)}, u32[]{:S(2)}) async-start(bf16[32,4,4,16,128]{4,3,2,1,0:T(8,128)(2,1)} %bitcast.33), calls=%async_computation.1 | async-start | bytes 4194304 | tf_op jit(solution)/shard_map/all_to_all | solution.py:562
  67.7 0.3 collective-permute-start.15
  68.0 1.6 collective-permute-done.15.rest_17_
  69.6 0.8 copy-done.20
  70.4 37.0 %absorb.10 = (f32[2,8,512,256]{3,2,1,0:T(8,128)}, bf16[8,2,2,4,4,16,128]{6,5,4,3,2,1,0:T(8,128)(2,1)}) custom-call(s32[8]{0:T(128)S(1)} %select_reduce_fusion.place_ref, s32[1]{0:T(128)} %bitcast.core_ref, f32[2]{0:T(128)S(1)} %get-tuple-element.50.time_ref.refs_0_, f32[1,1024]{1,0:T(1,128)S(1)} %bitcast.32, f32[1,6144]{1,0:T(1,128)S(1)} %bitcast.26, ...), custom_call_target="tpu_custom_call" | custom-call | flops 15032385536 | bytes 33030144 | tf_op jit(solution)/shard_map/absorb/pallas_call | solution.py:337
  107.4 9.0 %all-to-all-done.1 = bf16[32,4,4,16,128]{4,3,2,1,0:T(8,128)(2,1)S(1)} async-done(((bf16[32,4,4,16,128]{4,3,2,1,0:T(8,128)(2,1)}), bf16[32,4,4,16,128]{4,3,2,1,0:T(8,128)(2,1)S(1)}, u32[]{:S(2)}, u32[]{:S(2)}) %all-to-all-start.1) | async-done | bytes 2097184 | tf_op jit(solution)/shard_map/all_to_all | solution.py:562
  116.4 4.0 %all-to-all-start = ((bf16[32,4,4,16,128]{4,3,2,1,0:T(8,128)(2,1)}), bf16[32,4,4,16,128]{4,3,2,1,0:T(8,128)(2,1)}, u32[]{:S(2)}, u32[]{:S(2)}) async-start(bf16[32,4,4,16,128]{4,3,2,1,0:T(8,128)(2,1)} %bitcast.34), calls=%async_computation | async-start | bytes 4194304 | tf_op jit(solution)/shard_map/all_to_all | solution.py:562
  120.5 6.8 %transform.2.rest_0_ = f32[1,32,16,64,128]{4,3,2,1,0:T(8,128)} custom-call(bf16[128,64]{1,0:T(8,128)(2,1)S(1)} %copy-done.19, bf16[256,256]{1,0:T(8,128)(2,1)S(1)} %copy-done.17, bf16[256,256]{1,0:T(8,128)(2,1)S(1)} %copy-done.16, bf16[16,2,4,4,16,128]{5,4,3,2,1,0:T(8,128)(2,1)S(1)} %bitcast.15), custom_call_target="tpu_custom_call" | custom-call | flops 1879048192 | bytes 10485760 | tf_op jit(solution)/shard_map/transform/pallas_call | solution.py:404
  127.2 41.7 %all-to-all-done = bf16[32,4,4,16,128]{4,3,2,1,0:T(8,128)(2,1)} async-done(((bf16[32,4,4,16,128]{4,3,2,1,0:T(8,128)(2,1)}), bf16[32,4,4,16,128]{4,3,2,1,0:T(8,128)(2,1)}, u32[]{:S(2)}, u32[]{:S(2)}) %all-to-all-start) | async-done | bytes 2097184 | tf_op jit(solution)/shard_map/all_to_all | solution.py:562
  168.9 7.8 %transform.3 = f32[1,32,16,64,128]{4,3,2,1,0:T(8,128)} custom-call(bf16[128,64]{1,0:T(8,128)(2,1)S(1)} %copy-done.19, bf16[256,256]{1,0:T(8,128)(2,1)S(1)} %copy-done.17, bf16[256,256]{1,0:T(8,128)(2,1)S(1)} %copy-done.16, bf16[16,2,4,4,16,128]{5,4,3,2,1,0:T(8,128)(2,1)} %bitcast.9.in_ref, ...), custom_call_target="tpu_custom_call", output_to_operand_aliasing={{}: (4, {})} | custom-call | flops 1879048192 | bytes 10485760 | tf_op jit(solution)/shard_map/transform/pallas_call | solution.py:404
  (68 shorter events, 1.2 us)
Async XLA Ops:
  1.7 14.7 %collective-permute-start.2 = (bf16[256,896]{1,0:T(8,128)(2,1)S(1)}, bf16[256,896]{1,0:T(8,128)(2,1)S(1)}, u32[]{:S(2)}, u32[]{:S(2)}) collective-permute-start(bf16[256,896]{1,0:T(8,128)(2,1)S(1)} %bitcast.16), channel_id=1, source_target_pairs={{8,0},{16,8},{24,16},{28,24},{20,28},{12,20},{4,12},{0,4},{9,1},{1... | collective-permute-start | bytes 1376264 | tf_op jit(solution)/shard_map/ppermute | solution.py:488
  4.7 12.0 %collective-permute-start.1 = (bf16[256,896]{1,0:T(8,128)(2,1)S(1)}, bf16[256,896]{1,0:T(8,128)(2,1)S(1)}, u32[]{:S(2)}, u32[]{:S(2)}) collective-permute-start(bf16[256,896]{1,0:T(8,128)(2,1)S(1)} %bitcast.17), channel_id=1, source_target_pairs={{0,8},{8,16},{16,24},{24,28},{28,20},{20,12},{12,4},{4,0},{1,9},{9... | collective-permute-start | bytes 1376264 | tf_op jit(solution)/shard_map/ppermute | solution.py:488
  4.8 6.2 %collective-permute-start = (bf16[256,896]{1,0:T(8,128)(2,1)S(1)}, bf16[256,896]{1,0:T(8,128)(2,1)S(1)}, u32[]{:S(2)}, u32[]{:S(2)}) collective-permute-start(bf16[256,896]{1,0:T(8,128)(2,1)S(1)} %bitcast.18), channel_id=1, source_target_pairs={{0,2},{2,0},{1,3},{3,1},{4,6},{6,4},{5,7},{7,5},{8,10},{10,8},{9,1... | collective-permute-start | bytes 1376264 | tf_op jit(solution)/shard_map/ppermute | solution.py:472
  16.7 12.2 %copy-start.4 = (bf16[256,896]{1,0:T(8,128)(2,1)}, bf16[256,896]{1,0:T(8,128)(2,1)S(1)}, u32[]{:S(2)}) copy-start(bf16[256,896]{1,0:T(8,128)(2,1)S(1)} %get-tuple-element.30.rest_4_.rest_6_) | copy-start | bytes 1376260
  16.7 12.2 %copy-start.5 = (bf16[256,896]{1,0:T(8,128)(2,1)}, bf16[256,896]{1,0:T(8,128)(2,1)S(1)}, u32[]{:S(2)}) copy-start(bf16[256,896]{1,0:T(8,128)(2,1)S(1)} %get-tuple-element.29.rest_2_.rest_4_) | copy-start | bytes 1376260
  16.7 2.5 %collective-permute-start.3 = (bf16[256,896]{1,0:T(8,128)(2,1)S(1)}, bf16[256,896]{1,0:T(8,128)(2,1)S(1)}, u32[]{:S(2)}, u32[]{:S(2)}) collective-permute-start(bf16[256,896]{1,0:T(8,128)(2,1)S(1)} %get-tuple-element.29.rest_2_.rest_4_), channel_id=1, source_target_pairs={{0,2},{2,0},{1,3},{3,1},{4,6},{6,4},{5,7},{7,5},{8,10},{10,8},{9,1... | collective-permute-start | bytes 1376264 | tf_op jit(solution)/shard_map/ppermute | solution.py:472
  17.0 2.2 %collective-permute-start.4 = (bf16[256,896]{1,0:T(8,128)(2,1)S(1)}, bf16[256,896]{1,0:T(8,128)(2,1)S(1)}, u32[]{:S(2)}, u32[]{:S(2)}) collective-permute-start(bf16[256,896]{1,0:T(8,128)(2,1)S(1)} %get-tuple-element.30.rest_4_.rest_6_), channel_id=1, source_target_pairs={{0,2},{2,0},{1,3},{3,1},{4,6},{6,4},{5,7},{7,5},{8,10},{10,8},{9,1... | collective-permute-start | bytes 1376264 | tf_op jit(solution)/shard_map/ppermute | solution.py:472
  17.2 12.9 %collective-permute-start.5 = (bf16[256,896]{1,0:T(8,128)(2,1)S(1)}, bf16[256,896]{1,0:T(8,128)(2,1)S(1)}, u32[]{:S(2)}, u32[]{:S(2)}) collective-permute-start(bf16[256,896]{1,0:T(8,128)(2,1)S(1)} %get-tuple-element.29.rest_2_.rest_4_), channel_id=1, source_target_pairs={{0,8},{8,16},{16,24},{24,28},{28,20},{20,12},{12,4},{4,0},{1,9},{9... | collective-permute-start | bytes 1376264 | tf_op jit(solution)/shard_map/ppermute | solution.py:488
  19.0 12.6 %collective-permute-start.6 = (bf16[256,896]{1,0:T(8,128)(2,1)S(1)}, bf16[256,896]{1,0:T(8,128)(2,1)S(1)}, u32[]{:S(2)}, u32[]{:S(2)}) collective-permute-start(bf16[256,896]{1,0:T(8,128)(2,1)S(1)} %get-tuple-element.30.rest_4_.rest_6_), channel_id=1, source_target_pairs={{8,0},{16,8},{24,16},{28,24},{20,28},{12,20},{4,12},{0,4},{9,1},{1... | collective-permute-start | bytes 1376264 | tf_op jit(solution)/shard_map/ppermute | solution.py:488
  19.2 9.7 %copy-start.10 = (bf16[256,896]{1,0:T(8,128)(2,1)}, bf16[256,896]{1,0:T(8,128)(2,1)S(1)}, u32[]{:S(2)}) copy-start(bf16[256,896]{1,0:T(8,128)(2,1)S(1)} %collective-permute-done.4.rest_5_.rest_7_) | copy-start | bytes 1376260
  31.6 12.2 %copy-start.6 = (bf16[256,896]{1,0:T(8,128)(2,1)}, bf16[256,896]{1,0:T(8,128)(2,1)S(1)}, u32[]{:S(2)}) copy-start(bf16[256,896]{1,0:T(8,128)(2,1)S(1)} %get-tuple-element.33.rest_2_.rest_8_) | copy-start | bytes 1376260
  31.6 12.3 %copy-start.7 = (bf16[256,896]{1,0:T(8,128)(2,1)}, bf16[256,896]{1,0:T(8,128)(2,1)S(1)}, u32[]{:S(2)}) copy-start(bf16[256,896]{1,0:T(8,128)(2,1)S(1)} %get-tuple-element.34.rest_4_.rest_10_) | copy-start | bytes 1376260
  31.6 2.5 %collective-permute-start.7 = (bf16[256,896]{1,0:T(8,128)(2,1)S(1)}, bf16[256,896]{1,0:T(8,128)(2,1)S(1)}, u32[]{:S(2)}, u32[]{:S(2)}) collective-permute-start(bf16[256,896]{1,0:T(8,128)(2,1)S(1)} %get-tuple-element.33.rest_2_.rest_8_), channel_id=1, source_target_pairs={{0,2},{2,0},{1,3},{3,1},{4,6},{6,4},{5,7},{7,5},{8,10},{10,8},{9,1... | collective-permute-start | bytes 1376264 | tf_op jit(solution)/shard_map/ppermute | solution.py:472
  31.6 2.5 %collective-permute-start.8 = (bf16[256,896]{1,0:T(8,128)(2,1)S(1)}, bf16[256,896]{1,0:T(8,128)(2,1)S(1)}, u32[]{:S(2)}, u32[]{:S(2)}) collective-permute-start(bf16[256,896]{1,0:T(8,128)(2,1)S(1)} %get-tuple-element.34.rest_4_.rest_10_), channel_id=1, source_target_pairs={{0,2},{2,0},{1,3},{3,1},{4,6},{6,4},{5,7},{7,5},{8,10},{10,8},{9,1... | collective-permute-start | bytes 1376264 | tf_op jit(solution)/shard_map/ppermute | solution.py:472
  32.1 12.5 %collective-permute-start.9 = (bf16[256,896]{1,0:T(8,128)(2,1)S(1)}, bf16[256,896]{1,0:T(8,128)(2,1)S(1)}, u32[]{:S(2)}, u32[]{:S(2)}) collective-permute-start(bf16[256,896]{1,0:T(8,128)(2,1)S(1)} %get-tuple-element.33.rest_2_.rest_8_), channel_id=1, source_target_pairs={{0,8},{8,16},{16,24},{24,28},{28,20},{20,12},{12,4},{4,0},{1,9},{9... | collective-permute-start | bytes 1376264 | tf_op jit(solution)/shard_map/ppermute | solution.py:488
  33.7 12.2 %collective-permute-start.10 = (bf16[256,896]{1,0:T(8,128)(2,1)S(1)}, bf16[256,896]{1,0:T(8,128)(2,1)S(1)}, u32[]{:S(2)}, u32[]{:S(2)}) collective-permute-start(bf16[256,896]{1,0:T(8,128)(2,1)S(1)} %get-tuple-element.34.rest_4_.rest_10_), channel_id=1, source_target_pairs={{8,0},{16,8},{24,16},{28,24},{20,28},{12,20},{4,12},{0,4},{9,1},{1... | collective-permute-start | bytes 1376264 | tf_op jit(solution)/shard_map/ppermute | solution.py:488
  34.2 9.7 %copy-start.11 = (bf16[256,896]{1,0:T(8,128)(2,1)}, bf16[256,896]{1,0:T(8,128)(2,1)S(1)}, u32[]{:S(2)}) copy-start(bf16[256,896]{1,0:T(8,128)(2,1)S(1)} %collective-permute-done.7.rest_3_.rest_9_) | copy-start | bytes 1376260
  34.2 9.7 %copy-start.12 = (bf16[256,896]{1,0:T(8,128)(2,1)}, bf16[256,896]{1,0:T(8,128)(2,1)S(1)}, u32[]{:S(2)}) copy-start(bf16[256,896]{1,0:T(8,128)(2,1)S(1)} %collective-permute-done.8.rest_5_.rest_11_) | copy-start | bytes 1376260
  45.9 12.2 %copy-start = (bf16[256,896]{1,0:T(8,128)(2,1)}, bf16[256,896]{1,0:T(8,128)(2,1)S(1)}, u32[]{:S(2)}) copy-start(bf16[256,896]{1,0:T(8,128)(2,1)S(1)} %get-tuple-element.37.first_ref.rest_2_.rest_12_) | copy-start | bytes 1376260
  45.9 12.2 %copy-start.1 = (bf16[256,896]{1,0:T(8,128)(2,1)}, bf16[256,896]{1,0:T(8,128)(2,1)S(1)}, u32[]{:S(2)}) copy-start(bf16[256,896]{1,0:T(8,128)(2,1)S(1)} %get-tuple-element.38.second_ref.rest_4_.rest_14_) | copy-start | bytes 1376260
  45.9 2.4 %collective-permute-start.11 = (bf16[256,896]{1,0:T(8,128)(2,1)S(1)}, bf16[256,896]{1,0:T(8,128)(2,1)S(1)}, u32[]{:S(2)}, u32[]{:S(2)}) collective-permute-start(bf16[256,896]{1,0:T(8,128)(2,1)S(1)} %get-tuple-element.37.first_ref.rest_2_.rest_12_), channel_id=1, source_target_pairs={{0,2},{2,0},{1,3},{3,1},{4,6},{6,4},{5,7},{7,5},{8,10},{10,8},{9,1... | collective-permute-start | bytes 1376264 | tf_op jit(solution)/shard_map/ppermute | solution.py:472
  45.9 2.5 %collective-permute-start.12 = (bf16[256,896]{1,0:T(8,128)(2,1)S(1)}, bf16[256,896]{1,0:T(8,128)(2,1)S(1)}, u32[]{:S(2)}, u32[]{:S(2)}) collective-permute-start(bf16[256,896]{1,0:T(8,128)(2,1)S(1)} %get-tuple-element.38.second_ref.rest_4_.rest_14_), channel_id=1, source_target_pairs={{0,2},{2,0},{1,3},{3,1},{4,6},{6,4},{5,7},{7,5},{8,10},{10,8},{9,1... | collective-permute-start | bytes 1376264 | tf_op jit(solution)/shard_map/ppermute | solution.py:472
  46.5 11.6 %collective-permute-start.13 = (bf16[256,896]{1,0:T(8,128)(2,1)S(1)}, bf16[256,896]{1,0:T(8,128)(2,1)S(1)}, u32[]{:S(2)}, u32[]{:S(2)}) collective-permute-start(bf16[256,896]{1,0:T(8,128)(2,1)S(1)} %get-tuple-element.39), channel_id=1, source_target_pairs={{0,8},{8,16},{16,24},{24,28},{28,20},{20,12},{12,4},{4,0},{10,2},{... | collective-permute-start | bytes 1376264 | tf_op jit(solution)/shard_map/ppermute | solution.py:498
  48.3 9.8 %collective-permute-start.14 = (bf16[128,896]{1,0:T(8,128)(2,1)S(1)}, bf16[128,896]{1,0:T(8,128)(2,1)S(1)}, u32[]{:S(2)}, u32[]{:S(2)}) collective-permute-start(bf16[128,896]{1,0:T(8,128)(2,1)S(1)} %get-tuple-element.40), channel_id=1, source_target_pairs={{0,10},{8,18},{16,26},{24,30},{28,22},{20,14},{12,6},{4,2},{10,0},... | collective-permute-start | bytes 688136 | tf_op jit(solution)/shard_map/ppermute | solution.py:498
  48.3 9.8 %copy-start.13 = (bf16[256,896]{1,0:T(8,128)(2,1)}, bf16[256,896]{1,0:T(8,128)(2,1)S(1)}, u32[]{:S(2)}) copy-start(bf16[256,896]{1,0:T(8,128)(2,1)S(1)} %collective-permute-done.11.rest_3_.rest_13_) | copy-start | bytes 1376260
  48.4 9.7 %copy-start.14 = (bf16[256,896]{1,0:T(8,128)(2,1)}, bf16[256,896]{1,0:T(8,128)(2,1)S(1)}, u32[]{:S(2)}) copy-start(bf16[256,896]{1,0:T(8,128)(2,1)S(1)} %collective-permute-done.12.rest_5_.rest_15_) | copy-start | bytes 1376260
  63.7 52.7 %all-to-all-start.1 = ((bf16[32,4,4,16,128]{4,3,2,1,0:T(8,128)(2,1)}), bf16[32,4,4,16,128]{4,3,2,1,0:T(8,128)(2,1)S(1)}, u32[]{:S(2)}, u32[]{:S(2)}) async-start(bf16[32,4,4,16,128]{4,3,2,1,0:T(8,128)(2,1)} %bitcast.33), calls=%async_computation.1 | async-start | bytes 4194304 | tf_op jit(solution)/shard_map/all_to_all | solution.py:562
  67.7 52.8 %copy-start.16 = (bf16[256,256]{1,0:T(8,128)(2,1)S(1)}, bf16[256,256]{1,0:T(8,128)(2,1)}, u32[]{:S(2)}) copy-start(bf16[256,256]{1,0:T(8,128)(2,1)} %constant.31.clone.low_ref) | copy-start | bytes 393220
  67.7 52.8 %copy-start.17 = (bf16[256,256]{1,0:T(8,128)(2,1)S(1)}, bf16[256,256]{1,0:T(8,128)(2,1)}, u32[]{:S(2)}) copy-start(bf16[256,256]{1,0:T(8,128)(2,1)} %constant.30.clone.high_ref) | copy-start | bytes 393220
  67.7 52.8 %copy-start.19 = (bf16[128,64]{1,0:T(8,128)(2,1)S(1)}, bf16[128,64]{1,0:T(8,128)(2,1)}, u32[]{:S(2)}) copy-start(bf16[128,64]{1,0:T(8,128)(2,1)} %constant.29.clone.line_ref) | copy-start | bytes 49156
  67.7 1.9 %collective-permute-start.15 = (bf16[256,896]{1,0:T(8,128)(2,1)S(1)}, bf16[256,896]{1,0:T(8,128)(2,1)S(1)}, u32[]{:S(2)}, u32[]{:S(2)}) collective-permute-start(bf16[256,896]{1,0:T(8,128)(2,1)S(1)} %get-tuple-element.43.rest_16_.rest_1_), channel_id=1, source_target_pairs={{0,2},{2,0},{1,3},{3,1},{4,6},{6,4},{5,7},{7,5},{8,10},{10,8},{9,1... | collective-permute-start | bytes 1376264 | tf_op jit(solution)/shard_map/ppermute | solution.py:472
  116.4 52.5 %all-to-all-start = ((bf16[32,4,4,16,128]{4,3,2,1,0:T(8,128)(2,1)}), bf16[32,4,4,16,128]{4,3,2,1,0:T(8,128)(2,1)}, u32[]{:S(2)}, u32[]{:S(2)}) async-start(bf16[32,4,4,16,128]{4,3,2,1,0:T(8,128)(2,1)} %bitcast.34), calls=%async_computation | async-start | bytes 4194304 | tf_op jit(solution)/shard_map/all_to_all | solution.py:562
  (7 other events, 41.8 us)
